TPU v7x, 128 devices: a whole 4x4x4 slice. The times are simulated.
128 devices in a mesh: rows: 64 (over y, z, x), grp: 2 (over core).
Axes of the slice: x: 4, y: 4, z: 4, core: 2. Of those that a mesh axis runs over, the one named last changes fastest.
Arguments:
- start_basis: bfloat16 [65536, 64], P(('rows', 'grp')), may hold values from -6 to 6
- kernel_blocks: bfloat16 [11776, 256, 256], P(('rows', 'grp')), may hold values from -0.0390625 to 0.0390625
- block_row: int32 [11776], P(('rows', 'grp')), may hold values from 0 to 255, as said below
- block_col: int32 [11776], P(('rows', 'grp')), may hold values from 0 to 255, as said below
- block_count: int32 [128], P(('rows', 'grp')), may hold values from 1 to 92, as said below
Outputs:
- embedding: float32 [65536, 64], P(('rows', 'grp'))
- projected: float32 [64, 64], replicated
Inputs may be any that keep to these rules, and one draw needn't show every extreme that they name: block_count[d] is the number of live slots of device d, its first ones; device 0 has all 92 live and the last device has 1. `block_row`: each slot's row block is one of its own device's 2 row blocks. `block_col`: each slot's column block is at least its row block; among one device's live slots at most 1 have their column block on any one device, the last device's live slots all lie on itself, and device 0 has a live slot whose column block lies on the last device.
All inputs are finite; a program needn't handle non-finite values.
Results may differ from a plain program's by a relative error of at most 0.0034.
Values may be sent and summed in bfloat16 or wider, within the bound.
No kernel may reach another device: no remote copies, remote signals or barrier semaphores. Data moves between devices by JAX's collectives and lax.ppermute only.
A program may use at most 128 MiB of HBM per device.

v0:
```python
import jax
import jax.numpy as jnp
from jax import lax
from jax.sharding import PartitionSpec as P

ITERS = 2


def onehot(index, count, dtype):
    return (index[:, None] == jnp.arange(count, dtype=jnp.int32)[None, :]).astype(dtype)


def on_device(start_basis, kernel_blocks, block_row, block_col, block_count):
    devices = lax.axis_size(("rows", "grp"))
    my_index = lax.axis_index(("rows", "grp"))
    block_size = kernel_blocks.shape[1]
    columns = start_basis.shape[1]
    own_rows = start_basis.shape[0]
    row_blocks = own_rows // block_size
    slot_count = kernel_blocks.shape[0]
    per_peer = (slot_count + devices - 1) // devices
    total_rows = own_rows * devices
    outside = devices * per_peer
    positions = jnp.arange(slot_count, dtype=jnp.int32)
    alive_mask = positions < block_count[0]
    local_row = block_row - my_index * row_blocks
    target = block_col // row_blocks
    target_block = block_col - target * row_blocks
    earlier = (
        (target[:, None] == target[None, :])
        & alive_mask[None, :]
        & (positions[None, :] < positions[:, None])
    )
    order_rank = jnp.sum(earlier.astype(jnp.int32), axis=1)
    slot_place = jnp.where(alive_mask, target * per_peer + order_rank, outside)
    wanted_local = jnp.full((outside,), -1, jnp.int32).at[slot_place].set(target_block, mode="drop")
    incoming = lax.all_to_all(
        wanted_local, ("rows", "grp"), split_axis=0, concat_axis=0, tiled=True
    )
    row_select = (
        onehot(local_row, row_blocks, jnp.float32) * alive_mask[:, None].astype(jnp.float32)
    ).T
    reply_select = onehot(incoming, row_blocks, jnp.bfloat16)
    receive_select = reply_select.T
    basis = start_basis
    result = None
    projected = None
    for iteration in range(ITERS):
        basis_tiles = basis.reshape(row_blocks, block_size, columns)
        gathered = lax.all_gather(basis, ("rows", "grp"), axis=0, tiled=True)
        partners = jnp.take(gathered.reshape(-1, block_size, columns), block_col, axis=0)
        forward = jnp.einsum(
            "sij,sjc->sic", kernel_blocks, partners, preferred_element_type=jnp.float32
        )
        own_tiles = jnp.take(basis_tiles, local_row, axis=0)
        mirrored = jnp.einsum(
            "sji,sjc->sic", kernel_blocks, own_tiles, preferred_element_type=jnp.float32
        ).astype(jnp.bfloat16)
        outgoing = (
            jnp.zeros((outside, block_size, columns), jnp.bfloat16)
            .at[slot_place]
            .set(mirrored, mode="drop")
        )
        arrived = lax.all_to_all(outgoing, ("rows", "grp"), split_axis=0, concat_axis=0, tiled=True)
        image_rows = jnp.einsum("ks,sic->kic", row_select, forward, precision=lax.Precision.HIGHEST)
        image_rows = image_rows + jnp.einsum(
            "kr,ric->kic", receive_select, arrived, preferred_element_type=jnp.float32
        )
        flat_image = image_rows.reshape(own_rows, columns)
        gram_part = jnp.dot(flat_image.T, flat_image, precision=lax.Precision.HIGHEST)
        if iteration == ITERS - 1:
            projection = jnp.dot(
                basis.astype(jnp.float32).T, flat_image, precision=lax.Precision.HIGHEST
            )
            gram_part, projection = lax.psum((gram_part, projection), ("rows", "grp"))
            projected = projection / total_rows
        else:
            gram_part = lax.psum(gram_part, ("rows", "grp"))
        lower_factor = jnp.linalg.cholesky(gram_part / total_rows)
        inverse = jax.scipy.linalg.solve_triangular(
            lower_factor, jnp.eye(columns, dtype=jnp.float32), lower=True
        )
        result = jnp.dot(flat_image, inverse.T, precision=lax.Precision.HIGHEST)
        basis = result.astype(jnp.bfloat16)
    return (result, projected)


def solution(mesh):
    in_specs = (
        P(("rows", "grp"), None),
        P(("rows", "grp"), None, None),
        P(("rows", "grp")),
        P(("rows", "grp")),
        P(("rows", "grp")),
    )
    out_specs = (P(("rows", "grp"), None), P())
    return jax.shard_map(
        on_device, mesh=mesh, in_specs=in_specs, out_specs=out_specs, check_vma=False
    )
```

profile of v0, /device:TPU:1, one launch (start us, length us, event | category | flops | bytes accessed | tf_op | source)
XLA Modules:
  0.0 482.5 jit_solution(16354992929485339264)
XLA Ops:
  7.2 0.0 all-gather.3.cloned.1.call-start
  7.2 0.7 all-gather.3.cloned.1.call-update
  8.6 0.7 multiply_subtract_fusion
  9.2 0.2 convert_reduce_fusion
  9.4 0.9 scatter_custom_fusion
  10.3 0.7 copy.91
  11.0 11.5 %all-to-all-start = ((s32[128,1,1]{2,1,0:T(1,128)}), s32[128,1,1]{2,1,0:T(1,128)S(1)}, u32[]{:S(2)}, u32[]{:S(2)}) async-start(s32[128,1,1]{2,1,0:T(1,128)} %copy.91), calls=%async_computation | async-start | bytes 131072 | tf_op jit(solution)/shard_map/all_to_all | solution.py:37
  22.5 0.8 copy.142
  23.4 0.7 compare_and_fusion.1
  24.1 0.8 gather_fusion.1
  24.9 8.4 %convert_bitcast_fusion.1 = bf16[92,256,64]{1,2,0:T(8,128)(2,1)} fusion(bf16[92,256,256]{2,1,0:T(8,128)(2,1)} %param.13, bf16[92,256,64]{1,2,0:T(8,128)(2,1)S(1)} %gather_fusion.1, pred[92]{0:T(512)(128)(4,1)S(1)} %get-tuple-element.22), kind=kOutput, calls=%fused_computation.26 | convolution fusion | flops 774766592 | bytes 18088028 | tf_op jit(solution)/shard_map/sji,sjc->sic/dot_general | solution.py:56
  33.2 0.0 copy-start.1
  33.2 2.5 broadcast.76.clone
  35.7 0.3 copy-done.1
  36.0 13.0 %scatter_fusion = bf16[128,256,64]{1,2,0:T(8,128)(2,1)} fusion(bf16[128,256,64]{1,2,0:T(8,128)(2,1)} %broadcast.76.clone, s32[92]{0:T(128)S(1)} %compare_select_fusion.1, bf16[92,256,64]{1,2,0:T(8,128)(2,1)S(1)} %copy-done.1), kind=kCustom, calls=%fused_computation.5 | custom fusion | bytes 9044336 | tf_op jit(solution)/shard_map/scatter | solution.py:62
  49.0 0.0 copy-start.3
  49.0 0.0 all-to-all-done
  49.0 10.6 %all-to-all-start.1 = ((bf16[128,256,64]{1,2,0:T(8,128)(2,1)}), bf16[128,256,64]{1,2,0:T(8,128)(2,1)}, u32[]{:S(2)}, u32[]{:S(2)}) async-start(bf16[128,256,64]{1,2,0:T(8,128)(2,1)} %scatter_fusion), calls=%async_computation.1 | async-start | bytes 8388608 | tf_op jit(solution)/shard_map/all_to_all | solution.py:64
  59.7 0.3 all-gather.5.cloned.1.call-start
  60.0 0.0 copy-done.3
  60.1 2.4 reduce.4
  62.4 65.6 %all-gather.3.cloned.1.call-done = bf16[65536,64]{0,1:T(8,128)(2,1)} async-done(((bf16[512,64]{0,1:T(8,128)(2,1)}), bf16[65536,64]{0,1:T(8,128)(2,1)}) %all-gather.3.cloned.1.call-update) | async-done | bytes 8388624 | tf_op jit(solution)/shard_map/all_gather | solution.py:50
  128.1 7.8 %copy.140 = bf16[8,256,8,256]{3,2,0,1:T(8,128)(2,1)} copy(bf16[8,256,8,256]{3,2,1,0:T(8,128)(2,1)} %bitcast.85) | data formatting | bytes 16777216 | tf_op jit(solution)/shard_map/reshape | solution.py:51
  135.8 4.2 gather_fusion
  140.0 10.7 %fusion.20 = f32[92,256,64]{1,2,0:T(8,128)} fusion(bf16[92,256,256]{2,1,0:T(8,128)(2,1)} %param.13, bf16[92,256,64]{1,2,0:T(8,128)(2,1)S(1)} %gather_fusion, pred[92]{0:T(512)(128)(4,1)S(1)} %compare_and_fusion), kind=kOutput, calls=%fused_computation.31 | convolution fusion | flops 773259264 | bytes 21102684 | tf_op jit(solution)/shard_map/sij,sjc->sic/dot_general | solution.py:52
  150.8 9.3 %fusion.2 = f32[2,256,64]{1,0,2:T(2,128)S(1)} fusion(f32[92,256,64]{1,2,0:T(8,128)} %fusion.20, f32[92]{0:T(128)S(1)} %fusion.74, s32[92]{0:T(128)S(1)} %get-tuple-element.23), kind=kOutput, calls=%fused_computation.11 | convolution fusion | flops 36176240 | bytes 6161120 | tf_op jit(solution)/shard_map/ks,sic->kic/dot_general | solution.py:65
  160.1 0.0 all-to-all-done.1
  160.1 4.5 fusion.34
  164.6 0.3 convolution_bitcast_fusion.1
  164.9 65.4 %psum.21 = f32[64,64]{0,1:T(8,128)S(1)} all-reduce(f32[64,64]{0,1:T(8,128)S(1)} %convolution_bitcast_fusion.1), channel_id=1, replica_groups=mesh['rows'=64,'grp'=2] {'rows','grp'}, use_global_device_ids=true, to_apply=%region_3.6 | all-reduce | flops 4096 | bytes 32768 | tf_op jit(solution)/shard_map/psum | solution.py:78
  230.3 0.1 copy.97
  230.4 5.8 %cholesky.44 = f32[64,64]{1,0:T(8,128)S(1)} custom-call(f32[64,64]{1,0:T(8,128)S(1)} %fusion.52), custom_call_target="Cholesky" | custom-call | tf_op jit(solution)/shard_map/jit(cholesky)/cholesky | solution.py:79
  236.3 0.6 compare_reduce_fusion.1
  237.0 0.7 fusion.47
  237.6 4.9 %custom-call.6 = f32[1,64,64]{1,2,0:T(8,128)S(1)} custom-call(f32[1,64,64]{2,1,0:T(8,128)S(1)} %fusion.47), custom_call_target="InvertDiagBlocksLowerTriangular" | custom-call | tf_op jit(solution)/shard_map/jit(_solve_triangular)/triangular_solve | solution.py:80
  242.5 0.3 fusion.45
  242.8 0.9 convolution_convert_fusion
  243.7 0.0 all-gather.5.cloned.1.call-update
  243.7 0.8 copy.141
  244.6 0.8 gather_fusion.3
  245.3 8.4 %convert_bitcast_fusion = bf16[92,256,64]{1,2,0:T(8,128)(2,1)} fusion(bf16[92,256,256]{2,1,0:T(8,128)(2,1)} %param.13, bf16[92,256,64]{1,2,0:T(8,128)(2,1)S(1)} %gather_fusion.3, pred[92]{0:T(512)(128)(4,1)S(1)} %get-tuple-element.22), kind=kOutput, calls=%fused_computation.25 | convolution fusion | flops 774766592 | bytes 18088028 | tf_op jit(solution)/shard_map/sji,sjc->sic/dot_general | solution.py:56
  253.7 2.5 broadcast.76
  256.2 0.3 copy-done
  256.5 13.0 %scatter_fusion.1 = bf16[128,256,64]{1,2,0:T(8,128)(2,1)} fusion(bf16[128,256,64]{1,2,0:T(8,128)(2,1)} %broadcast.76, s32[92]{0:T(128)S(1)} %compare_select_fusion.1, bf16[92,256,64]{1,2,0:T(8,128)(2,1)S(1)} %copy-done), kind=kCustom, calls=%fused_computation.6 | custom fusion | bytes 9044336 | tf_op jit(solution)/shard_map/scatter | solution.py:62
  269.5 6.7 %all-to-all-start.2 = ((bf16[128,256,64]{1,2,0:T(8,128)(2,1)}), bf16[128,256,64]{1,2,0:T(8,128)(2,1)}, u32[]{:S(2)}, u32[]{:S(2)}) async-start(bf16[128,256,64]{1,2,0:T(8,128)(2,1)} %scatter_fusion.1), calls=%async_computation.2 | async-start | bytes 8388608 | tf_op jit(solution)/shard_map/all_to_all | solution.py:64
  276.2 83.2 %all-gather.5.cloned.1.call-done = bf16[65536,64]{0,1:T(8,128)(2,1)} async-done(((bf16[512,64]{0,1:T(8,128)(2,1)}), bf16[65536,64]{0,1:T(8,128)(2,1)}) %all-gather.5.cloned.1.call-update) | async-done | bytes 8388624 | tf_op jit(solution)/shard_map/all_gather | solution.py:50
  359.4 7.8 %copy.139 = bf16[8,256,8,256]{3,2,0,1:T(8,128)(2,1)} copy(bf16[8,256,8,256]{3,2,1,0:T(8,128)(2,1)} %bitcast.86) | data formatting | bytes 16777216 | tf_op jit(solution)/shard_map/reshape | solution.py:51
  367.2 4.2 gather_fusion.2
  371.3 10.8 %fusion.23 = f32[92,256,64]{1,2,0:T(8,128)} fusion(bf16[92,256,256]{2,1,0:T(8,128)(2,1)} %param.13, bf16[92,256,64]{1,2,0:T(8,128)(2,1)S(1)} %gather_fusion.2, pred[92]{0:T(512)(128)(4,1)S(1)} %compare_and_fusion), kind=kOutput, calls=%fused_computation.32 | convolution fusion | flops 773259264 | bytes 21102684 | tf_op jit(solution)/shard_map/sij,sjc->sic/dot_general | solution.py:52
  382.1 9.4 %fusion = f32[2,256,64]{1,0,2:T(2,128)S(1)} fusion(f32[92,256,64]{1,2,0:T(8,128)} %fusion.23, f32[92]{0:T(128)S(1)} %fusion.74, s32[92]{0:T(128)S(1)} %get-tuple-element.23), kind=kOutput, calls=%fused_computation.9 | convolution fusion | flops 36176240 | bytes 6161120 | tf_op jit(solution)/shard_map/ks,sic->kic/dot_general | solution.py:65
  391.5 0.0 all-to-all-done.2
  391.5 4.5 fusion.37
  396.0 0.3 convolution_bitcast_fusion
  396.3 0.0 copy-done.2
  396.3 0.2 fusion.76
  396.5 64.9 %all-reduce = (f32[64,64]{0,1:T(8,128)S(1)}, f32[64,64]{0,1:T(8,128)S(1)}) all-reduce(f32[64,64]{0,1:T(8,128)S(1)} %convolution_bitcast_fusion, f32[64,64]{0,1:T(8,128)S(1)} %fusion.76), channel_id=1, replica_groups=mesh['rows'=64,'grp'=2] {'rows','grp'}, use_global_device_ids=true, to_apply=%region_7.12 | all-reduce | flops 8192 | bytes 65536 | tf_op jit(solution)/shard_map/psum | solution.py:75
  461.4 0.7 copy.107
  462.1 0.1 copy.105
  462.2 5.8 %cholesky.55 = f32[64,64]{1,0:T(8,128)S(1)} custom-call(f32[64,64]{1,0:T(8,128)S(1)} %fusion.50), custom_call_target="Cholesky" | custom-call | tf_op jit(solution)/shard_map/jit(cholesky)/cholesky | solution.py:79
  468.1 0.6 compare_reduce_fusion
  468.7 0.7 fusion.48
  469.4 4.9 %custom-call.7 = f32[1,64,64]{1,2,0:T(8,128)S(1)} custom-call(f32[1,64,64]{2,1,0:T(8,128)S(1)} %fusion.48), custom_call_target="InvertDiagBlocksLowerTriangular" | custom-call | tf_op jit(solution)/shard_map/jit(_solve_triangular)/triangular_solve | solution.py:80
  474.3 0.3 fusion.43
  474.5 0.9 fusion.75
  (17 shorter events, 0.2 us)
Async XLA Ops:
  7.2 120.9 %all-gather.3.cloned.1.call-start = ((), (), s32[]{:S(2)}) async-start(), calls=%async_computation.3 | async-start | bytes 8454144 | tf_op jit(solution)/shard_map/all_gather | solution.py:50
  11.0 38.0 %all-to-all-start = ((s32[128,1,1]{2,1,0:T(1,128)}), s32[128,1,1]{2,1,0:T(1,128)S(1)}, u32[]{:S(2)}, u32[]{:S(2)}) async-start(s32[128,1,1]{2,1,0:T(1,128)} %copy.91), calls=%async_computation | async-start | bytes 131072 | tf_op jit(solution)/shard_map/all_to_all | solution.py:37
  33.2 2.8 copy-start.1
  49.0 11.0 %copy-start.3 = (s32[92]{0:T(128)S(1)}, s32[92]{0:T(128)}, u32[]{:S(2)}) copy-start(s32[92]{0:T(128)} %param.15) | copy-start | bytes 1108
  49.0 111.1 %all-to-all-start.1 = ((bf16[128,256,64]{1,2,0:T(8,128)(2,1)}), bf16[128,256,64]{1,2,0:T(8,128)(2,1)}, u32[]{:S(2)}, u32[]{:S(2)}) async-start(bf16[128,256,64]{1,2,0:T(8,128)(2,1)} %scatter_fusion), calls=%async_computation.1 | async-start | bytes 8388608 | tf_op jit(solution)/shard_map/all_to_all | solution.py:64
  59.7 299.7 %all-gather.5.cloned.1.call-start = ((), (), s32[]{:S(2)}) async-start(), calls=%async_computation.4 | async-start | bytes 8454144 | tf_op jit(solution)/shard_map/all_gather | solution.py:50
  253.7 2.8 copy-start
  269.5 122.0 %all-to-all-start.2 = ((bf16[128,256,64]{1,2,0:T(8,128)(2,1)}), bf16[128,256,64]{1,2,0:T(8,128)(2,1)}, u32[]{:S(2)}, u32[]{:S(2)}) async-start(bf16[128,256,64]{1,2,0:T(8,128)(2,1)} %scatter_fusion.1), calls=%async_computation.2 | async-start | bytes 8388608 | tf_op jit(solution)/shard_map/all_to_all | solution.py:64
  382.1 14.2 %copy-start.2 = (bf16[512,64]{0,1:T(8,128)(2,1)S(1)}, bf16[512,64]{0,1:T(8,128)(2,1)}, u32[]{:S(2)}) copy-start(bf16[512,64]{0,1:T(8,128)(2,1)} %convolution_convert_fusion) | copy-start | bytes 196612
Sparse Core Ops, SparseCore 0:
  10.8 117.1 all-gather.2
  243.8 115.5 all-gather.4
where the time goes:
time: 489 us; the launch traced here: 483 us
  waiting for transfers between devices  150 us (31%)
  blocking collectives  130 us (27%)
  matrix products  69 us (14%)
  local copies, waits for them, and re-layouts  61.2 us (13%)
  starting transfers between devices  29.2 us (6%)
  other arithmetic  28.1 us (6%)
  between operations  15.2 us (3%)
    all_gather x2, waiting for transfers between devices, on_device(): gathered = lax.all_gather(basis, ('rows', 'grp'), axis=0, tiled=True)  149 us
    psum x1, blocking collectives, on_device(): gram_part = lax.psum(gram_part, ('rows', 'grp'))  65.4 us
    psum x1, blocking collectives, on_device(): gram_part, projection = lax.psum((gram_part, projection), ('rows', 'grp'))  64.9 us
    scatter x2, local copies, waits for them, and re-layouts, on_device(): outgoing = jnp.zeros((outside, block_size, columns), jnp.bfloat16).at[slo...  26 us
    dot_general x2, matrix products, on_device(): jnp.einsum('sij,sjc->sic', kernel_blocks, partners, preferred_element_typ...  21.5 us
    dot_general x2, matrix products, on_device(): jnp.einsum('ks,sic->kic', row_select, forward, precision=lax.Precision.HI...  18.7 us
    all_to_all x2, starting transfers between devices, on_device(): lax.all_to_all(outgoing, ('rows', 'grp'), split_axis=0, concat_axis=0, ti...  17.4 us
    dot_general x2, matrix products, on_device(): jnp.einsum('sji,sjc->sic', kernel_blocks, own_tiles, preferred_element_ty...  16.8 us
  transfers between devices with their start and end apart: 5, of which 2 were waited for; matrix products, arithmetic and copies ran while one was open for 25% of the time, Pallas kernels for 0%

commit v1 on v0

v1 whole, which is shorter than its diff:
```python
import functools

import jax
import jax.numpy as jnp
from jax import lax
from jax.experimental import pallas as pl
from jax.experimental.pallas import tpu as pltpu
from jax.sharding import PartitionSpec as P

AXES = ("rows", "grp")
HIGHEST = lax.Precision.HIGHEST
CHUNK = 4
NT = (((1,), (1,)), ((), ()))
VMEM = pl.BlockSpec(memory_space=pltpu.VMEM)
SMEM = pl.BlockSpec(memory_space=pltpu.SMEM)
ANY = pl.BlockSpec(memory_space=pl.ANY)


def block_copies(blocks_ref, held, sems):
    chunks = blocks_ref.shape[0] // CHUNK
    return [
        pltpu.make_async_copy(
            blocks_ref.at[pl.ds(i * CHUNK, CHUNK)], held.at[pl.ds(i * CHUNK, CHUNK)], sems.at[i]
        )
        for i in range(chunks)
    ]


def wait_chunk(blocks_ref, held, sems, i):
    at = pl.ds(i * CHUNK, CHUNK)
    pltpu.make_async_copy(blocks_ref.at[at], held.at[at], sems.at[i]).wait()


def mirror_blocks(me, row_ref, col_ref, count_ref, tiles_ref, blocks_ref, held, sems, out_ref):
    live = count_ref[0]
    row_blocks = tiles_ref.shape[0]

    def visit(i, carry):
        wait_chunk(blocks_ref, held, sems, i)
        for j in range(CHUNK):
            s = i * CHUNK + j
            local = row_ref[s] - me * row_blocks
            place = jnp.where(s < live, col_ref[s] // row_blocks, 0)
            product = jnp.dot(tiles_ref[local], held[s], preferred_element_type=jnp.float32)
            out_ref[place] = product.astype(out_ref.dtype)
        return carry

    lax.fori_loop(0, held.shape[0] // CHUNK, visit, 0)


def place_tiles(me, wanted_ref, tiles_ref, out_ref):
    def visit(d, carry):
        @pl.when(wanted_ref[d] >= 0)
        def _():
            out_ref[d] = tiles_ref[wanted_ref[d]]

        return carry

    lax.fori_loop(0, me, visit, 0)


def first_kernel(me_ref, row_ref, col_ref, count_ref, basis_ref, blocks_ref, out_ref, tiles_ref, held, sems):
    for copy in block_copies(blocks_ref, held, sems):
        copy.start()
    row_blocks, _, size = tiles_ref.shape
    for j in range(row_blocks):
        rows = basis_ref[j * size : (j + 1) * size, :].astype(jnp.float32)
        tiles_ref[j] = rows.T.astype(tiles_ref.dtype)
    mirror_blocks(me_ref[0], row_ref, col_ref, count_ref, tiles_ref, blocks_ref, held, sems, out_ref)


def place_kernel(me_ref, wanted_ref, tiles_ref, given_ref, out_ref):
    del given_ref
    place_tiles(me_ref[0], wanted_ref, tiles_ref, out_ref)


def fold(square):
    half = square.shape[0] // 2
    return jnp.concatenate([square[:half], square[half:]], axis=1)


def unfold(folded):
    half = folded.shape[1] // 2
    return jnp.concatenate([folded[:, :half], folded[:, half:]], axis=0)


def image_kernel(
    with_projection, me_ref, row_ref, col_ref, count_ref, wanted_ref, tiles_ref, arrived_ref, blocks_ref,
    image_ref, sums_ref, held, sems,
):
    for copy in block_copies(blocks_ref, held, sems):
        copy.start()
    me, live = me_ref[0], count_ref[0]
    row_blocks = tiles_ref.shape[0]
    image_ref[...] = jnp.zeros_like(image_ref)

    def add_mirror(d, carry):
        @pl.when(wanted_ref[d] >= 0)
        def _():
            image_ref[wanted_ref[d]] += arrived_ref[d].astype(jnp.float32)

        return carry

    lax.fori_loop(0, me + 1, add_mirror, 0)

    def visit(i, carry):
        wait_chunk(blocks_ref, held, sems, i)
        for j in range(CHUNK):
            s = i * CHUNK + j
            local = row_ref[s] - me * row_blocks
            column = col_ref[s]
            owner = column // row_blocks
            tile = jnp.where(owner == me, tiles_ref[column - owner * row_blocks], arrived_ref[owner])
            tile = jnp.where(s < live, tile, jnp.zeros_like(tile))
            image_ref[local] += lax.dot_general(tile, held[s], NT, preferred_element_type=jnp.float32)
        return carry

    lax.fori_loop(0, held.shape[0] // CHUNK, visit, 0)

    def summed(left_ref):
        total = None
        for j in range(row_blocks):
            term = lax.dot_general(
                left_ref[j].astype(jnp.float32), image_ref[j], NT, precision=HIGHEST,
                preferred_element_type=jnp.float32,
            )
            total = term if total is None else total + term
        return fold(total)

    parts = [summed(image_ref)] + ([summed(tiles_ref)] if with_projection else [])
    half = sums_ref.shape[1] // len(parts)
    for c in range(2):
        for k, part in enumerate(parts):
            sums_ref[c, k * half : (k + 1) * half, :] = part[c * half : (c + 1) * half, :]


def inverse_factor(gram):
    n = gram.shape[0]
    row_at = lax.broadcasted_iota(jnp.int32, (n, n), 0)
    col_at = lax.broadcasted_iota(jnp.int32, (n, n), 1)
    identity = (row_at == col_at).astype(jnp.float32)
    work = jnp.concatenate([gram, identity], axis=1)
    at = lax.broadcasted_iota(jnp.int32, (n, 1), 0)
    scale = jnp.zeros((n, 1), jnp.float32)
    for k in range(n):
        row = work[k : k + 1, :]
        column = work[:, k : k + 1]
        pivot = row[:, k : k + 1]
        factor = jnp.where(at > k, column, 0.0) / pivot
        scale = jnp.where(at == k, pivot, scale)
        work = work - factor * row
    return work[:, n:] * (1.0 / jnp.sqrt(scale))


def whole_sum(core, own_ref, other_ref, k, parts):
    half = own_ref.shape[0] // parts
    own = own_ref[k * half : (k + 1) * half, :]
    other = other_ref[k * half : (k + 1) * half, :]
    first = jnp.where(core == 0, own, other)
    second = jnp.where(core == 0, other, own)
    return unfold(jnp.concatenate([first, second], axis=0))


def normal_kernel(
    total_rows, me_ref, row_ref, col_ref, count_ref, wanted_ref, own_ref, other_ref, image_ref, blocks_ref,
    out_ref, tiles_ref, held, sems,
):
    for copy in block_copies(blocks_ref, held, sems):
        copy.start()
    me = me_ref[0]
    inverse = inverse_factor(whole_sum(me % 2, own_ref, other_ref, 0, 1) / total_rows)
    for j in range(tiles_ref.shape[0]):
        tiles_ref[j] = jnp.dot(
            inverse, image_ref[j], precision=HIGHEST, preferred_element_type=jnp.float32
        ).astype(tiles_ref.dtype)
    mirror_blocks(me, row_ref, col_ref, count_ref, tiles_ref, blocks_ref, held, sems, out_ref)
    place_tiles(me, wanted_ref, tiles_ref, out_ref)


def last_kernel(total_rows, me_ref, own_ref, other_ref, image_ref, result_ref, projected_ref):
    core = me_ref[0] % 2
    inverse = inverse_factor(whole_sum(core, own_ref, other_ref, 0, 2) / total_rows)
    size = image_ref.shape[2]
    for j in range(image_ref.shape[0]):
        result = jnp.dot(inverse, image_ref[j], precision=HIGHEST, preferred_element_type=jnp.float32)
        result_ref[j * size : (j + 1) * size, :] = result.T
    projected_ref[...] = whole_sum(core, own_ref, other_ref, 1, 2) / total_rows


def sum_over_devices(halves):
    core = lax.axis_index("grp")
    swap = [(0, 1), (1, 0)]
    mine = lax.dynamic_index_in_dim(halves, core, 0, keepdims=False)
    given = lax.dynamic_index_in_dim(halves, 1 - core, 0, keepdims=False)
    mine = mine + lax.ppermute(given, "grp", swap)
    spread = jnp.broadcast_to(mine[None], (lax.axis_size("rows"),) + mine.shape)
    own = jnp.sum(lax.all_to_all(spread, "rows", 0, 0, tiled=True), axis=0)
    return own, lax.ppermute(own, "grp", swap)


def on_device(start_basis, kernel_blocks, block_row, block_col, block_count):
    devices = lax.axis_size(AXES)
    me = lax.axis_index(AXES)
    slots, size, _ = kernel_blocks.shape
    own_rows, columns = start_basis.shape
    row_blocks = own_rows // size
    total_rows = own_rows * devices
    me_array = me.reshape(1).astype(jnp.int32)

    owner = block_col // row_blocks
    alive = jnp.arange(slots, dtype=jnp.int32) < block_count[0]
    asked = jnp.max(
        jnp.where(
            (owner[None, :] == jnp.arange(devices, dtype=jnp.int32)[:, None]) & alive[None, :],
            (block_col - owner * row_blocks)[None, :],
            -1,
        ),
        axis=1,
    )
    wanted = lax.all_to_all(asked, AXES, split_axis=0, concat_axis=0, tiled=True)

    params = pltpu.CompilerParams(vmem_limit_bytes=48 * 1024 * 1024)
    scratch = [
        pltpu.VMEM(kernel_blocks.shape, kernel_blocks.dtype),
        pltpu.SemaphoreType.DMA((slots // CHUNK,)),
    ]
    tiles_shape = jax.ShapeDtypeStruct((row_blocks, columns, size), jnp.bfloat16)
    image_shape = jax.ShapeDtypeStruct((row_blocks, columns, size), jnp.float32)
    out_shape = jax.ShapeDtypeStruct((devices, columns, size), jnp.bfloat16)

    def image_of(tiles, arrived, with_projection):
        parts = 2 if with_projection else 1
        sums_shape = jax.ShapeDtypeStruct((2, parts * columns // 4, 2 * columns), jnp.float32)
        return pl.pallas_call(
            functools.partial(image_kernel, with_projection),
            out_shape=(image_shape, sums_shape),
            in_specs=[SMEM] * 5 + [VMEM] * 2 + [ANY],
            out_specs=(VMEM, VMEM),
            scratch_shapes=scratch,
            compiler_params=params,
        )(me_array, block_row, block_col, block_count, wanted, tiles, arrived, kernel_blocks)

    def exchange(outgoing):
        return lax.all_to_all(outgoing, AXES, split_axis=0, concat_axis=0, tiled=True)

    outgoing, tiles = pl.pallas_call(
        first_kernel,
        out_shape=(out_shape, tiles_shape),
        in_specs=[SMEM] * 4 + [VMEM, ANY],
        out_specs=(VMEM, VMEM),
        scratch_shapes=scratch,
        compiler_params=params,
    )(me_array, block_row, block_col, block_count, start_basis, kernel_blocks)
    outgoing = pl.pallas_call(
        place_kernel,
        out_shape=out_shape,
        in_specs=[SMEM] * 2 + [VMEM] * 2,
        out_specs=VMEM,
        input_output_aliases={3: 0},
        compiler_params=params,
    )(me_array, wanted, tiles, outgoing)
    image, sums = image_of(tiles, exchange(outgoing), False)
    own, other = sum_over_devices(sums)
    outgoing, tiles = pl.pallas_call(
        functools.partial(normal_kernel, total_rows),
        out_shape=(out_shape, tiles_shape),
        in_specs=[SMEM] * 5 + [VMEM] * 3 + [ANY],
        out_specs=(VMEM, VMEM),
        scratch_shapes=scratch,
        compiler_params=params,
    )(me_array, block_row, block_col, block_count, wanted, own, other, image, kernel_blocks)
    image, sums = image_of(tiles, exchange(outgoing), True)
    own, other = sum_over_devices(sums)
    return pl.pallas_call(
        functools.partial(last_kernel, total_rows),
        out_shape=(
            jax.ShapeDtypeStruct((own_rows, columns), jnp.float32),
            jax.ShapeDtypeStruct((columns, columns), jnp.float32),
        ),
        in_specs=[SMEM] + [VMEM] * 3,
        out_specs=(VMEM, VMEM),
        compiler_params=params,
    )(me_array, own, other, image)


def solution(mesh):
    in_specs = (
        P(AXES, None),
        P(AXES, None, None),
        P(AXES),
        P(AXES),
        P(AXES),
    )
    out_specs = (P(AXES, None), P())
    return jax.shard_map(
        on_device, mesh=mesh, in_specs=in_specs, out_specs=out_specs, check_vma=False
    )
```

time: 489 us -> 246 us (0.50); the launches traced: 483 us -> 246 us
  waiting for transfers between devices: 150 us -> 56 us
  matrix products: 69 us -> 0 us
  local copies, waits for them, and re-layouts: 61.2 us -> 10.1 us
  Pallas kernels: 0 us -> 46.4 us
  blocking collectives: 130 us -> 99.2 us
  other arithmetic: 28.1 us -> 3.32 us
  between operations: 15.2 us -> 1.44 us
    all_gather x2 -> x0, waiting for transfers between devices: 149 us -> none  [on_device(): gathered = lax.all_gather(basis, ('rows', 'grp'), axis=0, tiled=True)]
    psum x2 -> x0, blocking collectives: 130 us -> none  [the longest x1 65.4 us: on_device(): gram_part = lax.psum(gram_part, ('rows', 'grp'))]
    all_to_all x0 -> x3, blocking collectives: none -> 99.2 us  [the longest x1 57.8 us: exchange(): lax.all_to_all(outgoing, AXES, split_axis=0, concat_axis=0, tiled=True)]
    dot_general x13 -> x0, matrix products: 68.5 us -> none  [the longest x2 21.5 us: on_device(): jnp.einsum('sij,sjc->sic', kernel_blocks, partners, preferred_element_typ...]
    all_to_all x3 -> x2, waiting for transfers between devices: 0.01 us -> 52.6 us  [the longest x1 52.6 us: exchange(): lax.all_to_all(outgoing, AXES, split_axis=0, concat_axis=0, tiled=True)]
    pallas_call x0 -> x6, Pallas kernels: none -> 46.4 us  [the longest x2 19.6 us: image_of(): pl.pallas_call(functools.partial(image_kernel, with_projection), out_shap...]
    scatter x3 -> x0, local copies, waits for them, and re-layouts: 26.9 us -> none  [the longest x2 26 us: on_device(): outgoing = jnp.zeros((outside, block_size, columns), jnp.bfloat16).at[slo...]
    another operation x10 -> x0, other arithmetic: 24.1 us -> none  [the longest x6 13 us: on_device(): lower_factor = jnp.linalg.cholesky(gram_part / total_rows)]
  transfers between devices with their start and end apart: 5 -> 6, of which waited for: 2 -> 5; matrix products, arithmetic and copies ran while one was open for 25% -> 0% of each run, Pallas kernels for 0% -> 3%
where the time goes in v1:
time: 246 us
  blocking collectives  99.2 us (40%)
  waiting for transfers between devices  56 us (23%)
  Pallas kernels  46.4 us (19%)
  starting transfers between devices  29.1 us (12%)
  local copies, waits for them, and re-layouts  10.1 us (4%)
  other arithmetic  3.32 us (1%)
    all_to_all x1, blocking collectives, exchange(): lax.all_to_all(outgoing, AXES, split_axis=0, concat_axis=0, tiled=True)  57.8 us
    all_to_all x1, waiting for transfers between devices, exchange(): lax.all_to_all(outgoing, AXES, split_axis=0, concat_axis=0, tiled=True)  52.6 us
    all_to_all x2, blocking collectives, sum_over_devices(): own = jnp.sum(lax.all_to_all(spread, 'rows', 0, 0, tiled=True), axis=0)  41.4 us
    pallas_call x2, Pallas kernels, image_of(): pl.pallas_call(functools.partial(image_kernel, with_projection), out_shap...  19.6 us
    pallas_call x1, Pallas kernels, on_device(): pl.pallas_call(functools.partial(normal_kernel, total_rows), out_shape=(o...  12.7 us
    all_to_all x1, starting transfers between devices, exchange(): lax.all_to_all(outgoing, AXES, split_axis=0, concat_axis=0, tiled=True)  11.8 us
    all_to_all x1, starting transfers between devices, on_device(): lax.all_to_all(asked, AXES, split_axis=0, concat_axis=0, tiled=True)  11.5 us
    unnamed x15, local copies, waits for them, and re-layouts  8.37 us
  transfers between devices with their start and end apart: 6, of which 5 were waited for; matrix products, arithmetic and copies ran while one was open for 0% of the time, Pallas kernels for 3%

profile of v1, /device:TPU:1, one launch (start us, length us, event | category | flops | bytes accessed | tf_op | source)
XLA Modules:
  0.0 245.5 jit_solution(12913407324244355675)
XLA Ops:
  1.3 0.7 multiply_subtract_fusion
  2.0 0.1 select_reduce_fusion
  2.1 0.7 copy.16
  2.8 11.5 %all-to-all-start = ((s32[128,1,1]{2,1,0:T(1,128)}), s32[128,1,1]{2,1,0:T(1,128)S(1)}, u32[]{:S(2)}, u32[]{:S(2)}) async-start(s32[128,1,1]{2,1,0:T(1,128)} %copy.16), calls=%async_computation | async-start | bytes 131072 | tf_op jit(solution)/shard_map/all_to_all | solution.py:220
  14.3 1.0 copy.17.basis_ref
  15.3 0.0 copy-start.3
  15.3 0.6 copy-done.3
  16.0 0.0 copy-start.5
  16.0 0.7 copy-done.5
  16.6 6.6 %shard_map.68 = (bf16[128,64,256]{2,1,0:T(8,128)(2,1)S(1)}, bf16[2,64,256]{2,1,0:T(8,128)(2,1)S(1)}) custom-call(s32[1]{0:T(128)} %bitcast.me_ref, s32[92]{0:T(128)S(1)} %copy-done.3, s32[92]{0:T(128)S(1)} %copy-done.5, s32[1]{0:T(128)} %copy.20.count_ref, bf16[512,64]{1,0:T(8,128)(2,1)S(1)} %copy.17.basis_ref, bf16[92,256,256]{2,1,0:T(8,128)(2,1)} %blocks_ref.7), custom_call_target="tpu_custom_call" | custom-call | tf_op jit(solution)/shard_map/pallas_call | solution.py:246
  23.3 0.0 copy-start
  23.3 1.9 copy-done
  25.2 0.0 all-to-all-done
  25.2 2.4 reduce.wanted_ref
  27.6 0.0 copy-start.1
  27.6 2.2 copy-done.1
  29.8 0.6 shard_map.69
  30.3 0.0 copy-start.2
  30.4 2.0 copy-done.2
  32.3 0.0 copy-start.4
  32.3 0.0 copy-start.6
  32.3 11.8 %all-to-all-start.1 = ((bf16[128,64,256]{2,1,0:T(8,128)(2,1)}), bf16[128,64,256]{2,1,0:T(8,128)(2,1)}, u32[]{:S(2)}, u32[]{:S(2)}) async-start(bf16[128,64,256]{2,1,0:T(8,128)(2,1)} %copy-done.2), calls=%async_computation.1 | async-start | bytes 8388608 | tf_op jit(solution)/shard_map/all_to_all | solution.py:244
  44.2 52.6 %all-to-all-done.1.arrived_ref = bf16[128,64,256]{2,1,0:T(8,128)(2,1)} async-done(((bf16[128,64,256]{2,1,0:T(8,128)(2,1)}), bf16[128,64,256]{2,1,0:T(8,128)(2,1)}, u32[]{:S(2)}, u32[]{:S(2)}) %all-to-all-start.1) | async-done | bytes 4194336 | tf_op jit(solution)/shard_map/all_to_all | solution.py:244
  96.8 0.0 copy-done.4
  96.8 0.0 copy-done.6
  96.8 10.6 %shard_map.70 = (f32[2,64,256]{2,1,0:T(8,128)S(1)}, f32[2,16,128]{2,1,0:T(8,128)S(1)}) custom-call(s32[1]{0:T(128)} %bitcast.me_ref, s32[92]{0:T(128)S(1)} %copy-done.4, s32[92]{0:T(128)S(1)} %copy-done.6, s32[1]{0:T(128)} %copy.20.count_ref, s32[128]{0:T(128)S(1)} %reduce.wanted_ref, bf16[2,64,256]{2,1,0:T(8,128)(2,1)S(1)} %get-tuple-element.10.tiles_ref, ...), custom_call_target="tpu_custom_call" | custom-call | tf_op jit(solution)/shard_map/pallas_call | solution.py:234
  107.4 1.0 collective-permute-start
  108.4 0.8 collective-permute-done
  109.3 17.8 %all_to_all.31 = f32[64,16,128]{2,1,0:T(8,128)S(1)} all-to-all(f32[64,16,128]{2,1,0:T(8,128)S(1)} %broadcast_in_dim.18), channel_id=1, replica_groups=mesh['rows'=64,'grp'=2] {'rows'}, dimensions={0} | all-to-all | bytes 1048576 | tf_op jit(solution)/shard_map/all_to_all | solution.py:197
  127.1 0.1 reduce_sum.18.own_ref
  127.2 2.0 collective-permute-start.1
  129.2 0.8 collective-permute-done.1.other_ref
  130.0 12.7 %shard_map.71 = (bf16[128,64,256]{2,1,0:T(8,128)(2,1)S(1)}, bf16[2,64,256]{2,1,0:T(8,128)(2,1)S(1)}) custom-call(s32[1]{0:T(128)} %bitcast.me_ref, s32[92]{0:T(128)S(1)} %copy-done.4, s32[92]{0:T(128)S(1)} %copy-done.6, s32[1]{0:T(128)} %copy.20.count_ref, s32[128]{0:T(128)S(1)} %reduce.wanted_ref, f32[16,128]{1,0:T(8,128)S(1)} %reduce_sum.18.own_ref, ...), custom_call_target="tpu_custom_call" | custom-call | tf_op jit(solution)/shard_map/pallas_call | solution.py:264
  142.7 57.8 %all_to_all.32.arrived_ref = bf16[128,64,256]{2,1,0:T(8,128)(2,1)S(1)} all-to-all(bf16[128,64,256]{2,1,0:T(8,128)(2,1)S(1)} %get-tuple-element.15), channel_id=1, replica_groups=mesh['rows'=64,'grp'=2] {'rows','grp'}, dimensions={0} | all-to-all | bytes 8388608 | tf_op jit(solution)/shard_map/all_to_all | solution.py:244
  200.5 9.0 %shard_map.72 = (f32[2,64,256]{2,1,0:T(8,128)S(1)}, f32[2,32,128]{2,1,0:T(8,128)S(1)}) custom-call(s32[1]{0:T(128)} %bitcast.me_ref, s32[92]{0:T(128)S(1)} %copy-done.4, s32[92]{0:T(128)S(1)} %copy-done.6, s32[1]{0:T(128)} %copy.20.count_ref, s32[128]{0:T(128)S(1)} %reduce.wanted_ref, bf16[2,64,256]{2,1,0:T(8,128)(2,1)S(1)} %get-tuple-element.14.tiles_ref, ...), custom_call_target="tpu_custom_call" | custom-call | tf_op jit(solution)/shard_map/pallas_call | solution.py:234
  209.6 1.0 collective-permute-start.2
  210.6 0.8 collective-permute-done.2
  211.4 0.1 broadcast_in_dim.19
  211.6 23.5 %all_to_all.33 = f32[64,32,128]{2,1,0:T(8,128)S(1)} all-to-all(f32[64,32,128]{2,1,0:T(8,128)S(1)} %broadcast_in_dim.19), channel_id=1, replica_groups=mesh['rows'=64,'grp'=2] {'rows'}, dimensions={0} | all-to-all | bytes 2097152 | tf_op jit(solution)/shard_map/all_to_all | solution.py:197
  235.1 0.1 reduce_sum.19.own_ref
  235.2 1.8 collective-permute-start.3
  237.0 0.8 collective-permute-done.3.other_ref
  237.8 6.9 %shard_map.73 = (f32[512,64]{1,0:T(8,128)S(1)}, f32[64,64]{1,0:T(8,128)}) custom-call(s32[1]{0:T(128)} %bitcast.me_ref, f32[32,128]{1,0:T(8,128)S(1)} %reduce_sum.19.own_ref, f32[32,128]{1,0:T(8,128)S(1)} %collective-permute-done.3.other_ref, f32[2,64,256]{2,1,0:T(8,128)S(1)} %get-tuple-element.17.image_ref), custom_call_target="tpu_custom_call" | custom-call | tf_op jit(solution)/shard_map/pallas_call | solution.py:274
  244.8 0.8 copy.18
  (6 shorter events, 0.1 us)
Async XLA Ops:
  2.8 22.4 %all-to-all-start = ((s32[128,1,1]{2,1,0:T(1,128)}), s32[128,1,1]{2,1,0:T(1,128)S(1)}, u32[]{:S(2)}, u32[]{:S(2)}) async-start(s32[128,1,1]{2,1,0:T(1,128)} %copy.16), calls=%async_computation | async-start | bytes 131072 | tf_op jit(solution)/shard_map/all_to_all | solution.py:220
  15.3 0.7 copy-start.3
  16.0 0.7 copy-start.5
  23.3 1.9 copy-start
  27.6 2.2 copy-start.1
  30.3 2.0 copy-start.2
  32.3 64.5 %copy-start.4 = (s32[92]{0:T(128)S(1)}, s32[92]{0:T(128)}, u32[]{:S(2)}) copy-start(s32[92]{0:T(128)} %row_ref.7) | copy-start | bytes 1108
  32.3 64.5 %copy-start.6 = (s32[92]{0:T(128)S(1)}, s32[92]{0:T(128)}, u32[]{:S(2)}) copy-start(s32[92]{0:T(128)} %col_ref.7) | copy-start | bytes 1108
  32.3 64.5 %all-to-all-start.1 = ((bf16[128,64,256]{2,1,0:T(8,128)(2,1)}), bf16[128,64,256]{2,1,0:T(8,128)(2,1)}, u32[]{:S(2)}, u32[]{:S(2)}) async-start(bf16[128,64,256]{2,1,0:T(8,128)(2,1)} %copy-done.2), calls=%async_computation.1 | async-start | bytes 8388608 | tf_op jit(solution)/shard_map/all_to_all | solution.py:244
  107.4 1.8 collective-permute-start
  127.2 2.8 %collective-permute-start.1 = (f32[16,128]{1,0:T(8,128)S(1)}, f32[16,128]{1,0:T(8,128)S(1)}, u32[]{:S(2)}, u32[]{:S(2)}) collective-permute-start(f32[16,128]{1,0:T(8,128)S(1)} %reduce_sum.18.own_ref), channel_id=1, source_target_pairs={{0,1},{1,0},{2,3},{3,2},{4,5},{5,4},{6,7},{7,6},{8,9},{9,8},{10,11... | collective-permute-start | bytes 24584 | tf_op jit(solution)/shard_map/ppermute | solution.py:198
  209.6 1.9 collective-permute-start.2
  235.2 2.6 %collective-permute-start.3 = (f32[32,128]{1,0:T(8,128)S(1)}, f32[32,128]{1,0:T(8,128)S(1)}, u32[]{:S(2)}, u32[]{:S(2)}) collective-permute-start(f32[32,128]{1,0:T(8,128)S(1)} %reduce_sum.19.own_ref), channel_id=1, source_target_pairs={{0,1},{1,0},{2,3},{3,2},{4,5},{5,4},{6,7},{7,6},{8,9},{9,8},{10,11... | collective-permute-start | bytes 49160 | tf_op jit(solution)/shard_map/ppermute | solution.py:198

commit v2 on v1

v2 whole, which is shorter than its diff:
```python
import functools

import jax
import jax.numpy as jnp
from jax import lax
from jax.experimental import pallas as pl
from jax.experimental.pallas import tpu as pltpu
from jax.sharding import PartitionSpec as P

AXES = ("rows", "grp")
HIGHEST = lax.Precision.HIGHEST
CHUNK = 4
PANEL = 8
ME, LIVE, FIRST = 0, 1, 2
NT = (((1,), (1,)), ((), ()))
VMEM = pl.BlockSpec(memory_space=pltpu.VMEM)
SMEM = pl.BlockSpec(memory_space=pltpu.SMEM)
ANY = pl.BlockSpec(memory_space=pl.ANY)
MIB = 1024 * 1024


def block_copy(blocks_ref, held, sems, i):
    at = pl.ds(i * CHUNK, CHUNK)
    return pltpu.make_async_copy(blocks_ref.at[at], held.at[at], sems.at[i])


def start_blocks(live, blocks_ref, held, sems):
    chunks = (live + CHUNK - 1) // CHUNK

    def start(i, carry):
        block_copy(blocks_ref, held, sems, i).start()
        return carry

    lax.fori_loop(0, chunks, start, 0)
    return chunks


def multiply_mirrors(me, table_ref, live, chunks, tiles_ref, blocks_ref, held, sems, out_ref):
    row_blocks = tiles_ref.shape[0]

    def visit(i, carry):
        block_copy(blocks_ref, held, sems, i).wait()
        for j in range(CHUNK):
            s = i * CHUNK + j
            local = table_ref[FIRST + s] - me * row_blocks
            place = jnp.where(s < live, table_ref[FIRST + held.shape[0] + s] // row_blocks, 0)
            product = jnp.dot(tiles_ref[local], held[s], preferred_element_type=jnp.float32)
            out_ref[place] = product.astype(out_ref.dtype)
        return carry

    lax.fori_loop(0, chunks, visit, 0)


def place_tiles(me, wanted_ref, tiles_ref, out_ref):
    def visit(i, carry):
        for j in range(CHUNK):
            d = jnp.minimum(i * CHUNK + j, me - 1)
            out_ref[d] = tiles_ref[jnp.maximum(wanted_ref[d], 0)]
        return carry

    lax.fori_loop(0, (me + CHUNK - 1) // CHUNK, visit, 0)


def ask_kernel(row_blocks, count_ref, col_ref, out_ref):
    devices, slots = out_ref.shape[0], col_ref.shape[1]
    column = jnp.broadcast_to(col_ref[...], (devices, slots))
    owner = column // row_blocks
    device = lax.broadcasted_iota(jnp.int32, (devices, slots), 0)
    alive = lax.broadcasted_iota(jnp.int32, (devices, slots), 1) < count_ref[0]
    block = jnp.where((owner == device) & alive, column - owner * row_blocks, -1)
    asked = jnp.max(block, axis=1, keepdims=True)
    out_ref[...] = jnp.broadcast_to(asked, (devices, out_ref.shape[2]))[:, None, :]


def first_kernel(table_ref, basis_ref, blocks_ref, out_ref, tiles_ref, held, sems):
    live = table_ref[LIVE]
    chunks = start_blocks(live, blocks_ref, held, sems)
    row_blocks, _, size = tiles_ref.shape
    for j in range(row_blocks):
        tiles_ref[j] = basis_ref[:, j * size : (j + 1) * size]
    multiply_mirrors(table_ref[ME], table_ref, live, chunks, tiles_ref, blocks_ref, held, sems, out_ref)


def place_kernel(table_ref, wanted_ref, tiles_ref, given_ref, out_ref):
    me = table_ref[ME]
    place_tiles(me, wanted_ref, tiles_ref, out_ref)

    def keep(i, carry):
        for j in range(CHUNK):
            d = jnp.minimum(me + i * CHUNK + j, out_ref.shape[0] - 1)
            out_ref[d] = given_ref[d]
        return carry

    lax.fori_loop(0, (out_ref.shape[0] - me + CHUNK - 1) // CHUNK, keep, 0)


def fold(square):
    half = square.shape[0] // 2
    return jnp.concatenate([square[:half], square[half:]], axis=1)


def unfold(folded):
    half = folded.shape[1] // 2
    return jnp.concatenate([folded[:, :half], folded[:, half:]], axis=0)


def image_kernel(
    with_projection, table_ref, wanted_ref, tiles_ref, arrived_ref, blocks_ref,
    image_ref, own_ref, given_ref, held, sems,
):
    me, live = table_ref[ME], table_ref[LIVE]
    chunks = start_blocks(live, blocks_ref, held, sems)
    row_blocks = tiles_ref.shape[0]
    image_ref[...] = jnp.zeros_like(image_ref)

    def add_mirror(d, carry):
        @pl.when(wanted_ref[d] >= 0)
        def _():
            image_ref[wanted_ref[d]] += arrived_ref[d].astype(jnp.float32)

        return carry

    lax.fori_loop(0, me + 1, add_mirror, 0)

    def visit(i, carry):
        block_copy(blocks_ref, held, sems, i).wait()
        for j in range(CHUNK):
            s = i * CHUNK + j
            local = table_ref[FIRST + s] - me * row_blocks
            column = table_ref[FIRST + held.shape[0] + s]
            owner = column // row_blocks
            tile = jnp.where(owner == me, tiles_ref[column - owner * row_blocks], arrived_ref[owner])
            tile = jnp.where(s < live, tile, jnp.zeros_like(tile))
            image_ref[local] += lax.dot_general(tile, held[s], NT, preferred_element_type=jnp.float32)
        return carry

    lax.fori_loop(0, chunks, visit, 0)

    def summed(left_ref):
        total = None
        for j in range(image_ref.shape[0]):
            term = lax.dot_general(
                left_ref[j].astype(jnp.float32), image_ref[j], NT, precision=HIGHEST,
                preferred_element_type=jnp.float32,
            )
            total = term if total is None else total + term
        return fold(total)

    parts = [summed(image_ref)] + ([summed(tiles_ref)] if with_projection else [])
    half = own_ref.shape[0] // len(parts)
    for k, folded in enumerate(parts):
        at = slice(k * half, (k + 1) * half)
        low, high = folded[:half], folded[half:]
        own_ref[at, :] = jnp.where(me % 2 == 0, low, high)
        given_ref[at, :] = jnp.where(me % 2 == 0, high, low)


def inverse_factor(gram):
    n = gram.shape[0]
    row_at = lax.broadcasted_iota(jnp.int32, (n, n), 0)
    col_at = lax.broadcasted_iota(jnp.int32, (n, n), 1)
    work = jnp.concatenate([gram, (row_at == col_at).astype(jnp.float32)], axis=1)
    at = lax.broadcasted_iota(jnp.int32, work.shape, 0)
    pivots = jnp.zeros(work.shape, jnp.float32)
    for k in range(0, n, PANEL):
        spread = [jnp.broadcast_to(work[:, k + j : k + j + 1], work.shape) for j in range(PANEL)]
        rows = [work[k + j : k + j + 1, :] for j in range(PANEL)]
        for j in range(PANEL):
            pivot = spread[j][k + j : k + j + 1, :]
            pivots = jnp.where(at == k + j, pivot, pivots)
            share = 1.0 / pivot
            scaled = rows[j] * share
            for m in range(j + 1, PANEL):
                spread[m] = spread[m] - spread[j] * (spread[m][k + j : k + j + 1, :] * share)
                rows[m] = rows[m] - spread[j][k + m : k + m + 1, :] * scaled
            rows[j] = scaled
        for j in range(PANEL):
            work = work - jnp.where(at > k + j, spread[j], 0.0) * rows[j]
    return work[:, n:] * (1.0 / jnp.sqrt(pivots[:, n:]))


def whole_sum(core, own_ref, other_ref, k, parts):
    half = own_ref.shape[0] // parts
    own = own_ref[k * half : (k + 1) * half, :]
    other = other_ref[k * half : (k + 1) * half, :]
    first = jnp.where(core == 0, own, other)
    second = jnp.where(core == 0, other, own)
    return unfold(jnp.concatenate([first, second], axis=0))


def normal_kernel(
    total_rows, table_ref, wanted_ref, own_ref, other_ref, image_ref, blocks_ref,
    out_ref, tiles_ref, held, sems,
):
    me, live = table_ref[ME], table_ref[LIVE]
    chunks = start_blocks(live, blocks_ref, held, sems)
    inverse = inverse_factor(whole_sum(me % 2, own_ref, other_ref, 0, 1) / total_rows)
    for j in range(tiles_ref.shape[0]):
        tiles_ref[j] = jnp.dot(
            inverse, image_ref[j], precision=HIGHEST, preferred_element_type=jnp.float32
        ).astype(tiles_ref.dtype)
    multiply_mirrors(me, table_ref, live, chunks, tiles_ref, blocks_ref, held, sems, out_ref)
    place_tiles(me, wanted_ref, tiles_ref, out_ref)


def last_kernel(total_rows, table_ref, own_ref, other_ref, image_ref, result_ref, projected_ref):
    core = table_ref[ME] % 2
    inverse = inverse_factor(whole_sum(core, own_ref, other_ref, 0, 2) / total_rows)
    size = image_ref.shape[2]
    for j in range(image_ref.shape[0]):
        result_ref[:, j * size : (j + 1) * size] = jnp.dot(
            inverse, image_ref[j], precision=HIGHEST, preferred_element_type=jnp.float32
        )
    projected_ref[...] = whole_sum(core, own_ref, other_ref, 1, 2) / total_rows


def sum_over_devices(mine, given):
    swap = [(0, 1), (1, 0)]
    mine = mine + lax.ppermute(given, "grp", swap)
    spread = jnp.broadcast_to(mine[None], (lax.axis_size("rows"),) + mine.shape)
    own = jnp.sum(lax.all_to_all(spread, "rows", 0, 0, tiled=True), axis=0)
    return own, lax.ppermute(own, "grp", swap)


def exchange(outgoing):
    return lax.all_to_all(outgoing, AXES, split_axis=0, concat_axis=0, tiled=True)


def on_device(start_basis, kernel_blocks, block_row, block_col, block_count):
    devices = lax.axis_size(AXES)
    me = lax.axis_index(AXES)
    slots, size, _ = kernel_blocks.shape
    own_rows, columns = start_basis.shape
    row_blocks = own_rows // size
    total_rows = own_rows * devices

    asked = pl.pallas_call(
        functools.partial(ask_kernel, row_blocks),
        out_shape=jax.ShapeDtypeStruct((devices, 1, 128), jnp.int32),
        in_specs=[SMEM, VMEM],
        out_specs=VMEM,
        name="ask",
    )(block_count, block_col[None, :])
    wanted = exchange(asked)[:, 0, 0]
    table = jnp.concatenate([me.reshape(1).astype(jnp.int32), block_count, block_row, block_col])

    params = pltpu.CompilerParams(vmem_limit_bytes=48 * MIB)
    scratch = [
        pltpu.VMEM(kernel_blocks.shape, kernel_blocks.dtype),
        pltpu.SemaphoreType.DMA((slots // CHUNK,)),
    ]
    tiles_shape = jax.ShapeDtypeStruct((row_blocks, columns, size), jnp.bfloat16)
    image_shape = jax.ShapeDtypeStruct((row_blocks, columns, size), jnp.float32)
    out_shape = jax.ShapeDtypeStruct((devices, columns, size), jnp.bfloat16)

    def image_of(tiles, arrived, with_projection):
        parts = 2 if with_projection else 1
        half = jax.ShapeDtypeStruct((parts * columns // 4, 2 * columns), jnp.float32)
        return pl.pallas_call(
            functools.partial(image_kernel, with_projection),
            out_shape=(image_shape, half, half),
            in_specs=[SMEM] * 2 + [VMEM] * 2 + [ANY],
            out_specs=(VMEM, VMEM, VMEM),
            scratch_shapes=scratch,
            compiler_params=params,
            name="image",
        )(table, wanted, tiles, arrived, kernel_blocks)

    outgoing, tiles = pl.pallas_call(
        first_kernel,
        out_shape=(out_shape, tiles_shape),
        in_specs=[SMEM] + [VMEM, ANY],
        out_specs=(VMEM, VMEM),
        scratch_shapes=scratch,
        compiler_params=params,
        name="first",
    )(table, start_basis.T, kernel_blocks)
    outgoing = pl.pallas_call(
        place_kernel,
        out_shape=out_shape,
        in_specs=[SMEM] * 2 + [VMEM] * 2,
        out_specs=VMEM,
        compiler_params=params,
        name="place",
    )(table, wanted, tiles, outgoing)
    image, own, given = image_of(tiles, exchange(outgoing), False)
    own, other = sum_over_devices(own, given)
    outgoing, tiles = pl.pallas_call(
        functools.partial(normal_kernel, total_rows),
        out_shape=(out_shape, tiles_shape),
        in_specs=[SMEM] * 2 + [VMEM] * 3 + [ANY],
        out_specs=(VMEM, VMEM),
        scratch_shapes=scratch,
        compiler_params=params,
        name="normal",
    )(table, wanted, own, other, image, kernel_blocks)
    image, own, given = image_of(tiles, exchange(outgoing), True)
    own, other = sum_over_devices(own, given)
    result, projected = pl.pallas_call(
        functools.partial(last_kernel, total_rows),
        out_shape=(
            jax.ShapeDtypeStruct((columns, own_rows), jnp.float32),
            jax.ShapeDtypeStruct((columns, columns), jnp.float32),
        ),
        in_specs=[SMEM] + [VMEM] * 3,
        out_specs=(VMEM, VMEM),
        compiler_params=params,
        name="last",
    )(table, own, other, image)
    return result.T, projected


def solution(mesh):
    in_specs = (
        P(AXES, None),
        P(AXES, None, None),
        P(AXES),
        P(AXES),
        P(AXES),
    )
    out_specs = (P(AXES, None), P())
    return jax.shard_map(
        on_device, mesh=mesh, in_specs=in_specs, out_specs=out_specs, check_vma=False
    )
```

time: 246 us -> 222 us (0.902)
  blocking collectives: 99.2 us -> 154 us
  waiting for transfers between devices: 56 us -> 3.34 us
  starting transfers between devices: 29.1 us -> 16.7 us
  Pallas kernels: 46.4 us -> 39.8 us
  local copies, waits for them, and re-layouts: 10.1 us -> 5.37 us
    all_to_all x1 -> x2, blocking collectives: 57.8 us -> 115 us  [exchange(): lax.all_to_all(outgoing, AXES, split_axis=0, concat_axis=0, tiled=True)]
    all_to_all x1, waiting for transfers between devices: 52.6 us -> 0.01 us  [exchange(): lax.all_to_all(outgoing, AXES, split_axis=0, concat_axis=0, tiled=True)]
    all_to_all x1 -> x0, starting transfers between devices: 11.5 us -> none  [on_device(): lax.all_to_all(asked, AXES, split_axis=0, concat_axis=0, tiled=True)]
    unnamed x15 -> x4, local copies, waits for them, and re-layouts: 8.37 us -> 2.77 us
    pallas_call x1, Pallas kernels: 12.7 us -> 7.75 us  [on_device(): pl.pallas_call(functools.partial(normal_kernel, total_rows), out_shape=(o...]
    pallas_call x1, Pallas kernels: 6.93 us -> 3.13 us  [on_device(): pl.pallas_call(functools.partial(last_kernel, total_rows), out_shape=(jax...]
  transfers between devices with their start and end apart: 6 -> 5, of which waited for: 5 -> 4; matrix products, arithmetic and copies ran while one was open for 0% -> 0% of each run, Pallas kernels for 3% -> 3%
where the time goes in v2:
time: 222 us
  blocking collectives  154 us (69%)
  Pallas kernels  39.8 us (18%)
  starting transfers between devices  16.7 us (8%)
  local copies, waits for them, and re-layouts  5.37 us (2%)
  waiting for transfers between devices  3.34 us (2%)
    all_to_all x2, blocking collectives, exchange(): lax.all_to_all(outgoing, AXES, split_axis=0, concat_axis=0, tiled=True)  115 us
    all_to_all x2, blocking collectives, sum_over_devices(): own = jnp.sum(lax.all_to_all(spread, 'rows', 0, 0, tiled=True), axis=0)  39 us
    pallas_call x2, Pallas kernels, image_of(): pl.pallas_call(functools.partial(image_kernel, with_projection), out_shap...  17.9 us
    all_to_all x1, starting transfers between devices, exchange(): lax.all_to_all(outgoing, AXES, split_axis=0, concat_axis=0, tiled=True)  11.5 us
    pallas_call x1, Pallas kernels, on_device(): pl.pallas_call(functools.partial(normal_kernel, total_rows), out_shape=(o...  7.75 us
    pallas_call x1, Pallas kernels, on_device(): pl.pallas_call(first_kernel, out_shape=(out_shape, tiles_shape), in_specs...  6.74 us
  transfers between devices with their start and end apart: 5, of which 4 were waited for; matrix products, arithmetic and copies ran while one was open for 0% of the time, Pallas kernels for 3%

profile of v2, /device:TPU:1, one launch (start us, length us, event | category | flops | bytes accessed | tf_op | source)
XLA Modules:
  0.0 221.9 jit_solution(14567104247984916912)
XLA Ops:
  1.3 1.5 ask.1
  2.8 11.5 %all-to-all-start = ((s32[128,1,128]{2,1,0:T(1,128)}), s32[128,1,128]{2,1,0:T(1,128)S(1)}, u32[]{:S(2)}, u32[]{:S(2)}) async-start(s32[128,1,128]{2,1,0:T(1,128)} %ask.1), calls=%async_computation | async-start | bytes 131072 | tf_op jit(solution)/shard_map/all_to_all | solution.py:226
  14.3 0.8 pad_add_fusion.table_ref
  15.0 0.0 copy-start.1
  15.0 0.8 copy-done.1
  15.9 6.7 %first.1 = (bf16[128,64,256]{2,1,0:T(8,128)(2,1)S(1)}, bf16[2,64,256]{2,1,0:T(8,128)(2,1)S(1)}) custom-call(s32[186]{0:T(256)S(1)} %pad_add_fusion.table_ref, bf16[64,512]{1,0:T(8,128)(2,1)S(1)} %bitcast.4, bf16[92,256,256]{2,1,0:T(8,128)(2,1)} %blocks_ref.7), custom_call_target="tpu_custom_call" | custom-call | tf_op jit(solution)/shard_map/first/pallas_call | solution.py:269
  22.6 0.0 copy-start
  22.6 1.9 copy-done
  24.6 0.0 all-to-all-done
  24.6 2.4 %slice_reduce_fusion.wanted_ref = s32[128]{0:T(128)S(1)} fusion(s32[128,1,128]{2,1,0:T(1,128)S(1)} %all-to-all-done), kind=kLoop, calls=%fused_computation | loop fusion | bytes 1024 | tf_op jit(solution)/shard_map/slice | solution.py:244
  27.0 2.8 %place.1 = bf16[128,64,256]{2,1,0:T(8,128)(2,1)S(1)} custom-call(s32[186]{0:T(256)S(1)} %pad_add_fusion.table_ref, s32[128]{0:T(128)S(1)} %slice_reduce_fusion.wanted_ref, bf16[2,64,256]{2,1,0:T(8,128)(2,1)S(1)} %get-tuple-element.14.tiles_ref, bf16[128,64,256]{2,1,0:T(8,128)(2,1)} %copy-done), custom_call_target="tpu_custom_call" | custom-call | tf_op jit(solution)/shard_map/place/pallas_call | solution.py:278
  29.8 59.2 %all_to_all.25.arrived_ref = bf16[128,64,256]{2,1,0:T(8,128)(2,1)S(1)} all-to-all(bf16[128,64,256]{2,1,0:T(8,128)(2,1)S(1)} %place.1), channel_id=1, replica_groups=mesh['rows'=64,'grp'=2] {'rows','grp'}, dimensions={0} | all-to-all | bytes 8388608 | tf_op jit(solution)/shard_map/all_to_all | solution.py:226
  89.0 8.9 %image.2 = (f32[2,64,256]{2,1,0:T(8,128)S(1)}, f32[16,128]{1,0:T(8,128)S(1)}, f32[16,128]{1,0:T(8,128)S(1)}) custom-call(s32[186]{0:T(256)S(1)} %pad_add_fusion.table_ref, s32[128]{0:T(128)S(1)} %slice_reduce_fusion.wanted_ref, bf16[2,64,256]{2,1,0:T(8,128)(2,1)S(1)} %get-tuple-element.14.tiles_ref, bf16[128,64,256]{2,1,0:T(8,128)(2,1)S(1)} %all_to_all.25.arrived_ref, ...), custom_call_target="tpu_custom_call" | custom-call | tf_op jit(solution)/shard_map/image/pallas_call | solution.py:259
  97.9 1.0 collective-permute-start
  98.9 0.8 collective-permute-done
  99.8 16.6 %all_to_all.26 = f32[64,16,128]{2,1,0:T(8,128)S(1)} all-to-all(f32[64,16,128]{2,1,0:T(8,128)S(1)} %broadcast_in_dim.7), channel_id=1, replica_groups=mesh['rows'=64,'grp'=2] {'rows'}, dimensions={0} | all-to-all | bytes 1048576 | tf_op jit(solution)/shard_map/all_to_all | solution.py:221
  116.4 0.1 reduce_sum.18.own_ref
  116.5 1.7 collective-permute-start.1
  118.2 0.8 collective-permute-done.1.other_ref
  119.0 7.7 %normal.1 = (bf16[128,64,256]{2,1,0:T(8,128)(2,1)S(1)}, bf16[2,64,256]{2,1,0:T(8,128)(2,1)S(1)}) custom-call(s32[186]{0:T(256)S(1)} %pad_add_fusion.table_ref, s32[128]{0:T(128)S(1)} %slice_reduce_fusion.wanted_ref, f32[16,128]{1,0:T(8,128)S(1)} %reduce_sum.18.own_ref, f32[16,128]{1,0:T(8,128)S(1)} %collective-permute-done.1.other_ref, ...), custom_call_target="tpu_custom_call" | custom-call | tf_op jit(solution)/shard_map/normal/pallas_call | solution.py:288
  126.7 56.3 %all_to_all.27.arrived_ref = bf16[128,64,256]{2,1,0:T(8,128)(2,1)S(1)} all-to-all(bf16[128,64,256]{2,1,0:T(8,128)(2,1)S(1)} %get-tuple-element.20), channel_id=1, replica_groups=mesh['rows'=64,'grp'=2] {'rows','grp'}, dimensions={0} | all-to-all | bytes 8388608 | tf_op jit(solution)/shard_map/all_to_all | solution.py:226
  183.0 9.0 %image.3 = (f32[2,64,256]{2,1,0:T(8,128)S(1)}, f32[32,128]{1,0:T(8,128)S(1)}, f32[32,128]{1,0:T(8,128)S(1)}) custom-call(s32[186]{0:T(256)S(1)} %pad_add_fusion.table_ref, s32[128]{0:T(128)S(1)} %slice_reduce_fusion.wanted_ref, bf16[2,64,256]{2,1,0:T(8,128)(2,1)S(1)} %get-tuple-element.19.tiles_ref, bf16[128,64,256]{2,1,0:T(8,128)(2,1)S(1)} %all_to_all.27.arrived_ref, ...), custom_call_target="tpu_custom_call" | custom-call | tf_op jit(solution)/shard_map/image/pallas_call | solution.py:259
  192.1 1.0 collective-permute-start.2
  193.1 0.8 collective-permute-done.2
  193.9 0.1 broadcast_in_dim.8
  194.0 22.3 %all_to_all.28 = f32[64,32,128]{2,1,0:T(8,128)S(1)} all-to-all(f32[64,32,128]{2,1,0:T(8,128)S(1)} %broadcast_in_dim.8), channel_id=1, replica_groups=mesh['rows'=64,'grp'=2] {'rows'}, dimensions={0} | all-to-all | bytes 2097152 | tf_op jit(solution)/shard_map/all_to_all | solution.py:221
  216.4 0.1 reduce_sum.19.own_ref
  216.5 1.5 collective-permute-start.3
  217.9 0.8 collective-permute-done.3.other_ref
  218.8 3.1 %last.1 = (f32[64,512]{1,0:T(8,128)}, f32[64,64]{1,0:T(8,128)}) custom-call(s32[186]{0:T(256)S(1)} %pad_add_fusion.table_ref, f32[32,128]{1,0:T(8,128)S(1)} %reduce_sum.19.own_ref, f32[32,128]{1,0:T(8,128)S(1)} %collective-permute-done.3.other_ref, f32[2,64,256]{2,1,0:T(8,128)S(1)} %get-tuple-element.23.image_ref), custom_call_target="tpu_custom_call" | custom-call | tf_op jit(solution)/shard_map/last/pallas_call | solution.py:299
  (3 shorter events, 0.0 us)
Async XLA Ops:
  2.8 21.8 %all-to-all-start = ((s32[128,1,128]{2,1,0:T(1,128)}), s32[128,1,128]{2,1,0:T(1,128)S(1)}, u32[]{:S(2)}, u32[]{:S(2)}) async-start(s32[128,1,128]{2,1,0:T(1,128)} %ask.1), calls=%async_computation | async-start | bytes 131072 | tf_op jit(solution)/shard_map/all_to_all | solution.py:226
  15.0 0.8 copy-start.1
  22.6 1.9 copy-start
  97.9 1.8 collective-permute-start
  116.5 2.5 %collective-permute-start.1 = (f32[16,128]{1,0:T(8,128)S(1)}, f32[16,128]{1,0:T(8,128)S(1)}, u32[]{:S(2)}, u32[]{:S(2)}) collective-permute-start(f32[16,128]{1,0:T(8,128)S(1)} %reduce_sum.18.own_ref), channel_id=1, source_target_pairs={{0,1},{1,0},{2,3},{3,2},{4,5},{5,4},{6,7},{7,6},{8,9},{9,8},{10,11... | collective-permute-start | bytes 24584 | tf_op jit(solution)/shard_map/ppermute | solution.py:222
  192.1 1.8 collective-permute-start.2
  216.5 2.3 %collective-permute-start.3 = (f32[32,128]{1,0:T(8,128)S(1)}, f32[32,128]{1,0:T(8,128)S(1)}, u32[]{:S(2)}, u32[]{:S(2)}) collective-permute-start(f32[32,128]{1,0:T(8,128)S(1)} %reduce_sum.19.own_ref), channel_id=1, source_target_pairs={{0,1},{1,0},{2,3},{3,2},{4,5},{5,4},{6,7},{7,6},{8,9},{9,8},{10,11... | collective-permute-start | bytes 49160 | tf_op jit(solution)/shard_map/ppermute | solution.py:222

commit v3 on v2

--- a/solution.py
+++ b/solution.py
@@ -11,6 +11,7 @@
 HIGHEST = lax.Precision.HIGHEST
 CHUNK = 4
 PANEL = 8
+ROWS, LANES = 8, 128
 ME, LIVE, FIRST = 0, 1, 2
 NT = (((1,), (1,)), ((), ()))
 VMEM = pl.BlockSpec(memory_space=pltpu.VMEM)
@@ -51,14 +52,14 @@
     lax.fori_loop(0, chunks, visit, 0)
 
 
-def place_tiles(me, wanted_ref, tiles_ref, out_ref):
+def place_tiles(start, end, wanted_ref, tiles_ref, out_ref):
     def visit(i, carry):
         for j in range(CHUNK):
-            d = jnp.minimum(i * CHUNK + j, me - 1)
+            d = jnp.minimum(start + i * CHUNK + j, end - 1)
             out_ref[d] = tiles_ref[jnp.maximum(wanted_ref[d], 0)]
         return carry
 
-    lax.fori_loop(0, (me + CHUNK - 1) // CHUNK, visit, 0)
+    lax.fori_loop(0, (end - start + CHUNK - 1) // CHUNK, visit, 0)
 
 
 def ask_kernel(row_blocks, count_ref, col_ref, out_ref):
@@ -81,27 +82,66 @@
     multiply_mirrors(table_ref[ME], table_ref, live, chunks, tiles_ref, blocks_ref, held, sems, out_ref)
 
 
-def place_kernel(table_ref, wanted_ref, tiles_ref, given_ref, out_ref):
+def place_kernel(table_ref, asked_ref, tiles_ref, given_ref, out_ref, wanted_ref, sems):
     me = table_ref[ME]
-    place_tiles(me, wanted_ref, tiles_ref, out_ref)
-
-    def keep(i, carry):
+    groups = sems.shape[0]
+    size = out_ref.shape[0] // groups
+    first = me // size
+
+    def copy_of(g):
+        at = pl.ds(g * size, size)
+        return pltpu.make_async_copy(given_ref.at[at], out_ref.at[at], sems.at[g])
+
+    def start(g, carry):
+        copy_of(g).start()
+        return carry
+
+    def wait(g, carry):
+        copy_of(g).wait()
+        return carry
+
+    def compact(i, carry):
         for j in range(CHUNK):
-            d = jnp.minimum(me + i * CHUNK + j, out_ref.shape[0] - 1)
-            out_ref[d] = given_ref[d]
-        return carry
-
-    lax.fori_loop(0, (out_ref.shape[0] - me + CHUNK - 1) // CHUNK, keep, 0)
+            wanted_ref[i * CHUNK + j] = asked_ref[i * CHUNK + j, 0, 0]
+        return carry
+
+    lax.fori_loop(first, groups, start, 0)
+    lax.fori_loop(0, wanted_ref.shape[0] // CHUNK, compact, 0)
+    place_tiles(0, first * size, wanted_ref, tiles_ref, out_ref)
+    lax.fori_loop(first, groups, wait, 0)
+    place_tiles(first * size, me, wanted_ref, tiles_ref, out_ref)
+
+
+def row_of(k):
+    return slice(k * LANES, (k + 1) * LANES)
 
 
 def fold(square):
     half = square.shape[0] // 2
-    return jnp.concatenate([square[:half], square[half:]], axis=1)
-
-
-def unfold(folded):
-    half = folded.shape[1] // 2
-    return jnp.concatenate([folded[:, :half], folded[:, half:]], axis=0)
+    row_at = lax.broadcasted_iota(jnp.int32, (half, half), 0)
+    col_at = lax.broadcasted_iota(jnp.int32, (half, half), 1)
+    corner = square[half:, half:]
+    mixed = jnp.where(row_at >= col_at, square[:half, :half], corner)
+    sides = jnp.concatenate([mixed, square[half:, :half]], axis=1)
+    folded = jnp.concatenate([sides[: half // 2], sides[half // 2 :]], axis=1)
+    diagonal = jnp.sum(jnp.where(row_at == col_at, corner, 0.0), axis=0, keepdims=True)
+    return folded, diagonal
+
+
+def unfold(folded, diagonal):
+    width = folded.shape[1] // 2
+    half = width // 2
+    row_at = lax.broadcasted_iota(jnp.int32, (half, half), 0)
+    col_at = lax.broadcasted_iota(jnp.int32, (half, half), 1)
+    sides = jnp.concatenate([folded[:, :width], folded[:, width:]], axis=0)
+    mixed, side = sides[:, :half], sides[:, half:]
+    turned = mixed.T
+    upper = jnp.where(row_at >= col_at, mixed, turned)
+    corner = jnp.where(row_at < col_at, mixed, turned)
+    corner = jnp.where(row_at == col_at, jnp.broadcast_to(diagonal, (half, half)), corner)
+    return jnp.concatenate(
+        [jnp.concatenate([upper, side.T], axis=1), jnp.concatenate([side, corner], axis=1)], axis=0
+    )
 
 
 def image_kernel(
@@ -144,15 +184,27 @@
                 preferred_element_type=jnp.float32,
             )
             total = term if total is None else total + term
-        return fold(total)
-
-    parts = [summed(image_ref)] + ([summed(tiles_ref)] if with_projection else [])
-    half = own_ref.shape[0] // len(parts)
-    for k, folded in enumerate(parts):
-        at = slice(k * half, (k + 1) * half)
-        low, high = folded[:half], folded[half:]
-        own_ref[at, :] = jnp.where(me % 2 == 0, low, high)
-        given_ref[at, :] = jnp.where(me % 2 == 0, high, low)
+        return total
+
+    squares = [summed(image_ref)]
+    if with_projection:
+        product = summed(tiles_ref)
+        squares.append((product + product.T) * 0.5)
+    diagonals = []
+    for k, square in enumerate(squares):
+        folded, diagonal = fold(square)
+        diagonals.append(diagonal)
+        low, high = folded[:ROWS], folded[ROWS:]
+        own, given = jnp.where(me % 2 == 0, low, high), jnp.where(me % 2 == 0, high, low)
+        for r in range(ROWS):
+            at = row_of(k * ROWS + r)
+            own_ref[:, at] = own[r : r + 1]
+            given_ref[:, at] = given[r : r + 1]
+    rest = own_ref.shape[1] // LANES - 1
+    missing = LANES - len(diagonals) * diagonals[0].shape[1]
+    last = jnp.concatenate(diagonals + [jnp.zeros((1, missing), jnp.float32)], axis=1)
+    own_ref[:, row_of(rest)] = last
+    given_ref[:, row_of(rest)] = last
 
 
 def inverse_factor(gram):
@@ -179,13 +231,16 @@
     return work[:, n:] * (1.0 / jnp.sqrt(pivots[:, n:]))
 
 
-def whole_sum(core, own_ref, other_ref, k, parts):
-    half = own_ref.shape[0] // parts
-    own = own_ref[k * half : (k + 1) * half, :]
-    other = other_ref[k * half : (k + 1) * half, :]
+def whole_sum(core, own_ref, other_ref, k):
+    at = [row_of(k * ROWS + r) for r in range(ROWS)]
+    own = jnp.concatenate([own_ref[:, a] for a in at], axis=0)
+    other = jnp.concatenate([other_ref[:, a] for a in at], axis=0)
+    rest = row_of(own_ref.shape[1] // LANES - 1)
+    diagonals = jnp.where(core == 0, own_ref[:, rest], other_ref[:, rest])
     first = jnp.where(core == 0, own, other)
     second = jnp.where(core == 0, other, own)
-    return unfold(jnp.concatenate([first, second], axis=0))
+    width = LANES // 4
+    return unfold(jnp.concatenate([first, second], axis=0), diagonals[:, k * width : (k + 1) * width])
 
 
 def normal_kernel(
@@ -194,31 +249,56 @@
 ):
     me, live = table_ref[ME], table_ref[LIVE]
     chunks = start_blocks(live, blocks_ref, held, sems)
-    inverse = inverse_factor(whole_sum(me % 2, own_ref, other_ref, 0, 1) / total_rows)
+    inverse = inverse_factor(whole_sum(me % 2, own_ref, other_ref, 0) / total_rows)
     for j in range(tiles_ref.shape[0]):
         tiles_ref[j] = jnp.dot(
             inverse, image_ref[j], precision=HIGHEST, preferred_element_type=jnp.float32
         ).astype(tiles_ref.dtype)
     multiply_mirrors(me, table_ref, live, chunks, tiles_ref, blocks_ref, held, sems, out_ref)
-    place_tiles(me, wanted_ref, tiles_ref, out_ref)
+    place_tiles(0, me, wanted_ref, tiles_ref, out_ref)
 
 
 def last_kernel(total_rows, table_ref, own_ref, other_ref, image_ref, result_ref, projected_ref):
     core = table_ref[ME] % 2
-    inverse = inverse_factor(whole_sum(core, own_ref, other_ref, 0, 2) / total_rows)
+    inverse = inverse_factor(whole_sum(core, own_ref, other_ref, 0) / total_rows)
     size = image_ref.shape[2]
     for j in range(image_ref.shape[0]):
         result_ref[:, j * size : (j + 1) * size] = jnp.dot(
             inverse, image_ref[j], precision=HIGHEST, preferred_element_type=jnp.float32
         )
-    projected_ref[...] = whole_sum(core, own_ref, other_ref, 1, 2) / total_rows
+    projected_ref[...] = whole_sum(core, own_ref, other_ref, 1) / total_rows
+
+
+def spread_kernel(own_ref, given_ref, out_ref):
+    chip = own_ref[...] + given_ref[...]
+    for i in range(out_ref.shape[0]):
+        out_ref[i] = chip
+
+
+def total_kernel(parts_ref, out_ref):
+    terms = [parts_ref[i] for i in range(parts_ref.shape[0])]
+    while len(terms) > 1:
+        terms = [a + b for a, b in zip(terms[::2], terms[1::2])] + terms[len(terms) // 2 * 2 :]
+    out_ref[...] = terms[0]
 
 
 def sum_over_devices(mine, given):
     swap = [(0, 1), (1, 0)]
-    mine = mine + lax.ppermute(given, "grp", swap)
-    spread = jnp.broadcast_to(mine[None], (lax.axis_size("rows"),) + mine.shape)
-    own = jnp.sum(lax.all_to_all(spread, "rows", 0, 0, tiled=True), axis=0)
+    chips = lax.axis_size("rows")
+    spread = pl.pallas_call(
+        spread_kernel,
+        out_shape=jax.ShapeDtypeStruct((chips,) + mine.shape, mine.dtype),
+        in_specs=[VMEM] * 2,
+        out_specs=VMEM,
+        name="spread",
+    )(mine, lax.ppermute(given, "grp", swap))
+    own = pl.pallas_call(
+        total_kernel,
+        out_shape=jax.ShapeDtypeStruct(mine.shape, mine.dtype),
+        in_specs=[VMEM],
+        out_specs=VMEM,
+        name="total",
+    )(lax.all_to_all(spread, "rows", 0, 0, tiled=True))
     return own, lax.ppermute(own, "grp", swap)
 
 
@@ -241,7 +321,7 @@
         out_specs=VMEM,
         name="ask",
     )(block_count, block_col[None, :])
-    wanted = exchange(asked)[:, 0, 0]
+    asked = exchange(asked)
     table = jnp.concatenate([me.reshape(1).astype(jnp.int32), block_count, block_row, block_col])
 
     params = pltpu.CompilerParams(vmem_limit_bytes=48 * MIB)
@@ -253,9 +333,9 @@
     image_shape = jax.ShapeDtypeStruct((row_blocks, columns, size), jnp.float32)
     out_shape = jax.ShapeDtypeStruct((devices, columns, size), jnp.bfloat16)
 
-    def image_of(tiles, arrived, with_projection):
+    def image_of(tiles, wanted, arrived, with_projection):
         parts = 2 if with_projection else 1
-        half = jax.ShapeDtypeStruct((parts * columns // 4, 2 * columns), jnp.float32)
+        half = jax.ShapeDtypeStruct((1, (parts * ROWS + 1) * LANES), jnp.float32)
         return pl.pallas_call(
             functools.partial(image_kernel, with_projection),
             out_shape=(image_shape, half, half),
@@ -275,15 +355,16 @@
         compiler_params=params,
         name="first",
     )(table, start_basis.T, kernel_blocks)
-    outgoing = pl.pallas_call(
+    outgoing, wanted = pl.pallas_call(
         place_kernel,
-        out_shape=out_shape,
-        in_specs=[SMEM] * 2 + [VMEM] * 2,
-        out_specs=VMEM,
+        out_shape=(out_shape, jax.ShapeDtypeStruct((devices,), jnp.int32)),
+        in_specs=[SMEM] * 2 + [VMEM, ANY],
+        out_specs=(VMEM, SMEM),
+        scratch_shapes=[pltpu.SemaphoreType.DMA((8,))],
         compiler_params=params,
         name="place",
-    )(table, wanted, tiles, outgoing)
-    image, own, given = image_of(tiles, exchange(outgoing), False)
+    )(table, asked, tiles, outgoing)
+    image, own, given = image_of(tiles, wanted, exchange(outgoing), False)
     own, other = sum_over_devices(own, given)
     outgoing, tiles = pl.pallas_call(
         functools.partial(normal_kernel, total_rows),
@@ -294,7 +375,7 @@
         compiler_params=params,
         name="normal",
     )(table, wanted, own, other, image, kernel_blocks)
-    image, own, given = image_of(tiles, exchange(outgoing), True)
+    image, own, given = image_of(tiles, wanted, exchange(outgoing), True)
     own, other = sum_over_devices(own, given)
     result, projected = pl.pallas_call(
         functools.partial(last_kernel, total_rows),

time: 222 us -> 228 us (1.027)
  Pallas kernels: 39.8 us -> 47.5 us
  blocking collectives: 154 us -> 150 us
    pallas_call x1 -> x5, Pallas kernels: 2.75 us -> 10.8 us  [the longest x1 4.46 us: on_device(): pl.pallas_call(place_kernel, out_shape=(out_shape, jax.ShapeDtypeStruct((...]
    all_to_all x2, blocking collectives: 39 us -> 34.3 us  [sum_over_devices(): lax.all_to_all(spread, 'rows', 0, 0, tiled=True)]
    unnamed x4 -> x16, local copies, waits for them, and re-layouts: 2.77 us -> 6.54 us
    slice x1 -> x0, local copies, waits for them, and re-layouts: 2.45 us -> none  [on_device(): wanted = exchange(asked)[:, 0, 0]]
where the time goes in v3:
time: 228 us; the launch traced here: 227 us
  blocking collectives  150 us (66%)
  Pallas kernels  47.5 us (21%)
  starting transfers between devices  17.1 us (8%)
  local copies, waits for them, and re-layouts  6.54 us (3%)
  waiting for transfers between devices  3.73 us (2%)
    all_to_all x2, blocking collectives, exchange(): lax.all_to_all(outgoing, AXES, split_axis=0, concat_axis=0, tiled=True)  116 us
    all_to_all x2, blocking collectives, sum_over_devices(): lax.all_to_all(spread, 'rows', 0, 0, tiled=True)  34.3 us
    pallas_call x2, Pallas kernels, image_of(): pl.pallas_call(functools.partial(image_kernel, with_projection), out_shap...  17.6 us
    all_to_all x1, starting transfers between devices, exchange(): lax.all_to_all(outgoing, AXES, split_axis=0, concat_axis=0, tiled=True)  11.5 us
    pallas_call x1, Pallas kernels, on_device(): pl.pallas_call(functools.partial(normal_kernel, total_rows), out_shape=(o...  7.75 us
    unnamed x16, local copies, waits for them, and re-layouts  6.54 us
    pallas_call x1, Pallas kernels, on_device(): pl.pallas_call(first_kernel, out_shape=(out_shape, tiles_shape), in_specs...  6.53 us
  transfers between devices with their start and end apart: 5, of which 4 were waited for; matrix products, arithmetic and copies ran while one was open for 0% of the time, Pallas kernels for 3%

profile of v3, /device:TPU:1, one launch (start us, length us, event | category | flops | bytes accessed | tf_op | source)
XLA Modules:
  0.0 227.1 jit_solution(16670428006811054102)
XLA Ops:
  1.3 1.5 ask.1
  2.8 11.5 %all-to-all-start = ((s32[128,1,128]{2,1,0:T(1,128)}), s32[128,1,128]{2,1,0:T(1,128)S(1)}, u32[]{:S(2)}, u32[]{:S(2)}) async-start(s32[128,1,128]{2,1,0:T(1,128)} %ask.1), calls=%async_computation | async-start | bytes 131072 | tf_op jit(solution)/shard_map/all_to_all | solution.py:306
  14.3 0.8 pad_add_fusion.table_ref
  15.0 0.0 copy-start.1
  15.0 0.8 copy-done.1
  15.9 6.5 %first.1 = (bf16[128,64,256]{2,1,0:T(8,128)(2,1)S(1)}, bf16[2,64,256]{2,1,0:T(8,128)(2,1)S(1)}) custom-call(s32[186]{0:T(256)S(1)} %pad_add_fusion.table_ref, bf16[64,512]{1,0:T(8,128)(2,1)S(1)} %bitcast.4, bf16[92,256,256]{2,1,0:T(8,128)(2,1)} %blocks_ref.7), custom_call_target="tpu_custom_call" | custom-call | tf_op jit(solution)/shard_map/first/pallas_call | solution.py:349
  22.4 0.0 copy-start
  22.4 1.9 copy-done
  24.4 0.0 all-to-all-done.asked_ref
  24.4 4.5 %place.1 = (bf16[128,64,256]{2,1,0:T(8,128)(2,1)S(1)}, s32[128]{0:T(128)S(1)}) custom-call(s32[186]{0:T(256)S(1)} %pad_add_fusion.table_ref, s32[128,1,128]{2,1,0:T(1,128)S(1)} %all-to-all-done.asked_ref, bf16[2,64,256]{2,1,0:T(8,128)(2,1)S(1)} %get-tuple-element.16.tiles_ref, bf16[128,64,256]{2,1,0:T(8,128)(2,1)} %copy-done), custom_call_target="tpu_custom_call" | custom-call | tf_op jit(solution)/shard_map/place/pallas_call | solution.py:358
  28.8 59.4 %all_to_all.25.arrived_ref = bf16[128,64,256]{2,1,0:T(8,128)(2,1)S(1)} all-to-all(bf16[128,64,256]{2,1,0:T(8,128)(2,1)S(1)} %get-tuple-element.19), channel_id=1, replica_groups=mesh['rows'=64,'grp'=2] {'rows','grp'}, dimensions={0} | all-to-all | bytes 8388608 | tf_op jit(solution)/shard_map/all_to_all | solution.py:306
  88.3 8.7 %image.2 = (f32[2,64,256]{2,1,0:T(8,128)S(1)}, f32[1,1152]{1,0:T(1,128)S(1)}, f32[1,1152]{1,0:T(1,128)S(1)}) custom-call(s32[186]{0:T(256)S(1)} %pad_add_fusion.table_ref, s32[128]{0:T(128)S(1)} %get-tuple-element.18.wanted_ref, bf16[2,64,256]{2,1,0:T(8,128)(2,1)S(1)} %get-tuple-element.16.tiles_ref, bf16[128,64,256]{2,1,0:T(8,128)(2,1)S(1)} %all_to_all.25.arrived_ref, ...), custom_call_target="tpu_custom_call" | custom-call | tf_op jit(solution)/shard_map/image/pallas_call | solution.py:339
  97.0 0.0 copy-start.5
  97.0 0.6 copy-done.5
  97.6 1.2 collective-permute-start
  98.8 0.8 collective-permute-done.given_ref
  99.6 0.0 copy-start.7
  99.6 0.6 copy-done.7
  100.2 1.4 spread.2
  101.7 15.7 %all_to_all.26.parts_ref = f32[64,1,1152]{2,1,0:T(1,128)} all-to-all(f32[64,1,1152]{2,1,0:T(1,128)} %spread.2), channel_id=1, replica_groups=mesh['rows'=64,'grp'=2] {'rows'}, dimensions={0} | all-to-all | bytes 589824 | tf_op jit(solution)/shard_map/all_to_all | solution.py:301
  117.4 1.6 total.2.own_ref
  119.0 1.5 collective-permute-start.1
  120.5 1.0 collective-permute-done.1.other_ref
  121.6 0.0 copy-start.3
  121.6 0.7 copy-done.3
  122.3 7.8 %normal.1 = (bf16[128,64,256]{2,1,0:T(8,128)(2,1)S(1)}, bf16[2,64,256]{2,1,0:T(8,128)(2,1)S(1)}) custom-call(s32[186]{0:T(256)S(1)} %pad_add_fusion.table_ref, s32[128]{0:T(128)S(1)} %get-tuple-element.18.wanted_ref, f32[1,1152]{1,0:T(1,128)S(1)} %copy-done.3, f32[1,1152]{1,0:T(1,128)S(1)} %collective-permute-done.1.other_ref, ...), custom_call_target="tpu_custom_call" | custom-call | tf_op jit(solution)/shard_map/normal/pallas_call | solution.py:369
  130.0 56.5 %all_to_all.27.arrived_ref = bf16[128,64,256]{2,1,0:T(8,128)(2,1)S(1)} all-to-all(bf16[128,64,256]{2,1,0:T(8,128)(2,1)S(1)} %get-tuple-element.24), channel_id=1, replica_groups=mesh['rows'=64,'grp'=2] {'rows','grp'}, dimensions={0} | all-to-all | bytes 8388608 | tf_op jit(solution)/shard_map/all_to_all | solution.py:306
  186.5 8.9 %image.3 = (f32[2,64,256]{2,1,0:T(8,128)S(1)}, f32[1,2176]{1,0:T(1,128)S(1)}, f32[1,2176]{1,0:T(1,128)S(1)}) custom-call(s32[186]{0:T(256)S(1)} %pad_add_fusion.table_ref, s32[128]{0:T(128)S(1)} %get-tuple-element.18.wanted_ref, bf16[2,64,256]{2,1,0:T(8,128)(2,1)S(1)} %get-tuple-element.23.tiles_ref, bf16[128,64,256]{2,1,0:T(8,128)(2,1)S(1)} %all_to_all.27.arrived_ref, ...), custom_call_target="tpu_custom_call" | custom-call | tf_op jit(solution)/shard_map/image/pallas_call | solution.py:339
  195.4 0.0 copy-start.4
  195.4 0.6 copy-done.4
  196.0 1.2 collective-permute-start.2
  197.2 0.8 collective-permute-done.2.given_ref
  198.0 0.0 copy-start.6
  198.0 0.6 copy-done.6
  198.6 1.6 spread.3
  200.2 18.6 %all_to_all.28.parts_ref = f32[64,1,2176]{2,1,0:T(1,128)} all-to-all(f32[64,1,2176]{2,1,0:T(1,128)} %spread.3), channel_id=1, replica_groups=mesh['rows'=64,'grp'=2] {'rows'}, dimensions={0} | all-to-all | bytes 1114112 | tf_op jit(solution)/shard_map/all_to_all | solution.py:301
  218.8 1.7 total.3.own_ref
  220.5 1.6 collective-permute-start.3
  222.1 1.0 collective-permute-done.3.other_ref
  223.1 0.0 copy-start.2
  223.1 0.7 copy-done.2
  223.8 3.4 %last.1 = (f32[64,512]{1,0:T(8,128)}, f32[64,64]{1,0:T(8,128)}) custom-call(s32[186]{0:T(256)S(1)} %pad_add_fusion.table_ref, f32[1,2176]{1,0:T(1,128)S(1)} %copy-done.2, f32[1,2176]{1,0:T(1,128)S(1)} %collective-permute-done.3.other_ref, f32[2,64,256]{2,1,0:T(8,128)S(1)} %get-tuple-element.27.image_ref), custom_call_target="tpu_custom_call" | custom-call | tf_op jit(solution)/shard_map/last/pallas_call | solution.py:380
Async XLA Ops:
  2.8 21.6 %all-to-all-start = ((s32[128,1,128]{2,1,0:T(1,128)}), s32[128,1,128]{2,1,0:T(1,128)S(1)}, u32[]{:S(2)}, u32[]{:S(2)}) async-start(s32[128,1,128]{2,1,0:T(1,128)} %ask.1), calls=%async_computation | async-start | bytes 131072 | tf_op jit(solution)/shard_map/all_to_all | solution.py:306
  15.0 0.8 copy-start.1
  22.4 2.0 copy-start
  97.0 0.6 copy-start.5
  97.6 2.0 collective-permute-start
  99.6 0.6 copy-start.7
  119.0 2.6 %collective-permute-start.1 = (f32[1,1152]{1,0:T(1,128)}, f32[1,1152]{1,0:T(1,128)S(1)}, u32[]{:S(2)}, u32[]{:S(2)}) collective-permute-start(f32[1,1152]{1,0:T(1,128)} %total.2.own_ref), channel_id=1, source_target_pairs={{0,1},{1,0},{2,3},{3,2},{4,5},{5,4},{6,7},{7,6},{8,9},{9,8},{10,11... | collective-permute-start | bytes 13832 | tf_op jit(solution)/shard_map/ppermute | solution.py:302
  121.6 0.7 copy-start.3
  195.4 0.6 copy-start.4
  196.0 2.1 collective-permute-start.2
  198.0 0.6 copy-start.6
  220.5 2.6 %collective-permute-start.3 = (f32[1,2176]{1,0:T(1,128)}, f32[1,2176]{1,0:T(1,128)S(1)}, u32[]{:S(2)}, u32[]{:S(2)}) collective-permute-start(f32[1,2176]{1,0:T(1,128)} %total.3.own_ref), channel_id=1, source_target_pairs={{0,1},{1,0},{2,3},{3,2},{4,5},{5,4},{6,7},{7,6},{8,9},{9,8},{10,11... | collective-permute-start | bytes 26120 | tf_op jit(solution)/shard_map/ppermute | solution.py:302
  223.1 0.7 copy-start.2

commit v4 on v3

--- a/solution.py
+++ b/solution.py
@@ -18,6 +18,7 @@
 SMEM = pl.BlockSpec(memory_space=pltpu.SMEM)
 ANY = pl.BlockSpec(memory_space=pl.ANY)
 MIB = 1024 * 1024
+SMALL = pltpu.CompilerParams(vmem_limit_bytes=8 * MIB)
 
 
 def block_copy(blocks_ref, held, sems, i):
@@ -290,6 +291,7 @@
         out_shape=jax.ShapeDtypeStruct((chips,) + mine.shape, mine.dtype),
         in_specs=[VMEM] * 2,
         out_specs=VMEM,
+        compiler_params=SMALL,
         name="spread",
     )(mine, lax.ppermute(given, "grp", swap))
     own = pl.pallas_call(
@@ -297,6 +299,7 @@
         out_shape=jax.ShapeDtypeStruct(mine.shape, mine.dtype),
         in_specs=[VMEM],
         out_specs=VMEM,
+        compiler_params=SMALL,
         name="total",
     )(lax.all_to_all(spread, "rows", 0, 0, tiled=True))
     return own, lax.ppermute(own, "grp", swap)
@@ -319,6 +322,7 @@
         out_shape=jax.ShapeDtypeStruct((devices, 1, 128), jnp.int32),
         in_specs=[SMEM, VMEM],
         out_specs=VMEM,
+        compiler_params=SMALL,
         name="ask",
     )(block_count, block_col[None, :])
     asked = exchange(asked)

time: 228 us -> 214 us (0.939)
  Pallas kernels: 47.5 us -> 39.7 us
  local copies, waits for them, and re-layouts: 6.54 us -> 3.43 us
    pallas_call x2, Pallas kernels: 3.27 us -> 0.07 us  [sum_over_devices(): pl.pallas_call(total_kernel, out_shape=jax.ShapeDtypeStruct(mine.shape, m...]
    all_to_all x2, blocking collectives: 34.3 us -> 31.2 us  [sum_over_devices(): lax.all_to_all(spread, 'rows', 0, 0, tiled=True)]
    unnamed x16 -> x6, local copies, waits for them, and re-layouts: 6.54 us -> 3.43 us
    pallas_call x2, Pallas kernels: 3.03 us -> 0.09 us  [sum_over_devices(): pl.pallas_call(spread_kernel, out_shape=jax.ShapeDtypeStruct((chips,) + m...]
where the time goes in v4:
time: 214 us
  blocking collectives  148 us (69%)
  Pallas kernels  39.7 us (19%)
  starting transfers between devices  18 us (8%)
  local copies, waits for them, and re-layouts  3.43 us (2%)
  waiting for transfers between devices  3.31 us (2%)
    all_to_all x2, blocking collectives, exchange(): lax.all_to_all(outgoing, AXES, split_axis=0, concat_axis=0, tiled=True)  116 us
    all_to_all x2, blocking collectives, sum_over_devices(): lax.all_to_all(spread, 'rows', 0, 0, tiled=True)  31.2 us
    pallas_call x2, Pallas kernels, image_of(): pl.pallas_call(functools.partial(image_kernel, with_projection), out_shap...  17 us
    all_to_all x1, starting transfers between devices, exchange(): lax.all_to_all(outgoing, AXES, split_axis=0, concat_axis=0, tiled=True)  11.5 us
    pallas_call x1, Pallas kernels, on_device(): pl.pallas_call(functools.partial(normal_kernel, total_rows), out_shape=(o...  7.53 us
    pallas_call x1, Pallas kernels, on_device(): pl.pallas_call(first_kernel, out_shape=(out_shape, tiles_shape), in_specs...  6.31 us
    pallas_call x1, Pallas kernels, on_device(): pl.pallas_call(place_kernel, out_shape=(out_shape, jax.ShapeDtypeStruct((...  4.46 us
  transfers between devices with their start and end apart: 5, of which 4 were waited for; matrix products, arithmetic and copies ran while one was open for 0% of the time, Pallas kernels for 3%

profile of v4, /device:TPU:1, one launch (start us, length us, event | category | flops | bytes accessed | tf_op | source)
XLA Modules:
  0.0 214.0 jit_solution(10526008303774793013)
XLA Ops:
  1.3 0.0 copy-start.2
  1.3 0.6 copy-done.2
  1.9 0.8 ask.1
  2.8 11.5 %all-to-all-start = ((s32[128,1,128]{2,1,0:T(1,128)}), s32[128,1,128]{2,1,0:T(1,128)S(1)}, u32[]{:S(2)}, u32[]{:S(2)}) async-start(s32[128,1,128]{2,1,0:T(1,128)} %ask.1), calls=%async_computation | async-start | bytes 131072 | tf_op jit(solution)/shard_map/all_to_all | solution.py:309
  14.3 0.8 pad_add_fusion.table_ref
  15.0 0.0 copy-start.1
  15.0 0.8 copy-done.1
  15.9 6.3 %first.1 = (bf16[128,64,256]{2,1,0:T(8,128)(2,1)S(1)}, bf16[2,64,256]{2,1,0:T(8,128)(2,1)S(1)}) custom-call(s32[186]{0:T(256)S(1)} %pad_add_fusion.table_ref, bf16[64,512]{1,0:T(8,128)(2,1)S(1)} %bitcast.4, bf16[92,256,256]{2,1,0:T(8,128)(2,1)} %blocks_ref.7), custom_call_target="tpu_custom_call" | custom-call | tf_op jit(solution)/shard_map/first/pallas_call | solution.py:353
  22.2 0.0 copy-start
  22.2 1.9 copy-done
  24.1 0.0 all-to-all-done.asked_ref
  24.2 4.5 %place.1 = (bf16[128,64,256]{2,1,0:T(8,128)(2,1)S(1)}, s32[128]{0:T(128)S(1)}) custom-call(s32[186]{0:T(256)S(1)} %pad_add_fusion.table_ref, s32[128,1,128]{2,1,0:T(1,128)S(1)} %all-to-all-done.asked_ref, bf16[2,64,256]{2,1,0:T(8,128)(2,1)S(1)} %get-tuple-element.16.tiles_ref, bf16[128,64,256]{2,1,0:T(8,128)(2,1)} %copy-done), custom_call_target="tpu_custom_call" | custom-call | tf_op jit(solution)/shard_map/place/pallas_call | solution.py:362
  28.6 59.6 %all_to_all.25.arrived_ref = bf16[128,64,256]{2,1,0:T(8,128)(2,1)S(1)} all-to-all(bf16[128,64,256]{2,1,0:T(8,128)(2,1)S(1)} %get-tuple-element.19), channel_id=1, replica_groups=mesh['rows'=64,'grp'=2] {'rows','grp'}, dimensions={0} | all-to-all | bytes 8388608 | tf_op jit(solution)/shard_map/all_to_all | solution.py:309
  88.3 8.4 %image.2 = (f32[2,64,256]{2,1,0:T(8,128)S(1)}, f32[1,1152]{1,0:T(1,128)S(1)}, f32[1,1152]{1,0:T(1,128)S(1)}) custom-call(s32[186]{0:T(256)S(1)} %pad_add_fusion.table_ref, s32[128]{0:T(128)S(1)} %get-tuple-element.18.wanted_ref, bf16[2,64,256]{2,1,0:T(8,128)(2,1)S(1)} %get-tuple-element.16.tiles_ref, bf16[128,64,256]{2,1,0:T(8,128)(2,1)S(1)} %all_to_all.25.arrived_ref, ...), custom_call_target="tpu_custom_call" | custom-call | tf_op jit(solution)/shard_map/image/pallas_call | solution.py:343
  96.7 1.6 collective-permute-start
  98.3 0.8 collective-permute-done.given_ref
  99.2 14.2 %all_to_all.26.parts_ref = f32[64,1,1152]{2,1,0:T(1,128)S(1)} all-to-all(f32[64,1,1152]{2,1,0:T(1,128)S(1)} %spread.2), channel_id=1, replica_groups=mesh['rows'=64,'grp'=2] {'rows'}, dimensions={0} | all-to-all | bytes 589824 | tf_op jit(solution)/shard_map/all_to_all | solution.py:304
  113.4 1.6 collective-permute-start.1
  115.0 0.8 collective-permute-done.1.other_ref
  115.8 7.5 %normal.1 = (bf16[128,64,256]{2,1,0:T(8,128)(2,1)S(1)}, bf16[2,64,256]{2,1,0:T(8,128)(2,1)S(1)}) custom-call(s32[186]{0:T(256)S(1)} %pad_add_fusion.table_ref, s32[128]{0:T(128)S(1)} %get-tuple-element.18.wanted_ref, f32[1,1152]{1,0:T(1,128)S(1)} %total.2.own_ref, f32[1,1152]{1,0:T(1,128)S(1)} %collective-permute-done.1.other_ref, ...), custom_call_target="tpu_custom_call" | custom-call | tf_op jit(solution)/shard_map/normal/pallas_call | solution.py:373
  123.3 56.7 %all_to_all.27.arrived_ref = bf16[128,64,256]{2,1,0:T(8,128)(2,1)S(1)} all-to-all(bf16[128,64,256]{2,1,0:T(8,128)(2,1)S(1)} %get-tuple-element.24), channel_id=1, replica_groups=mesh['rows'=64,'grp'=2] {'rows','grp'}, dimensions={0} | all-to-all | bytes 8388608 | tf_op jit(solution)/shard_map/all_to_all | solution.py:309
  180.0 8.6 %image.3 = (f32[2,64,256]{2,1,0:T(8,128)S(1)}, f32[1,2176]{1,0:T(1,128)S(1)}, f32[1,2176]{1,0:T(1,128)S(1)}) custom-call(s32[186]{0:T(256)S(1)} %pad_add_fusion.table_ref, s32[128]{0:T(128)S(1)} %get-tuple-element.18.wanted_ref, bf16[2,64,256]{2,1,0:T(8,128)(2,1)S(1)} %get-tuple-element.23.tiles_ref, bf16[128,64,256]{2,1,0:T(8,128)(2,1)S(1)} %all_to_all.27.arrived_ref, ...), custom_call_target="tpu_custom_call" | custom-call | tf_op jit(solution)/shard_map/image/pallas_call | solution.py:343
  188.6 1.6 collective-permute-start.2
  190.2 0.8 collective-permute-done.2.given_ref
  191.1 0.1 spread.3
  191.1 17.0 %all_to_all.28.parts_ref = f32[64,1,2176]{2,1,0:T(1,128)S(1)} all-to-all(f32[64,1,2176]{2,1,0:T(1,128)S(1)} %spread.3), channel_id=1, replica_groups=mesh['rows'=64,'grp'=2] {'rows'}, dimensions={0} | all-to-all | bytes 1114112 | tf_op jit(solution)/shard_map/all_to_all | solution.py:304
  208.2 1.7 collective-permute-start.3
  209.8 0.8 collective-permute-done.3.other_ref
  210.6 3.4 %last.1 = (f32[64,512]{1,0:T(8,128)}, f32[64,64]{1,0:T(8,128)}) custom-call(s32[186]{0:T(256)S(1)} %pad_add_fusion.table_ref, f32[1,2176]{1,0:T(1,128)S(1)} %total.3.own_ref, f32[1,2176]{1,0:T(1,128)S(1)} %collective-permute-done.3.other_ref, f32[2,64,256]{2,1,0:T(8,128)S(1)} %get-tuple-element.27.image_ref), custom_call_target="tpu_custom_call" | custom-call | tf_op jit(solution)/shard_map/last/pallas_call | solution.py:384
  (3 shorter events, 0.1 us)
Async XLA Ops:
  1.3 0.7 copy-start.2
  2.8 21.4 %all-to-all-start = ((s32[128,1,128]{2,1,0:T(1,128)}), s32[128,1,128]{2,1,0:T(1,128)S(1)}, u32[]{:S(2)}, u32[]{:S(2)}) async-start(s32[128,1,128]{2,1,0:T(1,128)} %ask.1), calls=%async_computation | async-start | bytes 131072 | tf_op jit(solution)/shard_map/all_to_all | solution.py:309
  15.0 0.8 copy-start.1
  22.2 1.9 copy-start
  96.7 2.4 %collective-permute-start = (f32[1,1152]{1,0:T(1,128)S(1)}, f32[1,1152]{1,0:T(1,128)S(1)}, u32[]{:S(2)}, u32[]{:S(2)}) collective-permute-start(f32[1,1152]{1,0:T(1,128)S(1)} %get-tuple-element.21), channel_id=1, source_target_pairs={{0,1},{1,0},{2,3},{3,2},{4,5},{5,4},{6,7},{7,6},{8,9},{9,8},{10,11... | collective-permute-start | bytes 13832 | tf_op jit(solution)/shard_map/ppermute | solution.py:296
  113.4 2.4 %collective-permute-start.1 = (f32[1,1152]{1,0:T(1,128)S(1)}, f32[1,1152]{1,0:T(1,128)S(1)}, u32[]{:S(2)}, u32[]{:S(2)}) collective-permute-start(f32[1,1152]{1,0:T(1,128)S(1)} %total.2.own_ref), channel_id=1, source_target_pairs={{0,1},{1,0},{2,3},{3,2},{4,5},{5,4},{6,7},{7,6},{8,9},{9,8},{10,11... | collective-permute-start | bytes 13832 | tf_op jit(solution)/shard_map/ppermute | solution.py:305
  188.6 2.4 %collective-permute-start.2 = (f32[1,2176]{1,0:T(1,128)S(1)}, f32[1,2176]{1,0:T(1,128)S(1)}, u32[]{:S(2)}, u32[]{:S(2)}) collective-permute-start(f32[1,2176]{1,0:T(1,128)S(1)} %get-tuple-element.26), channel_id=1, source_target_pairs={{0,1},{1,0},{2,3},{3,2},{4,5},{5,4},{6,7},{7,6},{8,9},{9,8},{10,11... | collective-permute-start | bytes 26120 | tf_op jit(solution)/shard_map/ppermute | solution.py:296
  208.2 2.5 %collective-permute-start.3 = (f32[1,2176]{1,0:T(1,128)S(1)}, f32[1,2176]{1,0:T(1,128)S(1)}, u32[]{:S(2)}, u32[]{:S(2)}) collective-permute-start(f32[1,2176]{1,0:T(1,128)S(1)} %total.3.own_ref), channel_id=1, source_target_pairs={{0,1},{1,0},{2,3},{3,2},{4,5},{5,4},{6,7},{7,6},{8,9},{9,8},{10,11... | collective-permute-start | bytes 26120 | tf_op jit(solution)/shard_map/ppermute | solution.py:305

commit v5 on v4

--- a/solution.py
+++ b/solution.py
@@ -9,7 +9,7 @@
 
 AXES = ("rows", "grp")
 HIGHEST = lax.Precision.HIGHEST
-CHUNK = 4
+CHUNK = 23
 PANEL = 8
 ROWS, LANES = 8, 128
 ME, LIVE, FIRST = 0, 1, 2
@@ -54,13 +54,24 @@
 
 
 def place_tiles(start, end, wanted_ref, tiles_ref, out_ref):
+    tiles = [tiles_ref[j].astype(jnp.float32) for j in range(tiles_ref.shape[0])]
+    group = 4
+
     def visit(i, carry):
-        for j in range(CHUNK):
-            d = jnp.minimum(start + i * CHUNK + j, end - 1)
-            out_ref[d] = tiles_ref[jnp.maximum(wanted_ref[d], 0)]
-        return carry
-
-    lax.fori_loop(0, (end - start + CHUNK - 1) // CHUNK, visit, 0)
+        for j in range(group):
+            d = jnp.minimum(start + i * group + j, end - 1)
+            wanted = spread_lanes(wanted_ref[d], tiles[0].shape[1])
+            tile = tiles[0]
+            for k in range(1, len(tiles)):
+                tile = jnp.where(wanted == k, tiles[k], tile)
+            out_ref[d] = tile.astype(out_ref.dtype)
+        return carry
+
+    lax.fori_loop(0, (end - start + group - 1) // group, visit, 0)
+
+
+def spread_lanes(row, width):
+    return jnp.concatenate([row] * (width // row.shape[1]), axis=1)
 
 
 def ask_kernel(row_blocks, count_ref, col_ref, out_ref):
@@ -83,7 +94,7 @@
     multiply_mirrors(table_ref[ME], table_ref, live, chunks, tiles_ref, blocks_ref, held, sems, out_ref)
 
 
-def place_kernel(table_ref, asked_ref, tiles_ref, given_ref, out_ref, wanted_ref, sems):
+def place_kernel(table_ref, wanted_ref, tiles_ref, given_ref, out_ref, sems):
     me = table_ref[ME]
     groups = sems.shape[0]
     size = out_ref.shape[0] // groups
@@ -101,13 +112,7 @@
         copy_of(g).wait()
         return carry
 
-    def compact(i, carry):
-        for j in range(CHUNK):
-            wanted_ref[i * CHUNK + j] = asked_ref[i * CHUNK + j, 0, 0]
-        return carry
-
     lax.fori_loop(first, groups, start, 0)
-    lax.fori_loop(0, wanted_ref.shape[0] // CHUNK, compact, 0)
     place_tiles(0, first * size, wanted_ref, tiles_ref, out_ref)
     lax.fori_loop(first, groups, wait, 0)
     place_tiles(first * size, me, wanted_ref, tiles_ref, out_ref)
@@ -152,16 +157,16 @@
     me, live = table_ref[ME], table_ref[LIVE]
     chunks = start_blocks(live, blocks_ref, held, sems)
     row_blocks = tiles_ref.shape[0]
-    image_ref[...] = jnp.zeros_like(image_ref)
-
-    def add_mirror(d, carry):
-        @pl.when(wanted_ref[d] >= 0)
-        def _():
-            image_ref[wanted_ref[d]] += arrived_ref[d].astype(jnp.float32)
-
-        return carry
-
-    lax.fori_loop(0, me + 1, add_mirror, 0)
+
+    def add_mirror(d, sums):
+        wanted = spread_lanes(wanted_ref[d], image_ref.shape[2])
+        mirror = arrived_ref[d].astype(jnp.float32)
+        return tuple(total + jnp.where(wanted == k, mirror, 0.0) for k, total in enumerate(sums))
+
+    zero = jnp.zeros(image_ref.shape[1:], image_ref.dtype)
+    sums = lax.fori_loop(0, me + 1, add_mirror, (zero,) * row_blocks)
+    for k, total in enumerate(sums):
+        image_ref[k] = total
 
     def visit(i, carry):
         block_copy(blocks_ref, held, sems, i).wait()
@@ -325,7 +330,7 @@
         compiler_params=SMALL,
         name="ask",
     )(block_count, block_col[None, :])
-    asked = exchange(asked)
+    wanted = exchange(asked)
     table = jnp.concatenate([me.reshape(1).astype(jnp.int32), block_count, block_row, block_col])
 
     params = pltpu.CompilerParams(vmem_limit_bytes=48 * MIB)
@@ -337,13 +342,13 @@
     image_shape = jax.ShapeDtypeStruct((row_blocks, columns, size), jnp.float32)
     out_shape = jax.ShapeDtypeStruct((devices, columns, size), jnp.bfloat16)
 
-    def image_of(tiles, wanted, arrived, with_projection):
+    def image_of(tiles, arrived, with_projection):
         parts = 2 if with_projection else 1
         half = jax.ShapeDtypeStruct((1, (parts * ROWS + 1) * LANES), jnp.float32)
         return pl.pallas_call(
             functools.partial(image_kernel, with_projection),
             out_shape=(image_shape, half, half),
-            in_specs=[SMEM] * 2 + [VMEM] * 2 + [ANY],
+            in_specs=[SMEM] + [VMEM] * 3 + [ANY],
             out_specs=(VMEM, VMEM, VMEM),
             scratch_shapes=scratch,
             compiler_params=params,
@@ -359,27 +364,27 @@
         compiler_params=params,
         name="first",
     )(table, start_basis.T, kernel_blocks)
-    outgoing, wanted = pl.pallas_call(
+    outgoing = pl.pallas_call(
         place_kernel,
-        out_shape=(out_shape, jax.ShapeDtypeStruct((devices,), jnp.int32)),
-        in_specs=[SMEM] * 2 + [VMEM, ANY],
-        out_specs=(VMEM, SMEM),
+        out_shape=out_shape,
+        in_specs=[SMEM] + [VMEM] * 2 + [ANY],
+        out_specs=VMEM,
         scratch_shapes=[pltpu.SemaphoreType.DMA((8,))],
         compiler_params=params,
         name="place",
-    )(table, asked, tiles, outgoing)
-    image, own, given = image_of(tiles, wanted, exchange(outgoing), False)
+    )(table, wanted, tiles, outgoing)
+    image, own, given = image_of(tiles, exchange(outgoing), False)
     own, other = sum_over_devices(own, given)
     outgoing, tiles = pl.pallas_call(
         functools.partial(normal_kernel, total_rows),
         out_shape=(out_shape, tiles_shape),
-        in_specs=[SMEM] * 2 + [VMEM] * 3 + [ANY],
+        in_specs=[SMEM] + [VMEM] * 4 + [ANY],
         out_specs=(VMEM, VMEM),
         scratch_shapes=scratch,
         compiler_params=params,
         name="normal",
     )(table, wanted, own, other, image, kernel_blocks)
-    image, own, given = image_of(tiles, wanted, exchange(outgoing), True)
+    image, own, given = image_of(tiles, exchange(outgoing), True)
     own, other = sum_over_devices(own, given)
     result, projected = pl.pallas_call(
         functools.partial(last_kernel, total_rows),

time: 214 us -> 207 us (0.967)
  Pallas kernels: 39.7 us -> 33.2 us
    pallas_call x2, Pallas kernels: 17 us -> 14.4 us  [image_of(): pl.pallas_call(functools.partial(image_kernel, with_projection), out_shap...]
  transfers between devices with their start and end apart: 5 -> 5, of which waited for: 4 -> 5; matrix products, arithmetic and copies ran while one was open for 0% -> 0% of each run, Pallas kernels for 3% -> 3%
where the time goes in v5:
time: 207 us; the launch traced here: 206 us
  blocking collectives  147 us (71%)
  Pallas kernels  33.2 us (16%)
  starting transfers between devices  16.9 us (8%)
  local copies, waits for them, and re-layouts  3.43 us (2%)
  waiting for transfers between devices  3.41 us (2%)
    all_to_all x2, blocking collectives, exchange(): lax.all_to_all(outgoing, AXES, split_axis=0, concat_axis=0, tiled=True)  116 us
    all_to_all x2, blocking collectives, sum_over_devices(): lax.all_to_all(spread, 'rows', 0, 0, tiled=True)  31 us
    pallas_call x2, Pallas kernels, image_of(): pl.pallas_call(functools.partial(image_kernel, with_projection), out_shap...  14.4 us
    all_to_all x1, starting transfers between devices, exchange(): lax.all_to_all(outgoing, AXES, split_axis=0, concat_axis=0, tiled=True)  11.5 us
    pallas_call x1, Pallas kernels, on_device(): pl.pallas_call(functools.partial(normal_kernel, total_rows), out_shape=(o...  5.82 us
    pallas_call x1, Pallas kernels, on_device(): pl.pallas_call(first_kernel, out_shape=(out_shape, tiles_shape), in_specs...  5.76 us
  transfers between devices with their start and end apart: 5, of which 5 were waited for; matrix products, arithmetic and copies ran while one was open for 0% of the time, Pallas kernels for 3%

profile of v5, /device:TPU:1, one launch (start us, length us, event | category | flops | bytes accessed | tf_op | source)
XLA Modules:
  0.0 206.1 jit_solution(14662951209692072388)
XLA Ops:
  1.3 0.0 copy-start.2
  1.3 0.6 copy-done.2
  1.9 0.8 ask.1
  2.8 11.5 %all-to-all-start = ((s32[128,1,128]{2,1,0:T(1,128)}), s32[128,1,128]{2,1,0:T(1,128)S(1)}, u32[]{:S(2)}, u32[]{:S(2)}) async-start(s32[128,1,128]{2,1,0:T(1,128)} %ask.1), calls=%async_computation | async-start | bytes 131072 | tf_op jit(solution)/shard_map/all_to_all | solution.py:314
  14.3 0.8 pad_add_fusion.table_ref
  15.0 0.0 copy-start.1
  15.0 0.8 copy-done.1
  15.9 5.8 %first.1 = (bf16[128,64,256]{2,1,0:T(8,128)(2,1)S(1)}, bf16[2,64,256]{2,1,0:T(8,128)(2,1)S(1)}) custom-call(s32[186]{0:T(256)S(1)} %pad_add_fusion.table_ref, bf16[64,512]{1,0:T(8,128)(2,1)S(1)} %bitcast.4, bf16[92,256,256]{2,1,0:T(8,128)(2,1)} %blocks_ref.7), custom_call_target="tpu_custom_call" | custom-call | tf_op jit(solution)/shard_map/first/pallas_call | solution.py:358
  21.6 0.0 copy-start
  21.7 1.9 copy-done
  23.6 0.1 all-to-all-done.wanted_ref
  23.7 2.8 %place.1 = bf16[128,64,256]{2,1,0:T(8,128)(2,1)S(1)} custom-call(s32[186]{0:T(256)S(1)} %pad_add_fusion.table_ref, s32[128,1,128]{2,1,0:T(1,128)S(1)} %all-to-all-done.wanted_ref, bf16[2,64,256]{2,1,0:T(8,128)(2,1)S(1)} %get-tuple-element.14.tiles_ref, bf16[128,64,256]{2,1,0:T(8,128)(2,1)} %copy-done), custom_call_target="tpu_custom_call" | custom-call | tf_op jit(solution)/shard_map/place/pallas_call | solution.py:367
  26.5 59.8 %all_to_all.25.arrived_ref = bf16[128,64,256]{2,1,0:T(8,128)(2,1)S(1)} all-to-all(bf16[128,64,256]{2,1,0:T(8,128)(2,1)S(1)} %place.1), channel_id=1, replica_groups=mesh['rows'=64,'grp'=2] {'rows','grp'}, dimensions={0} | all-to-all | bytes 8388608 | tf_op jit(solution)/shard_map/all_to_all | solution.py:314
  86.3 7.1 %image.2 = (f32[2,64,256]{2,1,0:T(8,128)S(1)}, f32[1,1152]{1,0:T(1,128)S(1)}, f32[1,1152]{1,0:T(1,128)S(1)}) custom-call(s32[186]{0:T(256)S(1)} %pad_add_fusion.table_ref, s32[128,1,128]{2,1,0:T(1,128)S(1)} %all-to-all-done.wanted_ref, bf16[2,64,256]{2,1,0:T(8,128)(2,1)S(1)} %get-tuple-element.14.tiles_ref, ...), custom_call_target="tpu_custom_call" | custom-call | tf_op jit(solution)/shard_map/image/pallas_call | solution.py:348
  93.4 1.0 collective-permute-start
  94.4 0.8 collective-permute-done.given_ref
  95.3 14.2 %all_to_all.26.parts_ref = f32[64,1,1152]{2,1,0:T(1,128)S(1)} all-to-all(f32[64,1,1152]{2,1,0:T(1,128)S(1)} %spread.2), channel_id=1, replica_groups=mesh['rows'=64,'grp'=2] {'rows'}, dimensions={0} | all-to-all | bytes 589824 | tf_op jit(solution)/shard_map/all_to_all | solution.py:309
  109.5 1.6 collective-permute-start.1
  111.1 0.8 collective-permute-done.1.other_ref
  111.9 5.8 %normal.1 = (bf16[128,64,256]{2,1,0:T(8,128)(2,1)S(1)}, bf16[2,64,256]{2,1,0:T(8,128)(2,1)S(1)}) custom-call(s32[186]{0:T(256)S(1)} %pad_add_fusion.table_ref, s32[128,1,128]{2,1,0:T(1,128)S(1)} %all-to-all-done.wanted_ref, f32[1,1152]{1,0:T(1,128)S(1)} %total.2.own_ref, f32[1,1152]{1,0:T(1,128)S(1)} %collective-permute-done.1.other_ref, ...), custom_call_target="tpu_custom_call" | custom-call | tf_op jit(solution)/shard_map/normal/pallas_call | solution.py:378
  117.7 56.3 %all_to_all.27.arrived_ref = bf16[128,64,256]{2,1,0:T(8,128)(2,1)S(1)} all-to-all(bf16[128,64,256]{2,1,0:T(8,128)(2,1)S(1)} %get-tuple-element.20), channel_id=1, replica_groups=mesh['rows'=64,'grp'=2] {'rows','grp'}, dimensions={0} | all-to-all | bytes 8388608 | tf_op jit(solution)/shard_map/all_to_all | solution.py:314
  174.0 7.3 %image.3 = (f32[2,64,256]{2,1,0:T(8,128)S(1)}, f32[1,2176]{1,0:T(1,128)S(1)}, f32[1,2176]{1,0:T(1,128)S(1)}) custom-call(s32[186]{0:T(256)S(1)} %pad_add_fusion.table_ref, s32[128,1,128]{2,1,0:T(1,128)S(1)} %all-to-all-done.wanted_ref, bf16[2,64,256]{2,1,0:T(8,128)(2,1)S(1)} %get-tuple-element.19.tiles_ref, ...), custom_call_target="tpu_custom_call" | custom-call | tf_op jit(solution)/shard_map/image/pallas_call | solution.py:348
  181.4 1.0 collective-permute-start.2
  182.4 0.8 collective-permute-done.2.given_ref
  183.2 0.1 spread.3
  183.3 16.9 %all_to_all.28.parts_ref = f32[64,1,2176]{2,1,0:T(1,128)S(1)} all-to-all(f32[64,1,2176]{2,1,0:T(1,128)S(1)} %spread.3), channel_id=1, replica_groups=mesh['rows'=64,'grp'=2] {'rows'}, dimensions={0} | all-to-all | bytes 1114112 | tf_op jit(solution)/shard_map/all_to_all | solution.py:309
  200.2 1.8 collective-permute-start.3
  202.0 0.8 collective-permute-done.3.other_ref
  202.8 3.4 %last.1 = (f32[64,512]{1,0:T(8,128)}, f32[64,64]{1,0:T(8,128)}) custom-call(s32[186]{0:T(256)S(1)} %pad_add_fusion.table_ref, f32[1,2176]{1,0:T(1,128)S(1)} %total.3.own_ref, f32[1,2176]{1,0:T(1,128)S(1)} %collective-permute-done.3.other_ref, f32[2,64,256]{2,1,0:T(8,128)S(1)} %get-tuple-element.23.image_ref), custom_call_target="tpu_custom_call" | custom-call | tf_op jit(solution)/shard_map/last/pallas_call | solution.py:389
  (3 shorter events, 0.1 us)
Async XLA Ops:
  1.3 0.7 copy-start.2
  2.8 20.9 %all-to-all-start = ((s32[128,1,128]{2,1,0:T(1,128)}), s32[128,1,128]{2,1,0:T(1,128)S(1)}, u32[]{:S(2)}, u32[]{:S(2)}) async-start(s32[128,1,128]{2,1,0:T(1,128)} %ask.1), calls=%async_computation | async-start | bytes 131072 | tf_op jit(solution)/shard_map/all_to_all | solution.py:314
  15.0 0.8 copy-start.1
  21.6 1.9 copy-start
  93.4 1.8 collective-permute-start
  109.5 2.5 %collective-permute-start.1 = (f32[1,1152]{1,0:T(1,128)S(1)}, f32[1,1152]{1,0:T(1,128)S(1)}, u32[]{:S(2)}, u32[]{:S(2)}) collective-permute-start(f32[1,1152]{1,0:T(1,128)S(1)} %total.2.own_ref), channel_id=1, source_target_pairs={{0,1},{1,0},{2,3},{3,2},{4,5},{5,4},{6,7},{7,6},{8,9},{9,8},{10,11... | collective-permute-start | bytes 13832 | tf_op jit(solution)/shard_map/ppermute | solution.py:310
  181.4 1.8 collective-permute-start.2
  200.2 2.6 %collective-permute-start.3 = (f32[1,2176]{1,0:T(1,128)S(1)}, f32[1,2176]{1,0:T(1,128)S(1)}, u32[]{:S(2)}, u32[]{:S(2)}) collective-permute-start(f32[1,2176]{1,0:T(1,128)S(1)} %total.3.own_ref), channel_id=1, source_target_pairs={{0,1},{1,0},{2,3},{3,2},{4,5},{5,4},{6,7},{7,6},{8,9},{9,8},{10,11... | collective-permute-start | bytes 26120 | tf_op jit(solution)/shard_map/ppermute | solution.py:310

commit v6 on v5

--- a/solution.py
+++ b/solution.py
@@ -19,6 +19,7 @@
 ANY = pl.BlockSpec(memory_space=pl.ANY)
 MIB = 1024 * 1024
 SMALL = pltpu.CompilerParams(vmem_limit_bytes=8 * MIB)
+LARGE = pltpu.CompilerParams(vmem_limit_bytes=48 * MIB)
 
 
 def block_copy(blocks_ref, held, sems, i):
@@ -27,21 +28,18 @@
 
 
 def start_blocks(live, blocks_ref, held, sems):
-    chunks = (live + CHUNK - 1) // CHUNK
-
     def start(i, carry):
         block_copy(blocks_ref, held, sems, i).start()
         return carry
 
-    lax.fori_loop(0, chunks, start, 0)
-    return chunks
-
-
-def multiply_mirrors(me, table_ref, live, chunks, tiles_ref, blocks_ref, held, sems, out_ref):
+    lax.fori_loop(0, (live + CHUNK - 1) // CHUNK, start, 0)
+
+
+def multiply_mirrors(me, table_ref, live, tiles_ref, held, out_ref, wait):
     row_blocks = tiles_ref.shape[0]
 
     def visit(i, carry):
-        block_copy(blocks_ref, held, sems, i).wait()
+        wait(i)
         for j in range(CHUNK):
             s = i * CHUNK + j
             local = table_ref[FIRST + s] - me * row_blocks
@@ -50,7 +48,7 @@
             out_ref[place] = product.astype(out_ref.dtype)
         return carry
 
-    lax.fori_loop(0, chunks, visit, 0)
+    lax.fori_loop(0, (live + CHUNK - 1) // CHUNK, visit, 0)
 
 
 def place_tiles(start, end, wanted_ref, tiles_ref, out_ref):
@@ -87,11 +85,14 @@
 
 def first_kernel(table_ref, basis_ref, blocks_ref, out_ref, tiles_ref, held, sems):
     live = table_ref[LIVE]
-    chunks = start_blocks(live, blocks_ref, held, sems)
+    start_blocks(live, blocks_ref, held, sems)
     row_blocks, _, size = tiles_ref.shape
     for j in range(row_blocks):
         tiles_ref[j] = basis_ref[:, j * size : (j + 1) * size]
-    multiply_mirrors(table_ref[ME], table_ref, live, chunks, tiles_ref, blocks_ref, held, sems, out_ref)
+    multiply_mirrors(
+        table_ref[ME], table_ref, live, tiles_ref, held, out_ref,
+        lambda i: block_copy(blocks_ref, held, sems, i).wait(),
+    )
 
 
 def place_kernel(table_ref, wanted_ref, tiles_ref, given_ref, out_ref, sems):
@@ -151,11 +152,10 @@
 
 
 def image_kernel(
-    with_projection, table_ref, wanted_ref, tiles_ref, arrived_ref, blocks_ref,
-    image_ref, own_ref, given_ref, held, sems,
+    with_projection, table_ref, wanted_ref, tiles_ref, arrived_ref, held,
+    image_ref, own_ref, given_ref,
 ):
     me, live = table_ref[ME], table_ref[LIVE]
-    chunks = start_blocks(live, blocks_ref, held, sems)
     row_blocks = tiles_ref.shape[0]
 
     def add_mirror(d, sums):
@@ -169,7 +169,6 @@
         image_ref[k] = total
 
     def visit(i, carry):
-        block_copy(blocks_ref, held, sems, i).wait()
         for j in range(CHUNK):
             s = i * CHUNK + j
             local = table_ref[FIRST + s] - me * row_blocks
@@ -180,7 +179,7 @@
             image_ref[local] += lax.dot_general(tile, held[s], NT, preferred_element_type=jnp.float32)
         return carry
 
-    lax.fori_loop(0, chunks, visit, 0)
+    lax.fori_loop(0, (live + CHUNK - 1) // CHUNK, visit, 0)
 
     def summed(left_ref):
         total = None
@@ -250,17 +249,15 @@
 
 
 def normal_kernel(
-    total_rows, table_ref, wanted_ref, own_ref, other_ref, image_ref, blocks_ref,
-    out_ref, tiles_ref, held, sems,
+    total_rows, table_ref, wanted_ref, own_ref, other_ref, image_ref, held, out_ref, tiles_ref,
 ):
     me, live = table_ref[ME], table_ref[LIVE]
-    chunks = start_blocks(live, blocks_ref, held, sems)
     inverse = inverse_factor(whole_sum(me % 2, own_ref, other_ref, 0) / total_rows)
     for j in range(tiles_ref.shape[0]):
         tiles_ref[j] = jnp.dot(
             inverse, image_ref[j], precision=HIGHEST, preferred_element_type=jnp.float32
         ).astype(tiles_ref.dtype)
-    multiply_mirrors(me, table_ref, live, chunks, tiles_ref, blocks_ref, held, sems, out_ref)
+    multiply_mirrors(me, table_ref, live, tiles_ref, held, out_ref, lambda i: None)
     place_tiles(0, me, wanted_ref, tiles_ref, out_ref)
 
 
@@ -333,11 +330,7 @@
     wanted = exchange(asked)
     table = jnp.concatenate([me.reshape(1).astype(jnp.int32), block_count, block_row, block_col])
 
-    params = pltpu.CompilerParams(vmem_limit_bytes=48 * MIB)
-    scratch = [
-        pltpu.VMEM(kernel_blocks.shape, kernel_blocks.dtype),
-        pltpu.SemaphoreType.DMA((slots // CHUNK,)),
-    ]
+    params = pltpu.CompilerParams(vmem_limit_bytes=12 * MIB)
     tiles_shape = jax.ShapeDtypeStruct((row_blocks, columns, size), jnp.bfloat16)
     image_shape = jax.ShapeDtypeStruct((row_blocks, columns, size), jnp.float32)
     out_shape = jax.ShapeDtypeStruct((devices, columns, size), jnp.bfloat16)
@@ -348,9 +341,8 @@
         return pl.pallas_call(
             functools.partial(image_kernel, with_projection),
             out_shape=(image_shape, half, half),
-            in_specs=[SMEM] + [VMEM] * 3 + [ANY],
+            in_specs=[SMEM] + [VMEM] * 4,
             out_specs=(VMEM, VMEM, VMEM),
-            scratch_shapes=scratch,
             compiler_params=params,
             name="image",
         )(table, wanted, tiles, arrived, kernel_blocks)
@@ -360,8 +352,11 @@
         out_shape=(out_shape, tiles_shape),
         in_specs=[SMEM] + [VMEM, ANY],
         out_specs=(VMEM, VMEM),
-        scratch_shapes=scratch,
-        compiler_params=params,
+        scratch_shapes=[
+            pltpu.VMEM(kernel_blocks.shape, kernel_blocks.dtype),
+            pltpu.SemaphoreType.DMA((slots // CHUNK,)),
+        ],
+        compiler_params=LARGE,
         name="first",
     )(table, start_basis.T, kernel_blocks)
     outgoing = pl.pallas_call(
@@ -370,7 +365,7 @@
         in_specs=[SMEM] + [VMEM] * 2 + [ANY],
         out_specs=VMEM,
         scratch_shapes=[pltpu.SemaphoreType.DMA((8,))],
-        compiler_params=params,
+        compiler_params=pltpu.CompilerParams(vmem_limit_bytes=56 * MIB),
         name="place",
     )(table, wanted, tiles, outgoing)
     image, own, given = image_of(tiles, exchange(outgoing), False)
@@ -378,9 +373,8 @@
     outgoing, tiles = pl.pallas_call(
         functools.partial(normal_kernel, total_rows),
         out_shape=(out_shape, tiles_shape),
-        in_specs=[SMEM] + [VMEM] * 4 + [ANY],
+        in_specs=[SMEM] + [VMEM] * 5,
         out_specs=(VMEM, VMEM),
-        scratch_shapes=scratch,
         compiler_params=params,
         name="normal",
     )(table, wanted, own, other, image, kernel_blocks)

time: 207 us -> 212 us (1.024)
  local copies, waits for them, and re-layouts: 3.43 us -> 9.12 us
    unnamed x6 -> x20, local copies, waits for them, and re-layouts: 3.43 us -> 9.12 us
    pallas_call x2, Pallas kernels: 14.4 us -> 10.8 us  [image_of(): pl.pallas_call(functools.partial(image_kernel, with_projection), out_shap...]
    pallas_call x1, Pallas kernels: 2.82 us -> 5.13 us  [on_device(): pl.pallas_call(place_kernel, out_shape=out_shape, in_specs=[SMEM] + [VMEM...]
  transfers between devices with their start and end apart: 5 -> 5, of which waited for: 5 -> 4; matrix products, arithmetic and copies ran while one was open for 0% -> 0% of each run, Pallas kernels for 3% -> 3%
where the time goes in v6:
time: 212 us; the launch traced here: 211 us
  blocking collectives  148 us (70%)
  Pallas kernels  31.4 us (15%)
  starting transfers between devices  17 us (8%)
  local copies, waits for them, and re-layouts  9.12 us (4%)
  waiting for transfers between devices  3.31 us (2%)
    all_to_all x2, blocking collectives, exchange(): lax.all_to_all(outgoing, AXES, split_axis=0, concat_axis=0, tiled=True)  116 us
    all_to_all x2, blocking collectives, sum_over_devices(): lax.all_to_all(spread, 'rows', 0, 0, tiled=True)  31.6 us
    all_to_all x1, starting transfers between devices, exchange(): lax.all_to_all(outgoing, AXES, split_axis=0, concat_axis=0, tiled=True)  11.5 us
    pallas_call x2, Pallas kernels, image_of(): pl.pallas_call(functools.partial(image_kernel, with_projection), out_shap...  10.8 us
    unnamed x20, local copies, waits for them, and re-layouts  9.12 us
    pallas_call x1, Pallas kernels, on_device(): pl.pallas_call(first_kernel, out_shape=(out_shape, tiles_shape), in_specs...  5.76 us
    pallas_call x1, Pallas kernels, on_device(): pl.pallas_call(functools.partial(normal_kernel, total_rows), out_shape=(o...  5.42 us
    pallas_call x1, Pallas kernels, on_device(): pl.pallas_call(place_kernel, out_shape=out_shape, in_specs=[SMEM] + [VMEM...  5.13 us
  transfers between devices with their start and end apart: 5, of which 4 were waited for; matrix products, arithmetic and copies ran while one was open for 0% of the time, Pallas kernels for 3%

profile of v6, /device:TPU:1, one launch (start us, length us, event | category | flops | bytes accessed | tf_op | source)
XLA Modules:
  0.0 210.9 jit_solution(10865293664159011765)
XLA Ops:
  1.3 0.0 copy-start.9
  1.3 0.6 copy-done.9
  1.9 0.8 ask.1
  2.8 11.5 %all-to-all-start = ((s32[128,1,128]{2,1,0:T(1,128)}), s32[128,1,128]{2,1,0:T(1,128)S(1)}, u32[]{:S(2)}, u32[]{:S(2)}) async-start(s32[128,1,128]{2,1,0:T(1,128)} %ask.1), calls=%async_computation | async-start | bytes 131072 | tf_op jit(solution)/shard_map/all_to_all | solution.py:311
  14.3 0.8 pad_add_fusion.table_ref
  15.0 0.0 copy-start.7
  15.0 0.0 copy-start.6
  15.0 0.8 copy-done.6
  15.9 5.8 %first.1 = (bf16[128,64,256]{2,1,0:T(8,128)(2,1)S(1)}, bf16[2,64,256]{2,1,0:T(8,128)(2,1)S(1)}) custom-call(s32[186]{0:T(256)S(1)} %pad_add_fusion.table_ref, bf16[64,512]{1,0:T(8,128)(2,1)S(1)} %bitcast.4, bf16[92,256,256]{2,1,0:T(8,128)(2,1)} %held.5), custom_call_target="tpu_custom_call" | custom-call | tf_op jit(solution)/shard_map/first/pallas_call | solution.py:350
  21.7 0.0 copy-done.7
  21.7 0.0 copy-start.1
  21.7 1.9 copy-done.1
  23.6 0.0 copy-start.4
  23.6 0.6 copy-done.4
  24.2 0.0 all-to-all-done.wanted_ref
  24.2 0.0 copy-start.2
  24.2 0.6 copy-done.2
  24.9 5.1 %place.1 = bf16[128,64,256]{2,1,0:T(8,128)(2,1)} custom-call(s32[186]{0:T(256)} %copy-done.7, s32[128,1,128]{2,1,0:T(1,128)} %copy-done.2, bf16[2,64,256]{2,1,0:T(8,128)(2,1)} %copy-done.4, bf16[128,64,256]{2,1,0:T(8,128)(2,1)} %copy-done.1), custom_call_target="tpu_custom_call" | custom-call | tf_op jit(solution)/shard_map/place/pallas_call | solution.py:362
  30.0 0.0 copy-start.3
  30.0 0.0 copy-start.5
  30.0 0.0 copy-start.8
  30.0 60.1 %all_to_all.25.arrived_ref = bf16[128,64,256]{2,1,0:T(8,128)(2,1)S(1)} all-to-all(bf16[128,64,256]{2,1,0:T(8,128)(2,1)} %place.1), channel_id=1, replica_groups=mesh['rows'=64,'grp'=2] {'rows','grp'}, dimensions={0} | all-to-all | bytes 8388608 | tf_op jit(solution)/shard_map/all_to_all | solution.py:311
  90.1 0.0 copy-done.3
  90.1 0.0 copy-done.5
  90.1 0.0 copy-done.8
  90.1 0.0 copy-start
  90.1 4.4 %copy-done = bf16[92,256,256]{2,1,0:T(8,128)(2,1)S(1)} copy-done((bf16[92,256,256]{2,1,0:T(8,128)(2,1)S(1)}, bf16[92,256,256]{2,1,0:T(8,128)(2,1)}, u32[]{:S(2)}) %copy-start) | copy-done | bytes 12058648
  94.5 5.3 %image.2 = (f32[2,64,256]{2,1,0:T(8,128)S(1)}, f32[1,1152]{1,0:T(1,128)S(1)}, f32[1,1152]{1,0:T(1,128)S(1)}) custom-call(s32[186]{0:T(256)S(1)} %copy-done.8, s32[128,1,128]{2,1,0:T(1,128)S(1)} %copy-done.3, bf16[2,64,256]{2,1,0:T(8,128)(2,1)S(1)} %copy-done.5, bf16[128,64,256]{2,1,0:T(8,128)(2,1)S(1)} %all_to_all.25.arrived_ref, ...), custom_call_target="tpu_custom_call" | custom-call | tf_op jit(solution)/shard_map/image/pallas_call | solution.py:341
  99.8 1.0 collective-permute-start
  100.8 0.8 collective-permute-done.given_ref
  101.7 14.5 %all_to_all.26.parts_ref = f32[64,1,1152]{2,1,0:T(1,128)S(1)} all-to-all(f32[64,1,1152]{2,1,0:T(1,128)S(1)} %spread.2), channel_id=1, replica_groups=mesh['rows'=64,'grp'=2] {'rows'}, dimensions={0} | all-to-all | bytes 589824 | tf_op jit(solution)/shard_map/all_to_all | solution.py:306
  116.2 1.6 collective-permute-start.1
  117.8 0.8 collective-permute-done.1.other_ref
  118.6 5.4 %normal.1 = (bf16[128,64,256]{2,1,0:T(8,128)(2,1)S(1)}, bf16[2,64,256]{2,1,0:T(8,128)(2,1)S(1)}) custom-call(s32[186]{0:T(256)S(1)} %copy-done.8, s32[128,1,128]{2,1,0:T(1,128)S(1)} %copy-done.3, f32[1,1152]{1,0:T(1,128)S(1)} %total.2.own_ref, f32[1,1152]{1,0:T(1,128)S(1)} %collective-permute-done.1.other_ref, ...), custom_call_target="tpu_custom_call" | custom-call | tf_op jit(solution)/shard_map/normal/pallas_call | solution.py:373
  124.1 56.3 %all_to_all.27.arrived_ref = bf16[128,64,256]{2,1,0:T(8,128)(2,1)S(1)} all-to-all(bf16[128,64,256]{2,1,0:T(8,128)(2,1)S(1)} %get-tuple-element.20), channel_id=1, replica_groups=mesh['rows'=64,'grp'=2] {'rows','grp'}, dimensions={0} | all-to-all | bytes 8388608 | tf_op jit(solution)/shard_map/all_to_all | solution.py:311
  180.3 5.5 %image.3 = (f32[2,64,256]{2,1,0:T(8,128)S(1)}, f32[1,2176]{1,0:T(1,128)S(1)}, f32[1,2176]{1,0:T(1,128)S(1)}) custom-call(s32[186]{0:T(256)S(1)} %copy-done.8, s32[128,1,128]{2,1,0:T(1,128)S(1)} %copy-done.3, bf16[2,64,256]{2,1,0:T(8,128)(2,1)S(1)} %get-tuple-element.19.tiles_ref, bf16[128,64,256]{2,1,0:T(8,128)(2,1)S(1)} %all_to_all.27.arrived_ref, ...), custom_call_target="tpu_custom_call" | custom-call | tf_op jit(solution)/shard_map/image/pallas_call | solution.py:341
  185.8 1.0 collective-permute-start.2
  186.8 0.8 collective-permute-done.2.given_ref
  187.7 0.1 spread.3
  187.7 17.1 %all_to_all.28.parts_ref = f32[64,1,2176]{2,1,0:T(1,128)S(1)} all-to-all(f32[64,1,2176]{2,1,0:T(1,128)S(1)} %spread.3), channel_id=1, replica_groups=mesh['rows'=64,'grp'=2] {'rows'}, dimensions={0} | all-to-all | bytes 1114112 | tf_op jit(solution)/shard_map/all_to_all | solution.py:306
  204.8 1.9 collective-permute-start.3
  206.7 0.8 collective-permute-done.3.other_ref
  207.6 3.4 %last.1 = (f32[64,512]{1,0:T(8,128)}, f32[64,64]{1,0:T(8,128)}) custom-call(s32[186]{0:T(256)S(1)} %copy-done.8, f32[1,2176]{1,0:T(1,128)S(1)} %total.3.own_ref, f32[1,2176]{1,0:T(1,128)S(1)} %collective-permute-done.3.other_ref, f32[2,64,256]{2,1,0:T(8,128)S(1)} %get-tuple-element.23.image_ref), custom_call_target="tpu_custom_call" | custom-call | tf_op jit(solution)/shard_map/last/pallas_call | solution.py:383
  (3 shorter events, 0.1 us)
Async XLA Ops:
  1.3 0.7 copy-start.9
  2.8 21.5 %all-to-all-start = ((s32[128,1,128]{2,1,0:T(1,128)}), s32[128,1,128]{2,1,0:T(1,128)S(1)}, u32[]{:S(2)}, u32[]{:S(2)}) async-start(s32[128,1,128]{2,1,0:T(1,128)} %ask.1), calls=%async_computation | async-start | bytes 131072 | tf_op jit(solution)/shard_map/all_to_all | solution.py:311
  15.0 6.6 %copy-start.7 = (s32[186]{0:T(256)}, s32[186]{0:T(256)S(1)}, u32[]{:S(2)}) copy-start(s32[186]{0:T(256)S(1)} %pad_add_fusion.table_ref) | copy-start | bytes 2236
  15.0 0.8 copy-start.6
  21.7 1.9 copy-start.1
  23.6 0.6 copy-start.4
  24.2 0.6 copy-start.2
  30.0 60.1 %copy-start.3 = (s32[128,1,128]{2,1,0:T(1,128)S(1)}, s32[128,1,128]{2,1,0:T(1,128)}, u32[]{:S(2)}) copy-start(s32[128,1,128]{2,1,0:T(1,128)} %copy-done.2) | copy-start | bytes 196612
  30.0 60.1 %copy-start.5 = (bf16[2,64,256]{2,1,0:T(8,128)(2,1)S(1)}, bf16[2,64,256]{2,1,0:T(8,128)(2,1)}, u32[]{:S(2)}) copy-start(bf16[2,64,256]{2,1,0:T(8,128)(2,1)} %copy-done.4) | copy-start | bytes 196612
  30.0 60.1 %copy-start.8 = (s32[186]{0:T(256)S(1)}, s32[186]{0:T(256)}, u32[]{:S(2)}) copy-start(s32[186]{0:T(256)} %copy-done.7) | copy-start | bytes 2236
  90.1 4.4 %copy-start = (bf16[92,256,256]{2,1,0:T(8,128)(2,1)S(1)}, bf16[92,256,256]{2,1,0:T(8,128)(2,1)}, u32[]{:S(2)}) copy-start(bf16[92,256,256]{2,1,0:T(8,128)(2,1)} %held.5) | copy-start | bytes 36175876
  99.8 1.8 collective-permute-start
  116.2 2.5 %collective-permute-start.1 = (f32[1,1152]{1,0:T(1,128)S(1)}, f32[1,1152]{1,0:T(1,128)S(1)}, u32[]{:S(2)}, u32[]{:S(2)}) collective-permute-start(f32[1,1152]{1,0:T(1,128)S(1)} %total.2.own_ref), channel_id=1, source_target_pairs={{0,1},{1,0},{2,3},{3,2},{4,5},{5,4},{6,7},{7,6},{8,9},{9,8},{10,11... | collective-permute-start | bytes 13832 | tf_op jit(solution)/shard_map/ppermute | solution.py:307
  185.8 1.8 collective-permute-start.2
  204.8 2.7 %collective-permute-start.3 = (f32[1,2176]{1,0:T(1,128)S(1)}, f32[1,2176]{1,0:T(1,128)S(1)}, u32[]{:S(2)}, u32[]{:S(2)}) collective-permute-start(f32[1,2176]{1,0:T(1,128)S(1)} %total.3.own_ref), channel_id=1, source_target_pairs={{0,1},{1,0},{2,3},{3,2},{4,5},{5,4},{6,7},{7,6},{8,9},{9,8},{10,11... | collective-permute-start | bytes 26120 | tf_op jit(solution)/shard_map/ppermute | solution.py:307

commit v7 on v6

--- a/solution.py
+++ b/solution.py
@@ -95,28 +95,18 @@
     )
 
 
-def place_kernel(table_ref, wanted_ref, tiles_ref, given_ref, out_ref, sems):
-    me = table_ref[ME]
-    groups = sems.shape[0]
-    size = out_ref.shape[0] // groups
-    first = me // size
-
-    def copy_of(g):
-        at = pl.ds(g * size, size)
-        return pltpu.make_async_copy(given_ref.at[at], out_ref.at[at], sems.at[g])
-
-    def start(g, carry):
-        copy_of(g).start()
-        return carry
-
-    def wait(g, carry):
-        copy_of(g).wait()
-        return carry
-
-    lax.fori_loop(first, groups, start, 0)
-    place_tiles(0, first * size, wanted_ref, tiles_ref, out_ref)
-    lax.fori_loop(first, groups, wait, 0)
-    place_tiles(first * size, me, wanted_ref, tiles_ref, out_ref)
+def place_kernel(table_ref, wanted_ref, tiles_ref, given_ref, out_ref):
+    me, devices = table_ref[ME], out_ref.shape[0]
+    place_tiles(0, me, wanted_ref, tiles_ref, out_ref)
+    group = 4
+
+    def keep(i, carry):
+        for j in range(group):
+            d = jnp.minimum(me + i * group + j, devices - 1)
+            out_ref[d] = given_ref[d]
+        return carry
+
+    lax.fori_loop(0, (devices - me + group - 1) // group, keep, 0)
 
 
 def row_of(k):
@@ -362,10 +352,9 @@
     outgoing = pl.pallas_call(
         place_kernel,
         out_shape=out_shape,
-        in_specs=[SMEM] + [VMEM] * 2 + [ANY],
+        in_specs=[SMEM] + [VMEM] * 3,
         out_specs=VMEM,
-        scratch_shapes=[pltpu.SemaphoreType.DMA((8,))],
-        compiler_params=pltpu.CompilerParams(vmem_limit_bytes=56 * MIB),
+        compiler_params=params,
         name="place",
     )(table, wanted, tiles, outgoing)
     image, own, given = image_of(tiles, exchange(outgoing), False)

time: 212 us -> 205 us (0.967)
  Pallas kernels: 31.4 us -> 27.4 us
  local copies, waits for them, and re-layouts: 9.12 us -> 5.63 us
    pallas_call x1, Pallas kernels: 5.13 us -> 1.1 us  [on_device(): pl.pallas_call(place_kernel, out_shape=out_shape, in_specs=[SMEM] + [VMEM...]
    unnamed x20 -> x10, local copies, waits for them, and re-layouts: 9.12 us -> 5.63 us
  transfers between devices with their start and end apart: 5 -> 5, of which waited for: 4 -> 5; matrix products, arithmetic and copies ran while one was open for 0% -> 0% of each run, Pallas kernels for 3% -> 3%
where the time goes in v7:
time: 205 us; the launch traced here: 204 us
  blocking collectives  148 us (72%)
  Pallas kernels  27.4 us (13%)
  starting transfers between devices  17 us (8%)
  local copies, waits for them, and re-layouts  5.63 us (3%)
  waiting for transfers between devices  3.4 us (2%)
    all_to_all x2, blocking collectives, exchange(): lax.all_to_all(outgoing, AXES, split_axis=0, concat_axis=0, tiled=True)  117 us
    all_to_all x2, blocking collectives, sum_over_devices(): lax.all_to_all(spread, 'rows', 0, 0, tiled=True)  31.5 us
    all_to_all x1, starting transfers between devices, exchange(): lax.all_to_all(outgoing, AXES, split_axis=0, concat_axis=0, tiled=True)  11.5 us
    pallas_call x2, Pallas kernels, image_of(): pl.pallas_call(functools.partial(image_kernel, with_projection), out_shap...  10.8 us
    pallas_call x1, Pallas kernels, on_device(): pl.pallas_call(first_kernel, out_shape=(out_shape, tiles_shape), in_specs...  5.76 us
    unnamed x10, local copies, waits for them, and re-layouts  5.63 us
    pallas_call x1, Pallas kernels, on_device(): pl.pallas_call(functools.partial(normal_kernel, total_rows), out_shape=(o...  5.42 us
  transfers between devices with their start and end apart: 5, of which 5 were waited for; matrix products, arithmetic and copies ran while one was open for 0% of the time, Pallas kernels for 3%

profile of v7, /device:TPU:1, one launch (start us, length us, event | category | flops | bytes accessed | tf_op | source)
XLA Modules:
  0.0 204.0 jit_solution(16693208237850655542)
XLA Ops:
  1.3 0.0 copy-start.4
  1.3 0.6 copy-done.4
  1.9 0.8 ask.1
  2.8 11.5 %all-to-all-start = ((s32[128,1,128]{2,1,0:T(1,128)}), s32[128,1,128]{2,1,0:T(1,128)S(1)}, u32[]{:S(2)}, u32[]{:S(2)}) async-start(s32[128,1,128]{2,1,0:T(1,128)} %ask.1), calls=%async_computation | async-start | bytes 131072 | tf_op jit(solution)/shard_map/all_to_all | solution.py:301
  14.3 0.8 pad_add_fusion.table_ref
  15.0 0.0 copy-start.3
  15.0 0.8 copy-done.3
  15.9 5.8 %first.1 = (bf16[128,64,256]{2,1,0:T(8,128)(2,1)S(1)}, bf16[2,64,256]{2,1,0:T(8,128)(2,1)S(1)}) custom-call(s32[186]{0:T(256)S(1)} %pad_add_fusion.table_ref, bf16[64,512]{1,0:T(8,128)(2,1)S(1)} %bitcast.4, bf16[92,256,256]{2,1,0:T(8,128)(2,1)} %held.5), custom_call_target="tpu_custom_call" | custom-call | tf_op jit(solution)/shard_map/first/pallas_call | solution.py:340
  21.6 0.0 copy-start.1
  21.7 1.9 copy-done.1
  23.6 0.1 all-to-all-done.wanted_ref
  23.7 0.0 copy-start.2
  23.7 2.2 %copy-done.2 = bf16[128,64,256]{2,1,0:T(8,128)(2,1)S(1)} copy-done((bf16[128,64,256]{2,1,0:T(8,128)(2,1)S(1)}, bf16[128,64,256]{2,1,0:T(8,128)(2,1)}, u32[]{:S(2)}) %copy-start.2) | copy-done | bytes 4194328
  25.9 0.0 copy-start
  25.9 1.1 place.1
  27.0 60.7 %all_to_all.25.arrived_ref = bf16[128,64,256]{2,1,0:T(8,128)(2,1)S(1)} all-to-all(bf16[128,64,256]{2,1,0:T(8,128)(2,1)S(1)} %place.1), channel_id=1, replica_groups=mesh['rows'=64,'grp'=2] {'rows','grp'}, dimensions={0} | all-to-all | bytes 8388608 | tf_op jit(solution)/shard_map/all_to_all | solution.py:301
  87.7 0.0 copy-done
  87.7 5.3 %image.2 = (f32[2,64,256]{2,1,0:T(8,128)S(1)}, f32[1,1152]{1,0:T(1,128)S(1)}, f32[1,1152]{1,0:T(1,128)S(1)}) custom-call(s32[186]{0:T(256)S(1)} %pad_add_fusion.table_ref, s32[128,1,128]{2,1,0:T(1,128)S(1)} %all-to-all-done.wanted_ref, bf16[2,64,256]{2,1,0:T(8,128)(2,1)S(1)} %get-tuple-element.14.tiles_ref, ...), custom_call_target="tpu_custom_call" | custom-call | tf_op jit(solution)/shard_map/image/pallas_call | solution.py:331
  92.9 1.0 collective-permute-start
  93.9 0.8 collective-permute-done.given_ref
  94.8 14.5 %all_to_all.26.parts_ref = f32[64,1,1152]{2,1,0:T(1,128)S(1)} all-to-all(f32[64,1,1152]{2,1,0:T(1,128)S(1)} %spread.2), channel_id=1, replica_groups=mesh['rows'=64,'grp'=2] {'rows'}, dimensions={0} | all-to-all | bytes 589824 | tf_op jit(solution)/shard_map/all_to_all | solution.py:296
  109.3 1.6 collective-permute-start.1
  110.9 0.8 collective-permute-done.1.other_ref
  111.8 5.4 %normal.1 = (bf16[128,64,256]{2,1,0:T(8,128)(2,1)S(1)}, bf16[2,64,256]{2,1,0:T(8,128)(2,1)S(1)}) custom-call(s32[186]{0:T(256)S(1)} %pad_add_fusion.table_ref, s32[128,1,128]{2,1,0:T(1,128)S(1)} %all-to-all-done.wanted_ref, f32[1,1152]{1,0:T(1,128)S(1)} %total.2.own_ref, f32[1,1152]{1,0:T(1,128)S(1)} %collective-permute-done.1.other_ref, ...), custom_call_target="tpu_custom_call" | custom-call | tf_op jit(solution)/shard_map/normal/pallas_call | solution.py:362
  117.2 56.3 %all_to_all.27.arrived_ref = bf16[128,64,256]{2,1,0:T(8,128)(2,1)S(1)} all-to-all(bf16[128,64,256]{2,1,0:T(8,128)(2,1)S(1)} %get-tuple-element.20), channel_id=1, replica_groups=mesh['rows'=64,'grp'=2] {'rows','grp'}, dimensions={0} | all-to-all | bytes 8388608 | tf_op jit(solution)/shard_map/all_to_all | solution.py:301
  173.5 5.5 %image.3 = (f32[2,64,256]{2,1,0:T(8,128)S(1)}, f32[1,2176]{1,0:T(1,128)S(1)}, f32[1,2176]{1,0:T(1,128)S(1)}) custom-call(s32[186]{0:T(256)S(1)} %pad_add_fusion.table_ref, s32[128,1,128]{2,1,0:T(1,128)S(1)} %all-to-all-done.wanted_ref, bf16[2,64,256]{2,1,0:T(8,128)(2,1)S(1)} %get-tuple-element.19.tiles_ref, ...), custom_call_target="tpu_custom_call" | custom-call | tf_op jit(solution)/shard_map/image/pallas_call | solution.py:331
  179.0 1.0 collective-permute-start.2
  180.0 0.8 collective-permute-done.2.given_ref
  180.8 0.1 spread.3
  180.8 17.1 %all_to_all.28.parts_ref = f32[64,1,2176]{2,1,0:T(1,128)S(1)} all-to-all(f32[64,1,2176]{2,1,0:T(1,128)S(1)} %spread.3), channel_id=1, replica_groups=mesh['rows'=64,'grp'=2] {'rows'}, dimensions={0} | all-to-all | bytes 1114112 | tf_op jit(solution)/shard_map/all_to_all | solution.py:296
  197.9 1.9 collective-permute-start.3
  199.8 0.8 collective-permute-done.3.other_ref
  200.7 3.4 %last.1 = (f32[64,512]{1,0:T(8,128)}, f32[64,64]{1,0:T(8,128)}) custom-call(s32[186]{0:T(256)S(1)} %pad_add_fusion.table_ref, f32[1,2176]{1,0:T(1,128)S(1)} %total.3.own_ref, f32[1,2176]{1,0:T(1,128)S(1)} %collective-permute-done.3.other_ref, f32[2,64,256]{2,1,0:T(8,128)S(1)} %get-tuple-element.23.image_ref), custom_call_target="tpu_custom_call" | custom-call | tf_op jit(solution)/shard_map/last/pallas_call | solution.py:372
  (3 shorter events, 0.1 us)
Async XLA Ops:
  1.3 0.7 copy-start.4
  2.8 20.9 %all-to-all-start = ((s32[128,1,128]{2,1,0:T(1,128)}), s32[128,1,128]{2,1,0:T(1,128)S(1)}, u32[]{:S(2)}, u32[]{:S(2)}) async-start(s32[128,1,128]{2,1,0:T(1,128)} %ask.1), calls=%async_computation | async-start | bytes 131072 | tf_op jit(solution)/shard_map/all_to_all | solution.py:301
  15.0 0.8 copy-start.3
  21.6 2.0 copy-start.1
  23.7 2.2 %copy-start.2 = (bf16[128,64,256]{2,1,0:T(8,128)(2,1)S(1)}, bf16[128,64,256]{2,1,0:T(8,128)(2,1)}, u32[]{:S(2)}) copy-start(bf16[128,64,256]{2,1,0:T(8,128)(2,1)} %copy-done.1) | copy-start | bytes 12582916
  25.9 61.8 %copy-start = (bf16[92,256,256]{2,1,0:T(8,128)(2,1)S(1)}, bf16[92,256,256]{2,1,0:T(8,128)(2,1)}, u32[]{:S(2)}) copy-start(bf16[92,256,256]{2,1,0:T(8,128)(2,1)} %held.5) | copy-start | bytes 36175876
  92.9 1.8 collective-permute-start
  109.3 2.5 %collective-permute-start.1 = (f32[1,1152]{1,0:T(1,128)S(1)}, f32[1,1152]{1,0:T(1,128)S(1)}, u32[]{:S(2)}, u32[]{:S(2)}) collective-permute-start(f32[1,1152]{1,0:T(1,128)S(1)} %total.2.own_ref), channel_id=1, source_target_pairs={{0,1},{1,0},{2,3},{3,2},{4,5},{5,4},{6,7},{7,6},{8,9},{9,8},{10,11... | collective-permute-start | bytes 13832 | tf_op jit(solution)/shard_map/ppermute | solution.py:297
  179.0 1.8 collective-permute-start.2
  197.9 2.7 %collective-permute-start.3 = (f32[1,2176]{1,0:T(1,128)S(1)}, f32[1,2176]{1,0:T(1,128)S(1)}, u32[]{:S(2)}, u32[]{:S(2)}) collective-permute-start(f32[1,2176]{1,0:T(1,128)S(1)} %total.3.own_ref), channel_id=1, source_target_pairs={{0,1},{1,0},{2,3},{3,2},{4,5},{5,4},{6,7},{7,6},{8,9},{9,8},{10,11... | collective-permute-start | bytes 26120 | tf_op jit(solution)/shard_map/ppermute | solution.py:297

commit v8 on v7

--- a/solution.py
+++ b/solution.py
@@ -35,7 +35,11 @@
     lax.fori_loop(0, (live + CHUNK - 1) // CHUNK, start, 0)
 
 
-def multiply_mirrors(me, table_ref, live, tiles_ref, held, out_ref, wait):
+def place_of(s, table_ref, live, row_blocks, slots):
+    return jnp.where(s < live, table_ref[FIRST + slots + s] // row_blocks, 0)
+
+
+def multiply_mirrors(me, table_ref, live, tiles_ref, held, out_ref, wait, placed):
     row_blocks = tiles_ref.shape[0]
 
     def visit(i, carry):
@@ -43,7 +47,7 @@
         for j in range(CHUNK):
             s = i * CHUNK + j
             local = table_ref[FIRST + s] - me * row_blocks
-            place = jnp.where(s < live, table_ref[FIRST + held.shape[0] + s] // row_blocks, 0)
+            place = place_of(s, table_ref, live, row_blocks, held.shape[0]) if placed else s
             product = jnp.dot(tiles_ref[local], held[s], preferred_element_type=jnp.float32)
             out_ref[place] = product.astype(out_ref.dtype)
         return carry
@@ -91,22 +95,23 @@
         tiles_ref[j] = basis_ref[:, j * size : (j + 1) * size]
     multiply_mirrors(
         table_ref[ME], table_ref, live, tiles_ref, held, out_ref,
-        lambda i: block_copy(blocks_ref, held, sems, i).wait(),
+        lambda i: block_copy(blocks_ref, held, sems, i).wait(), False,
     )
 
 
-def place_kernel(table_ref, wanted_ref, tiles_ref, given_ref, out_ref):
-    me, devices = table_ref[ME], out_ref.shape[0]
+def place_kernel(table_ref, wanted_ref, tiles_ref, products_ref, out_ref):
+    me, live = table_ref[ME], table_ref[LIVE]
+    slots = products_ref.shape[0]
+    group = 4
+
+    def place(i, carry):
+        for j in range(group):
+            s = i * group + j
+            out_ref[place_of(s, table_ref, live, tiles_ref.shape[0], slots)] = products_ref[s]
+        return carry
+
+    lax.fori_loop(0, (live + group - 1) // group, place, 0)
     place_tiles(0, me, wanted_ref, tiles_ref, out_ref)
-    group = 4
-
-    def keep(i, carry):
-        for j in range(group):
-            d = jnp.minimum(me + i * group + j, devices - 1)
-            out_ref[d] = given_ref[d]
-        return carry
-
-    lax.fori_loop(0, (devices - me + group - 1) // group, keep, 0)
 
 
 def row_of(k):
@@ -143,18 +148,25 @@
 
 def image_kernel(
     with_projection, table_ref, wanted_ref, tiles_ref, arrived_ref, held,
-    image_ref, own_ref, given_ref,
+    image_ref, own_ref, given_ref, *turned_ref,
 ):
     me, live = table_ref[ME], table_ref[LIVE]
     row_blocks = tiles_ref.shape[0]
 
-    def add_mirror(d, sums):
-        wanted = spread_lanes(wanted_ref[d], image_ref.shape[2])
-        mirror = arrived_ref[d].astype(jnp.float32)
-        return tuple(total + jnp.where(wanted == k, mirror, 0.0) for k, total in enumerate(sums))
+    group = 4
+
+    def add_mirrors(i, sums):
+        for j in range(group):
+            d = i * group + j
+            at = jnp.minimum(d, me)
+            wanted = spread_lanes(wanted_ref[at], image_ref.shape[2])
+            wanted = jnp.where(d <= me, wanted, -1)
+            mirror = arrived_ref[at].astype(jnp.float32)
+            sums = tuple(total + jnp.where(wanted == k, mirror, 0.0) for k, total in enumerate(sums))
+        return sums
 
     zero = jnp.zeros(image_ref.shape[1:], image_ref.dtype)
-    sums = lax.fori_loop(0, me + 1, add_mirror, (zero,) * row_blocks)
+    sums = lax.fori_loop(0, (me + group) // group, add_mirrors, (zero,) * row_blocks)
     for k, total in enumerate(sums):
         image_ref[k] = total
 
@@ -166,7 +178,11 @@
             owner = column // row_blocks
             tile = jnp.where(owner == me, tiles_ref[column - owner * row_blocks], arrived_ref[owner])
             tile = jnp.where(s < live, tile, jnp.zeros_like(tile))
-            image_ref[local] += lax.dot_general(tile, held[s], NT, preferred_element_type=jnp.float32)
+            block = held[s]
+            if turned_ref:
+                block = block.T
+                turned_ref[0][s] = block
+            image_ref[local] += jnp.dot(tile, block, preferred_element_type=jnp.float32)
         return carry
 
     lax.fori_loop(0, (live + CHUNK - 1) // CHUNK, visit, 0)
@@ -247,7 +263,7 @@
         tiles_ref[j] = jnp.dot(
             inverse, image_ref[j], precision=HIGHEST, preferred_element_type=jnp.float32
         ).astype(tiles_ref.dtype)
-    multiply_mirrors(me, table_ref, live, tiles_ref, held, out_ref, lambda i: None)
+    multiply_mirrors(me, table_ref, live, tiles_ref, held, out_ref, lambda i: None, True)
     place_tiles(0, me, wanted_ref, tiles_ref, out_ref)
 
 
@@ -325,21 +341,22 @@
     image_shape = jax.ShapeDtypeStruct((row_blocks, columns, size), jnp.float32)
     out_shape = jax.ShapeDtypeStruct((devices, columns, size), jnp.bfloat16)
 
-    def image_of(tiles, arrived, with_projection):
+    def image_of(tiles, arrived, blocks, with_projection):
         parts = 2 if with_projection else 1
         half = jax.ShapeDtypeStruct((1, (parts * ROWS + 1) * LANES), jnp.float32)
+        turned = () if with_projection else (jax.ShapeDtypeStruct(blocks.shape, blocks.dtype),)
         return pl.pallas_call(
             functools.partial(image_kernel, with_projection),
-            out_shape=(image_shape, half, half),
+            out_shape=(image_shape, half, half) + turned,
             in_specs=[SMEM] + [VMEM] * 4,
-            out_specs=(VMEM, VMEM, VMEM),
+            out_specs=(VMEM,) * (3 + len(turned)),
             compiler_params=params,
             name="image",
-        )(table, wanted, tiles, arrived, kernel_blocks)
-
-    outgoing, tiles = pl.pallas_call(
+        )(table, wanted, tiles, arrived, blocks)
+
+    products, tiles = pl.pallas_call(
         first_kernel,
-        out_shape=(out_shape, tiles_shape),
+        out_shape=(jax.ShapeDtypeStruct((slots, columns, size), jnp.bfloat16), tiles_shape),
         in_specs=[SMEM] + [VMEM, ANY],
         out_specs=(VMEM, VMEM),
         scratch_shapes=[
@@ -356,8 +373,8 @@
         out_specs=VMEM,
         compiler_params=params,
         name="place",
-    )(table, wanted, tiles, outgoing)
-    image, own, given = image_of(tiles, exchange(outgoing), False)
+    )(table, wanted, tiles, products)
+    image, own, given, turned = image_of(tiles, exchange(outgoing), kernel_blocks, False)
     own, other = sum_over_devices(own, given)
     outgoing, tiles = pl.pallas_call(
         functools.partial(normal_kernel, total_rows),
@@ -367,7 +384,7 @@
         compiler_params=params,
         name="normal",
     )(table, wanted, own, other, image, kernel_blocks)
-    image, own, given = image_of(tiles, exchange(outgoing), True)
+    image, own, given = image_of(tiles, exchange(outgoing), turned, True)
     own, other = sum_over_devices(own, given)
     result, projected = pl.pallas_call(
         functools.partial(last_kernel, total_rows),

time: 205 us -> 199 us (0.971)
  local copies, waits for them, and re-layouts: 5.63 us -> 1.49 us
    unnamed x10 -> x6, local copies, waits for them, and re-layouts: 5.63 us -> 1.49 us
where the time goes in v8:
time: 199 us
  blocking collectives  147 us (74%)
  Pallas kernels  26 us (13%)
  starting transfers between devices  17 us (9%)
  waiting for transfers between devices  5.36 us (3%)
    all_to_all x2, blocking collectives, exchange(): lax.all_to_all(outgoing, AXES, split_axis=0, concat_axis=0, tiled=True)  115 us
    all_to_all x2, blocking collectives, sum_over_devices(): lax.all_to_all(spread, 'rows', 0, 0, tiled=True)  32.3 us
    all_to_all x1, starting transfers between devices, exchange(): lax.all_to_all(outgoing, AXES, split_axis=0, concat_axis=0, tiled=True)  11.5 us
    pallas_call x2, Pallas kernels, image_of(): pl.pallas_call(functools.partial(image_kernel, with_projection), out_shap...  9.28 us
    pallas_call x1, Pallas kernels, on_device(): pl.pallas_call(first_kernel, out_shape=(jax.ShapeDtypeStruct((slots, colu...  5.76 us
    pallas_call x1, Pallas kernels, on_device(): pl.pallas_call(functools.partial(normal_kernel, total_rows), out_shape=(o...  5.34 us
  transfers between devices with their start and end apart: 5, of which 5 were waited for; matrix products, arithmetic and copies ran while one was open for 0% of the time, Pallas kernels for 3%

profile of v8, /device:TPU:1, one launch (start us, length us, event | category | flops | bytes accessed | tf_op | source)
XLA Modules:
  0.0 199.4 jit_solution(1595131485050958566)
XLA Ops:
  1.3 0.0 copy-start.2
  1.3 0.6 copy-done.2
  1.9 0.8 ask.1
  2.8 11.5 %all-to-all-start = ((s32[128,1,128]{2,1,0:T(1,128)}), s32[128,1,128]{2,1,0:T(1,128)S(1)}, u32[]{:S(2)}, u32[]{:S(2)}) async-start(s32[128,1,128]{2,1,0:T(1,128)} %ask.1), calls=%async_computation | async-start | bytes 131072 | tf_op jit(solution)/shard_map/all_to_all | solution.py:317
  14.3 0.8 pad_add_fusion.table_ref
  15.0 0.0 copy-start.1
  15.0 0.8 copy-done.1
  15.9 5.8 %first.1 = (bf16[92,64,256]{2,1,0:T(8,128)(2,1)S(1)}, bf16[2,64,256]{2,1,0:T(8,128)(2,1)S(1)}) custom-call(s32[186]{0:T(256)S(1)} %pad_add_fusion.table_ref, bf16[64,512]{1,0:T(8,128)(2,1)S(1)} %bitcast.4, bf16[92,256,256]{2,1,0:T(8,128)(2,1)} %held.3), custom_call_target="tpu_custom_call" | custom-call | tf_op jit(solution)/shard_map/first/pallas_call | solution.py:357
  21.6 2.1 %all-to-all-done.wanted_ref = s32[128,1,128]{2,1,0:T(1,128)S(1)} async-done(((s32[128,1,128]{2,1,0:T(1,128)}), s32[128,1,128]{2,1,0:T(1,128)S(1)}, u32[]{:S(2)}, u32[]{:S(2)}) %all-to-all-start) | async-done | bytes 65568 | tf_op jit(solution)/shard_map/all_to_all | solution.py:317
  23.7 0.0 copy-start
  23.7 1.3 place.1
  25.0 58.8 %all_to_all.25.arrived_ref = bf16[128,64,256]{2,1,0:T(8,128)(2,1)S(1)} all-to-all(bf16[128,64,256]{2,1,0:T(8,128)(2,1)S(1)} %place.1), channel_id=1, replica_groups=mesh['rows'=64,'grp'=2] {'rows','grp'}, dimensions={0} | all-to-all | bytes 8388608 | tf_op jit(solution)/shard_map/all_to_all | solution.py:317
  83.9 0.0 copy-done
  83.9 5.4 %image.2 = (f32[2,64,256]{2,1,0:T(8,128)S(1)}, f32[1,1152]{1,0:T(1,128)S(1)}, f32[1,1152]{1,0:T(1,128)S(1)}, bf16[92,256,256]{2,1,0:T(8,128)(2,1)S(1)}) custom-call(s32[186]{0:T(256)S(1)} %pad_add_fusion.table_ref, s32[128,1,128]{2,1,0:T(1,128)S(1)} %all-to-all-done.wanted_ref, bf16[2,64,256]{2,1,0:T(8,128)(2,1)S(1)} %get-tuple-element.15.tiles_ref, ...), custom_call_target="tpu_custom_call" | custom-call | tf_op jit(solution)/shard_map/image/pallas_call | solution.py:348
  89.2 1.0 collective-permute-start
  90.2 0.8 collective-permute-done.given_ref
  91.1 14.5 %all_to_all.26.parts_ref = f32[64,1,1152]{2,1,0:T(1,128)S(1)} all-to-all(f32[64,1,1152]{2,1,0:T(1,128)S(1)} %spread.2), channel_id=1, replica_groups=mesh['rows'=64,'grp'=2] {'rows'}, dimensions={0} | all-to-all | bytes 589824 | tf_op jit(solution)/shard_map/all_to_all | solution.py:312
  105.6 1.6 collective-permute-start.1
  107.2 0.8 collective-permute-done.1.other_ref
  108.0 5.3 %normal.1 = (bf16[128,64,256]{2,1,0:T(8,128)(2,1)S(1)}, bf16[2,64,256]{2,1,0:T(8,128)(2,1)S(1)}) custom-call(s32[186]{0:T(256)S(1)} %pad_add_fusion.table_ref, s32[128,1,128]{2,1,0:T(1,128)S(1)} %all-to-all-done.wanted_ref, f32[1,1152]{1,0:T(1,128)S(1)} %total.2.own_ref, f32[1,1152]{1,0:T(1,128)S(1)} %collective-permute-done.1.other_ref, ...), custom_call_target="tpu_custom_call" | custom-call | tf_op jit(solution)/shard_map/normal/pallas_call | solution.py:379
  113.4 56.3 %all_to_all.27.arrived_ref = bf16[128,64,256]{2,1,0:T(8,128)(2,1)S(1)} all-to-all(bf16[128,64,256]{2,1,0:T(8,128)(2,1)S(1)} %get-tuple-element.21), channel_id=1, replica_groups=mesh['rows'=64,'grp'=2] {'rows','grp'}, dimensions={0} | all-to-all | bytes 8388608 | tf_op jit(solution)/shard_map/all_to_all | solution.py:317
  169.7 3.9 %image.3 = (f32[2,64,256]{2,1,0:T(8,128)S(1)}, f32[1,2176]{1,0:T(1,128)S(1)}, f32[1,2176]{1,0:T(1,128)S(1)}) custom-call(s32[186]{0:T(256)S(1)} %pad_add_fusion.table_ref, s32[128,1,128]{2,1,0:T(1,128)S(1)} %all-to-all-done.wanted_ref, bf16[2,64,256]{2,1,0:T(8,128)(2,1)S(1)} %get-tuple-element.20.tiles_ref, ...), custom_call_target="tpu_custom_call" | custom-call | tf_op jit(solution)/shard_map/image/pallas_call | solution.py:348
  173.6 1.0 collective-permute-start.2
  174.6 0.8 collective-permute-done.2.given_ref
  175.4 0.1 spread.3
  175.5 17.8 %all_to_all.28.parts_ref = f32[64,1,2176]{2,1,0:T(1,128)S(1)} all-to-all(f32[64,1,2176]{2,1,0:T(1,128)S(1)} %spread.3), channel_id=1, replica_groups=mesh['rows'=64,'grp'=2] {'rows'}, dimensions={0} | all-to-all | bytes 1114112 | tf_op jit(solution)/shard_map/all_to_all | solution.py:312
  193.3 1.9 collective-permute-start.3
  195.2 0.8 collective-permute-done.3.other_ref
  196.1 3.4 %last.1 = (f32[64,512]{1,0:T(8,128)}, f32[64,64]{1,0:T(8,128)}) custom-call(s32[186]{0:T(256)S(1)} %pad_add_fusion.table_ref, f32[1,2176]{1,0:T(1,128)S(1)} %total.3.own_ref, f32[1,2176]{1,0:T(1,128)S(1)} %collective-permute-done.3.other_ref, f32[2,64,256]{2,1,0:T(8,128)S(1)} %get-tuple-element.25.image_ref), custom_call_target="tpu_custom_call" | custom-call | tf_op jit(solution)/shard_map/last/pallas_call | solution.py:389
  (3 shorter events, 0.1 us)
Async XLA Ops:
  1.3 0.7 copy-start.2
  2.8 20.9 %all-to-all-start = ((s32[128,1,128]{2,1,0:T(1,128)}), s32[128,1,128]{2,1,0:T(1,128)S(1)}, u32[]{:S(2)}, u32[]{:S(2)}) async-start(s32[128,1,128]{2,1,0:T(1,128)} %ask.1), calls=%async_computation | async-start | bytes 131072 | tf_op jit(solution)/shard_map/all_to_all | solution.py:317
  15.0 0.8 copy-start.1
  23.7 60.2 %copy-start = (bf16[92,256,256]{2,1,0:T(8,128)(2,1)S(1)}, bf16[92,256,256]{2,1,0:T(8,128)(2,1)}, u32[]{:S(2)}) copy-start(bf16[92,256,256]{2,1,0:T(8,128)(2,1)} %held.3) | copy-start | bytes 36175876
  89.2 1.8 collective-permute-start
  105.6 2.5 %collective-permute-start.1 = (f32[1,1152]{1,0:T(1,128)S(1)}, f32[1,1152]{1,0:T(1,128)S(1)}, u32[]{:S(2)}, u32[]{:S(2)}) collective-permute-start(f32[1,1152]{1,0:T(1,128)S(1)} %total.2.own_ref), channel_id=1, source_target_pairs={{0,1},{1,0},{2,3},{3,2},{4,5},{5,4},{6,7},{7,6},{8,9},{9,8},{10,11... | collective-permute-start | bytes 13832 | tf_op jit(solution)/shard_map/ppermute | solution.py:313
  173.6 1.8 collective-permute-start.2
  193.3 2.7 %collective-permute-start.3 = (f32[1,2176]{1,0:T(1,128)S(1)}, f32[1,2176]{1,0:T(1,128)S(1)}, u32[]{:S(2)}, u32[]{:S(2)}) collective-permute-start(f32[1,2176]{1,0:T(1,128)S(1)} %total.3.own_ref), channel_id=1, source_target_pairs={{0,1},{1,0},{2,3},{3,2},{4,5},{5,4},{6,7},{7,6},{8,9},{9,8},{10,11... | collective-permute-start | bytes 26120 | tf_op jit(solution)/shard_map/ppermute | solution.py:313

commit v9 on v8

--- a/solution.py
+++ b/solution.py
@@ -155,20 +155,21 @@
 
     group = 4
 
-    def add_mirrors(i, sums):
-        for j in range(group):
-            d = i * group + j
-            at = jnp.minimum(d, me)
-            wanted = spread_lanes(wanted_ref[at], image_ref.shape[2])
-            wanted = jnp.where(d <= me, wanted, -1)
-            mirror = arrived_ref[at].astype(jnp.float32)
-            sums = tuple(total + jnp.where(wanted == k, mirror, 0.0) for k, total in enumerate(sums))
-        return sums
-
-    zero = jnp.zeros(image_ref.shape[1:], image_ref.dtype)
-    sums = lax.fori_loop(0, (me + group) // group, add_mirrors, (zero,) * row_blocks)
-    for k, total in enumerate(sums):
-        image_ref[k] = total
+    for part in range(image_ref.shape[2] // LANES):
+
+        def add_mirrors(i, sums, at=row_of(part)):
+            for j in range(group):
+                d = i * group + j
+                inside = jnp.minimum(d, me)
+                wanted = jnp.where(d <= me, wanted_ref[inside], -1)
+                mirror = arrived_ref[inside, :, at].astype(jnp.float32)
+                sums = tuple(total + jnp.where(wanted == k, mirror, 0.0) for k, total in enumerate(sums))
+            return sums
+
+        zero = jnp.zeros((image_ref.shape[1], LANES), image_ref.dtype)
+        sums = lax.fori_loop(0, (me + group) // group, add_mirrors, (zero,) * row_blocks)
+        for k, total in enumerate(sums):
+            image_ref[k, :, row_of(part)] = total
 
     def visit(i, carry):
         for j in range(CHUNK):

time: 199 us -> 200 us (level)
  no operation moved by 1% of the time
where the time goes in v9:
time: 200 us
  blocking collectives  148 us (74%)
  Pallas kernels  26.1 us (13%)
  starting transfers between devices  17 us (8%)
  waiting for transfers between devices  5.36 us (3%)
    all_to_all x2, blocking collectives, exchange(): lax.all_to_all(outgoing, AXES, split_axis=0, concat_axis=0, tiled=True)  115 us
    all_to_all x2, blocking collectives, sum_over_devices(): lax.all_to_all(spread, 'rows', 0, 0, tiled=True)  32.6 us
    all_to_all x1, starting transfers between devices, exchange(): lax.all_to_all(outgoing, AXES, split_axis=0, concat_axis=0, tiled=True)  11.5 us
    pallas_call x2, Pallas kernels, image_of(): pl.pallas_call(functools.partial(image_kernel, with_projection), out_shap...  9.28 us
    pallas_call x1, Pallas kernels, on_device(): pl.pallas_call(first_kernel, out_shape=(jax.ShapeDtypeStruct((slots, colu...  5.76 us
    pallas_call x1, Pallas kernels, on_device(): pl.pallas_call(functools.partial(normal_kernel, total_rows), out_shape=(o...  5.35 us
  transfers between devices with their start and end apart: 5, of which 5 were waited for; matrix products, arithmetic and copies ran while one was open for 0% of the time, Pallas kernels for 3%

profile of v9, /device:TPU:1, one launch (start us, length us, event | category | flops | bytes accessed | tf_op | source)
XLA Modules:
  0.0 199.8 jit_solution(2231966849470368058)
XLA Ops:
  1.3 0.0 copy-start.2
  1.3 0.6 copy-done.2
  1.9 0.8 ask.1
  2.8 11.5 %all-to-all-start = ((s32[128,1,128]{2,1,0:T(1,128)}), s32[128,1,128]{2,1,0:T(1,128)S(1)}, u32[]{:S(2)}, u32[]{:S(2)}) async-start(s32[128,1,128]{2,1,0:T(1,128)} %ask.1), calls=%async_computation | async-start | bytes 131072 | tf_op jit(solution)/shard_map/all_to_all | solution.py:318
  14.3 0.8 pad_add_fusion.table_ref
  15.0 0.0 copy-start.1
  15.0 0.8 copy-done.1
  15.9 5.8 %first.1 = (bf16[92,64,256]{2,1,0:T(8,128)(2,1)S(1)}, bf16[2,64,256]{2,1,0:T(8,128)(2,1)S(1)}) custom-call(s32[186]{0:T(256)S(1)} %pad_add_fusion.table_ref, bf16[64,512]{1,0:T(8,128)(2,1)S(1)} %bitcast.4, bf16[92,256,256]{2,1,0:T(8,128)(2,1)} %held.3), custom_call_target="tpu_custom_call" | custom-call | tf_op jit(solution)/shard_map/first/pallas_call | solution.py:358
  21.6 2.1 %all-to-all-done.wanted_ref = s32[128,1,128]{2,1,0:T(1,128)S(1)} async-done(((s32[128,1,128]{2,1,0:T(1,128)}), s32[128,1,128]{2,1,0:T(1,128)S(1)}, u32[]{:S(2)}, u32[]{:S(2)}) %all-to-all-start) | async-done | bytes 65568 | tf_op jit(solution)/shard_map/all_to_all | solution.py:318
  23.7 0.0 copy-start
  23.7 1.3 place.1
  25.0 58.8 %all_to_all.25.arrived_ref = bf16[128,64,256]{2,1,0:T(8,128)(2,1)S(1)} all-to-all(bf16[128,64,256]{2,1,0:T(8,128)(2,1)S(1)} %place.1), channel_id=1, replica_groups=mesh['rows'=64,'grp'=2] {'rows','grp'}, dimensions={0} | all-to-all | bytes 8388608 | tf_op jit(solution)/shard_map/all_to_all | solution.py:318
  83.9 0.0 copy-done
  83.9 5.4 %image.2 = (f32[2,64,256]{2,1,0:T(8,128)S(1)}, f32[1,1152]{1,0:T(1,128)S(1)}, f32[1,1152]{1,0:T(1,128)S(1)}, bf16[92,256,256]{2,1,0:T(8,128)(2,1)S(1)}) custom-call(s32[186]{0:T(256)S(1)} %pad_add_fusion.table_ref, s32[128,1,128]{2,1,0:T(1,128)S(1)} %all-to-all-done.wanted_ref, bf16[2,64,256]{2,1,0:T(8,128)(2,1)S(1)} %get-tuple-element.15.tiles_ref, ...), custom_call_target="tpu_custom_call" | custom-call | tf_op jit(solution)/shard_map/image/pallas_call | solution.py:349
  89.2 1.0 collective-permute-start
  90.2 0.8 collective-permute-done.given_ref
  91.1 15.0 %all_to_all.26.parts_ref = f32[64,1,1152]{2,1,0:T(1,128)S(1)} all-to-all(f32[64,1,1152]{2,1,0:T(1,128)S(1)} %spread.2), channel_id=1, replica_groups=mesh['rows'=64,'grp'=2] {'rows'}, dimensions={0} | all-to-all | bytes 589824 | tf_op jit(solution)/shard_map/all_to_all | solution.py:313
  106.1 1.6 collective-permute-start.1
  107.7 0.8 collective-permute-done.1.other_ref
  108.6 5.3 %normal.1 = (bf16[128,64,256]{2,1,0:T(8,128)(2,1)S(1)}, bf16[2,64,256]{2,1,0:T(8,128)(2,1)S(1)}) custom-call(s32[186]{0:T(256)S(1)} %pad_add_fusion.table_ref, s32[128,1,128]{2,1,0:T(1,128)S(1)} %all-to-all-done.wanted_ref, f32[1,1152]{1,0:T(1,128)S(1)} %total.2.own_ref, f32[1,1152]{1,0:T(1,128)S(1)} %collective-permute-done.1.other_ref, ...), custom_call_target="tpu_custom_call" | custom-call | tf_op jit(solution)/shard_map/normal/pallas_call | solution.py:380
  113.9 56.3 %all_to_all.27.arrived_ref = bf16[128,64,256]{2,1,0:T(8,128)(2,1)S(1)} all-to-all(bf16[128,64,256]{2,1,0:T(8,128)(2,1)S(1)} %get-tuple-element.21), channel_id=1, replica_groups=mesh['rows'=64,'grp'=2] {'rows','grp'}, dimensions={0} | all-to-all | bytes 8388608 | tf_op jit(solution)/shard_map/all_to_all | solution.py:318
  170.2 3.9 %image.3 = (f32[2,64,256]{2,1,0:T(8,128)S(1)}, f32[1,2176]{1,0:T(1,128)S(1)}, f32[1,2176]{1,0:T(1,128)S(1)}) custom-call(s32[186]{0:T(256)S(1)} %pad_add_fusion.table_ref, s32[128,1,128]{2,1,0:T(1,128)S(1)} %all-to-all-done.wanted_ref, bf16[2,64,256]{2,1,0:T(8,128)(2,1)S(1)} %get-tuple-element.20.tiles_ref, ...), custom_call_target="tpu_custom_call" | custom-call | tf_op jit(solution)/shard_map/image/pallas_call | solution.py:349
  174.1 1.0 collective-permute-start.2
  175.1 0.8 collective-permute-done.2.given_ref
  176.0 0.1 spread.3
  176.0 17.6 %all_to_all.28.parts_ref = f32[64,1,2176]{2,1,0:T(1,128)S(1)} all-to-all(f32[64,1,2176]{2,1,0:T(1,128)S(1)} %spread.3), channel_id=1, replica_groups=mesh['rows'=64,'grp'=2] {'rows'}, dimensions={0} | all-to-all | bytes 1114112 | tf_op jit(solution)/shard_map/all_to_all | solution.py:313
  193.7 1.9 collective-permute-start.3
  195.6 0.8 collective-permute-done.3.other_ref
  196.4 3.4 %last.1 = (f32[64,512]{1,0:T(8,128)}, f32[64,64]{1,0:T(8,128)}) custom-call(s32[186]{0:T(256)S(1)} %pad_add_fusion.table_ref, f32[1,2176]{1,0:T(1,128)S(1)} %total.3.own_ref, f32[1,2176]{1,0:T(1,128)S(1)} %collective-permute-done.3.other_ref, f32[2,64,256]{2,1,0:T(8,128)S(1)} %get-tuple-element.25.image_ref), custom_call_target="tpu_custom_call" | custom-call | tf_op jit(solution)/shard_map/last/pallas_call | solution.py:390
  (3 shorter events, 0.1 us)
Async XLA Ops:
  1.3 0.7 copy-start.2
  2.8 20.9 %all-to-all-start = ((s32[128,1,128]{2,1,0:T(1,128)}), s32[128,1,128]{2,1,0:T(1,128)S(1)}, u32[]{:S(2)}, u32[]{:S(2)}) async-start(s32[128,1,128]{2,1,0:T(1,128)} %ask.1), calls=%async_computation | async-start | bytes 131072 | tf_op jit(solution)/shard_map/all_to_all | solution.py:318
  15.0 0.8 copy-start.1
  23.7 60.2 %copy-start = (bf16[92,256,256]{2,1,0:T(8,128)(2,1)S(1)}, bf16[92,256,256]{2,1,0:T(8,128)(2,1)}, u32[]{:S(2)}) copy-start(bf16[92,256,256]{2,1,0:T(8,128)(2,1)} %held.3) | copy-start | bytes 36175876
  89.2 1.8 collective-permute-start
  106.1 2.5 %collective-permute-start.1 = (f32[1,1152]{1,0:T(1,128)S(1)}, f32[1,1152]{1,0:T(1,128)S(1)}, u32[]{:S(2)}, u32[]{:S(2)}) collective-permute-start(f32[1,1152]{1,0:T(1,128)S(1)} %total.2.own_ref), channel_id=1, source_target_pairs={{0,1},{1,0},{2,3},{3,2},{4,5},{5,4},{6,7},{7,6},{8,9},{9,8},{10,11... | collective-permute-start | bytes 13832 | tf_op jit(solution)/shard_map/ppermute | solution.py:314
  174.1 1.8 collective-permute-start.2
  193.7 2.7 %collective-permute-start.3 = (f32[1,2176]{1,0:T(1,128)S(1)}, f32[1,2176]{1,0:T(1,128)S(1)}, u32[]{:S(2)}, u32[]{:S(2)}) collective-permute-start(f32[1,2176]{1,0:T(1,128)S(1)} %total.3.own_ref), channel_id=1, source_target_pairs={{0,1},{1,0},{2,3},{3,2},{4,5},{5,4},{6,7},{7,6},{8,9},{9,8},{10,11... | collective-permute-start | bytes 26120 | tf_op jit(solution)/shard_map/ppermute | solution.py:314

commit v10 on v9

--- a/solution.py
+++ b/solution.py
@@ -148,11 +148,11 @@
 
 def image_kernel(
     with_projection, table_ref, wanted_ref, tiles_ref, arrived_ref, held,
-    image_ref, own_ref, given_ref, *turned_ref,
+    image_ref, own_ref, given_ref, *rest,
 ):
     me, live = table_ref[ME], table_ref[LIVE]
     row_blocks = tiles_ref.shape[0]
-
+    turned_ref, sum_ref = rest[:-1], rest[-1]
     group = 4
 
     for part in range(image_ref.shape[2] // LANES):
@@ -169,24 +169,33 @@
         zero = jnp.zeros((image_ref.shape[1], LANES), image_ref.dtype)
         sums = lax.fori_loop(0, (me + group) // group, add_mirrors, (zero,) * row_blocks)
         for k, total in enumerate(sums):
-            image_ref[k, :, row_of(part)] = total
-
-    def visit(i, carry):
+            sum_ref[k, :, row_of(part)] = total
+
+    def visit(i, own_slot):
         for j in range(CHUNK):
             s = i * CHUNK + j
+            owner = table_ref[FIRST + held.shape[0] + s] // row_blocks
             local = table_ref[FIRST + s] - me * row_blocks
-            column = table_ref[FIRST + held.shape[0] + s]
-            owner = column // row_blocks
-            tile = jnp.where(owner == me, tiles_ref[column - owner * row_blocks], arrived_ref[owner])
-            tile = jnp.where(s < live, tile, jnp.zeros_like(tile))
+            own_slot = jnp.where((owner == me) & (s < live), s, own_slot)
+            place = jnp.where((owner == me) | (s >= live), row_blocks, local)
             block = held[s]
             if turned_ref:
                 block = block.T
                 turned_ref[0][s] = block
-            image_ref[local] += jnp.dot(tile, block, preferred_element_type=jnp.float32)
-        return carry
-
-    lax.fori_loop(0, (live + CHUNK - 1) // CHUNK, visit, 0)
+            sum_ref[place] += jnp.dot(arrived_ref[owner], block, preferred_element_type=jnp.float32)
+        return own_slot
+
+    own_slot = lax.fori_loop(0, (live + CHUNK - 1) // CHUNK, visit, jnp.int32(-1))
+
+    @pl.when(own_slot >= 0)
+    def _():
+        local = table_ref[FIRST + own_slot] - me * row_blocks
+        tile = tiles_ref[table_ref[FIRST + held.shape[0] + own_slot] - me * row_blocks]
+        block = turned_ref[0][own_slot] if turned_ref else held[own_slot]
+        sum_ref[local] += jnp.dot(tile, block, preferred_element_type=jnp.float32)
+
+    for k in range(row_blocks):
+        image_ref[k] = sum_ref[k]
 
     def summed(left_ref):
         total = None
@@ -351,6 +360,7 @@
             out_shape=(image_shape, half, half) + turned,
             in_specs=[SMEM] + [VMEM] * 4,
             out_specs=(VMEM,) * (3 + len(turned)),
+            scratch_shapes=[pltpu.VMEM((row_blocks + 1, columns, size), jnp.float32)],
             compiler_params=params,
             name="image",
         )(table, wanted, tiles, arrived, blocks)

time: 200 us -> 199 us (level)
  no operation moved by 1% of the time
where the time goes in v10:
time: 199 us
  blocking collectives  147 us (74%)
  Pallas kernels  26.2 us (13%)
  starting transfers between devices  17 us (9%)
  waiting for transfers between devices  5.36 us (3%)
    all_to_all x2, blocking collectives, exchange(): lax.all_to_all(outgoing, AXES, split_axis=0, concat_axis=0, tiled=True)  115 us
    all_to_all x2, blocking collectives, sum_over_devices(): lax.all_to_all(spread, 'rows', 0, 0, tiled=True)  31.8 us
    all_to_all x1, starting transfers between devices, exchange(): lax.all_to_all(outgoing, AXES, split_axis=0, concat_axis=0, tiled=True)  11.5 us
    pallas_call x2, Pallas kernels, image_of(): pl.pallas_call(functools.partial(image_kernel, with_projection), out_shap...  9.47 us
    pallas_call x1, Pallas kernels, on_device(): pl.pallas_call(first_kernel, out_shape=(jax.ShapeDtypeStruct((slots, colu...  5.76 us
    pallas_call x1, Pallas kernels, on_device(): pl.pallas_call(functools.partial(normal_kernel, total_rows), out_shape=(o...  5.35 us
  transfers between devices with their start and end apart: 5, of which 5 were waited for; matrix products, arithmetic and copies ran while one was open for 0% of the time, Pallas kernels for 3%

profile of v10, /device:TPU:1, one launch (start us, length us, event | category | flops | bytes accessed | tf_op | source)
XLA Modules:
  0.0 198.9 jit_solution(42265571678730971)
XLA Ops:
  1.3 0.0 copy-start.2
  1.3 0.6 copy-done.2
  1.9 0.8 ask.1
  2.8 11.5 %all-to-all-start = ((s32[128,1,128]{2,1,0:T(1,128)}), s32[128,1,128]{2,1,0:T(1,128)S(1)}, u32[]{:S(2)}, u32[]{:S(2)}) async-start(s32[128,1,128]{2,1,0:T(1,128)} %ask.1), calls=%async_computation | async-start | bytes 131072 | tf_op jit(solution)/shard_map/all_to_all | solution.py:327
  14.3 0.8 pad_add_fusion.table_ref
  15.0 0.0 copy-start.1
  15.0 0.8 copy-done.1
  15.9 5.8 %first.1 = (bf16[92,64,256]{2,1,0:T(8,128)(2,1)S(1)}, bf16[2,64,256]{2,1,0:T(8,128)(2,1)S(1)}) custom-call(s32[186]{0:T(256)S(1)} %pad_add_fusion.table_ref, bf16[64,512]{1,0:T(8,128)(2,1)S(1)} %bitcast.4, bf16[92,256,256]{2,1,0:T(8,128)(2,1)} %held.3), custom_call_target="tpu_custom_call" | custom-call | tf_op jit(solution)/shard_map/first/pallas_call | solution.py:368
  21.6 2.1 %all-to-all-done.wanted_ref = s32[128,1,128]{2,1,0:T(1,128)S(1)} async-done(((s32[128,1,128]{2,1,0:T(1,128)}), s32[128,1,128]{2,1,0:T(1,128)S(1)}, u32[]{:S(2)}, u32[]{:S(2)}) %all-to-all-start) | async-done | bytes 65568 | tf_op jit(solution)/shard_map/all_to_all | solution.py:327
  23.7 0.0 copy-start
  23.7 1.3 place.1
  25.0 58.6 %all_to_all.25.arrived_ref = bf16[128,64,256]{2,1,0:T(8,128)(2,1)S(1)} all-to-all(bf16[128,64,256]{2,1,0:T(8,128)(2,1)S(1)} %place.1), channel_id=1, replica_groups=mesh['rows'=64,'grp'=2] {'rows','grp'}, dimensions={0} | all-to-all | bytes 8388608 | tf_op jit(solution)/shard_map/all_to_all | solution.py:327
  83.6 0.0 copy-done
  83.6 5.4 %image.2 = (f32[2,64,256]{2,1,0:T(8,128)S(1)}, f32[1,1152]{1,0:T(1,128)S(1)}, f32[1,1152]{1,0:T(1,128)S(1)}, bf16[92,256,256]{2,1,0:T(8,128)(2,1)S(1)}) custom-call(s32[186]{0:T(256)S(1)} %pad_add_fusion.table_ref, s32[128,1,128]{2,1,0:T(1,128)S(1)} %all-to-all-done.wanted_ref, bf16[2,64,256]{2,1,0:T(8,128)(2,1)S(1)} %get-tuple-element.15.tiles_ref, ...), custom_call_target="tpu_custom_call" | custom-call | tf_op jit(solution)/shard_map/image/pallas_call | solution.py:358
  89.0 1.0 collective-permute-start
  90.1 0.8 collective-permute-done.given_ref
  90.9 14.4 %all_to_all.26.parts_ref = f32[64,1,1152]{2,1,0:T(1,128)S(1)} all-to-all(f32[64,1,1152]{2,1,0:T(1,128)S(1)} %spread.2), channel_id=1, replica_groups=mesh['rows'=64,'grp'=2] {'rows'}, dimensions={0} | all-to-all | bytes 589824 | tf_op jit(solution)/shard_map/all_to_all | solution.py:322
  105.3 1.6 collective-permute-start.1
  107.0 0.8 collective-permute-done.1.other_ref
  107.8 5.3 %normal.1 = (bf16[128,64,256]{2,1,0:T(8,128)(2,1)S(1)}, bf16[2,64,256]{2,1,0:T(8,128)(2,1)S(1)}) custom-call(s32[186]{0:T(256)S(1)} %pad_add_fusion.table_ref, s32[128,1,128]{2,1,0:T(1,128)S(1)} %all-to-all-done.wanted_ref, f32[1,1152]{1,0:T(1,128)S(1)} %total.2.own_ref, f32[1,1152]{1,0:T(1,128)S(1)} %collective-permute-done.1.other_ref, ...), custom_call_target="tpu_custom_call" | custom-call | tf_op jit(solution)/shard_map/normal/pallas_call | solution.py:390
  113.2 56.3 %all_to_all.27.arrived_ref = bf16[128,64,256]{2,1,0:T(8,128)(2,1)S(1)} all-to-all(bf16[128,64,256]{2,1,0:T(8,128)(2,1)S(1)} %get-tuple-element.21), channel_id=1, replica_groups=mesh['rows'=64,'grp'=2] {'rows','grp'}, dimensions={0} | all-to-all | bytes 8388608 | tf_op jit(solution)/shard_map/all_to_all | solution.py:327
  169.4 4.1 %image.3 = (f32[2,64,256]{2,1,0:T(8,128)S(1)}, f32[1,2176]{1,0:T(1,128)S(1)}, f32[1,2176]{1,0:T(1,128)S(1)}) custom-call(s32[186]{0:T(256)S(1)} %pad_add_fusion.table_ref, s32[128,1,128]{2,1,0:T(1,128)S(1)} %all-to-all-done.wanted_ref, bf16[2,64,256]{2,1,0:T(8,128)(2,1)S(1)} %get-tuple-element.20.tiles_ref, ...), custom_call_target="tpu_custom_call" | custom-call | tf_op jit(solution)/shard_map/image/pallas_call | solution.py:358
  173.5 1.0 collective-permute-start.2
  174.5 0.8 collective-permute-done.2.given_ref
  175.3 0.1 spread.3
  175.4 17.4 %all_to_all.28.parts_ref = f32[64,1,2176]{2,1,0:T(1,128)S(1)} all-to-all(f32[64,1,2176]{2,1,0:T(1,128)S(1)} %spread.3), channel_id=1, replica_groups=mesh['rows'=64,'grp'=2] {'rows'}, dimensions={0} | all-to-all | bytes 1114112 | tf_op jit(solution)/shard_map/all_to_all | solution.py:322
  192.9 1.9 collective-permute-start.3
  194.7 0.8 collective-permute-done.3.other_ref
  195.6 3.4 %last.1 = (f32[64,512]{1,0:T(8,128)}, f32[64,64]{1,0:T(8,128)}) custom-call(s32[186]{0:T(256)S(1)} %pad_add_fusion.table_ref, f32[1,2176]{1,0:T(1,128)S(1)} %total.3.own_ref, f32[1,2176]{1,0:T(1,128)S(1)} %collective-permute-done.3.other_ref, f32[2,64,256]{2,1,0:T(8,128)S(1)} %get-tuple-element.25.image_ref), custom_call_target="tpu_custom_call" | custom-call | tf_op jit(solution)/shard_map/last/pallas_call | solution.py:400
  (3 shorter events, 0.1 us)
Async XLA Ops:
  1.3 0.7 copy-start.2
  2.8 20.9 %all-to-all-start = ((s32[128,1,128]{2,1,0:T(1,128)}), s32[128,1,128]{2,1,0:T(1,128)S(1)}, u32[]{:S(2)}, u32[]{:S(2)}) async-start(s32[128,1,128]{2,1,0:T(1,128)} %ask.1), calls=%async_computation | async-start | bytes 131072 | tf_op jit(solution)/shard_map/all_to_all | solution.py:327
  15.0 0.8 copy-start.1
  23.7 59.9 %copy-start = (bf16[92,256,256]{2,1,0:T(8,128)(2,1)S(1)}, bf16[92,256,256]{2,1,0:T(8,128)(2,1)}, u32[]{:S(2)}) copy-start(bf16[92,256,256]{2,1,0:T(8,128)(2,1)} %held.3) | copy-start | bytes 36175876
  89.0 1.8 collective-permute-start
  105.3 2.5 %collective-permute-start.1 = (f32[1,1152]{1,0:T(1,128)S(1)}, f32[1,1152]{1,0:T(1,128)S(1)}, u32[]{:S(2)}, u32[]{:S(2)}) collective-permute-start(f32[1,1152]{1,0:T(1,128)S(1)} %total.2.own_ref), channel_id=1, source_target_pairs={{0,1},{1,0},{2,3},{3,2},{4,5},{5,4},{6,7},{7,6},{8,9},{9,8},{10,11... | collective-permute-start | bytes 13832 | tf_op jit(solution)/shard_map/ppermute | solution.py:323
  173.5 1.8 collective-permute-start.2
  192.9 2.7 %collective-permute-start.3 = (f32[1,2176]{1,0:T(1,128)S(1)}, f32[1,2176]{1,0:T(1,128)S(1)}, u32[]{:S(2)}, u32[]{:S(2)}) collective-permute-start(f32[1,2176]{1,0:T(1,128)S(1)} %total.3.own_ref), channel_id=1, source_target_pairs={{0,1},{1,0},{2,3},{3,2},{4,5},{5,4},{6,7},{7,6},{8,9},{9,8},{10,11... | collective-permute-start | bytes 26120 | tf_op jit(solution)/shard_map/ppermute | solution.py:323

commit v11 on v9

--- a/solution.py
+++ b/solution.py
@@ -9,7 +9,7 @@
 
 AXES = ("rows", "grp")
 HIGHEST = lax.Precision.HIGHEST
-CHUNK = 23
+CHUNK, FEW = 23, 6
 PANEL = 8
 ROWS, LANES = 8, 128
 ME, LIVE, FIRST = 0, 1, 2
@@ -39,20 +39,29 @@
     return jnp.where(s < live, table_ref[FIRST + slots + s] // row_blocks, 0)
 
 
-def multiply_mirrors(me, table_ref, live, tiles_ref, held, out_ref, wait, placed):
+def over_slots(live, turn):
+    full = (live + CHUNK - 2 * FEW - 1) // CHUNK
+
+    def whole(i, carry):
+        turn(i * CHUNK, CHUNK)
+        return carry
+
+    def part(i, carry):
+        turn(full * CHUNK + i * FEW, FEW)
+        return carry
+
+    lax.fori_loop(0, full, whole, 0)
+    lax.fori_loop(0, (jnp.maximum(live - full * CHUNK, 0) + FEW - 1) // FEW, part, 0)
+
+
+def multiply_mirrors(me, table_ref, live, tiles_ref, held, out_ref, placed, first, count):
     row_blocks = tiles_ref.shape[0]
-
-    def visit(i, carry):
-        wait(i)
-        for j in range(CHUNK):
-            s = i * CHUNK + j
-            local = table_ref[FIRST + s] - me * row_blocks
-            place = place_of(s, table_ref, live, row_blocks, held.shape[0]) if placed else s
-            product = jnp.dot(tiles_ref[local], held[s], preferred_element_type=jnp.float32)
-            out_ref[place] = product.astype(out_ref.dtype)
-        return carry
-
-    lax.fori_loop(0, (live + CHUNK - 1) // CHUNK, visit, 0)
+    for j in range(count):
+        s = first + j
+        local = table_ref[FIRST + s] - me * row_blocks
+        place = place_of(s, table_ref, live, row_blocks, held.shape[0]) if placed else s
+        product = jnp.dot(tiles_ref[local], held[s], preferred_element_type=jnp.float32)
+        out_ref[place] = product.astype(out_ref.dtype)
 
 
 def place_tiles(start, end, wanted_ref, tiles_ref, out_ref):
@@ -93,10 +102,13 @@
     row_blocks, _, size = tiles_ref.shape
     for j in range(row_blocks):
         tiles_ref[j] = basis_ref[:, j * size : (j + 1) * size]
-    multiply_mirrors(
-        table_ref[ME], table_ref, live, tiles_ref, held, out_ref,
-        lambda i: block_copy(blocks_ref, held, sems, i).wait(), False,
-    )
+
+    def visit(i, carry):
+        block_copy(blocks_ref, held, sems, i).wait()
+        multiply_mirrors(table_ref[ME], table_ref, live, tiles_ref, held, out_ref, False, i * CHUNK, CHUNK)
+        return carry
+
+    lax.fori_loop(0, (live + CHUNK - 1) // CHUNK, visit, 0)
 
 
 def place_kernel(table_ref, wanted_ref, tiles_ref, products_ref, out_ref):
@@ -171,9 +183,9 @@
         for k, total in enumerate(sums):
             image_ref[k, :, row_of(part)] = total
 
-    def visit(i, carry):
-        for j in range(CHUNK):
-            s = i * CHUNK + j
+    def visit(first, count):
+        for j in range(count):
+            s = first + j
             local = table_ref[FIRST + s] - me * row_blocks
             column = table_ref[FIRST + held.shape[0] + s]
             owner = column // row_blocks
@@ -184,9 +196,8 @@
                 block = block.T
                 turned_ref[0][s] = block
             image_ref[local] += jnp.dot(tile, block, preferred_element_type=jnp.float32)
-        return carry
-
-    lax.fori_loop(0, (live + CHUNK - 1) // CHUNK, visit, 0)
+
+    over_slots(live, visit)
 
     def summed(left_ref):
         total = None
@@ -264,7 +275,7 @@
         tiles_ref[j] = jnp.dot(
             inverse, image_ref[j], precision=HIGHEST, preferred_element_type=jnp.float32
         ).astype(tiles_ref.dtype)
-    multiply_mirrors(me, table_ref, live, tiles_ref, held, out_ref, lambda i: None, True)
+    over_slots(live, functools.partial(multiply_mirrors, me, table_ref, live, tiles_ref, held, out_ref, True))
     place_tiles(0, me, wanted_ref, tiles_ref, out_ref)
 
 

time: 200 us -> 199 us (level)
  blocking collectives: 148 us -> 146 us
where the time goes in v11:
time: 199 us; the launch traced here: 198 us
  blocking collectives  146 us (73%)
  Pallas kernels  25.5 us (13%)
  starting transfers between devices  17.4 us (9%)
  waiting for transfers between devices  5.36 us (3%)
    all_to_all x2, blocking collectives, exchange(): lax.all_to_all(outgoing, AXES, split_axis=0, concat_axis=0, tiled=True)  115 us
    all_to_all x2, blocking collectives, sum_over_devices(): lax.all_to_all(spread, 'rows', 0, 0, tiled=True)  31.5 us
    all_to_all x1, starting transfers between devices, exchange(): lax.all_to_all(outgoing, AXES, split_axis=0, concat_axis=0, tiled=True)  11.5 us
    pallas_call x2, Pallas kernels, image_of(): pl.pallas_call(functools.partial(image_kernel, with_projection), out_shap...  8.89 us
    pallas_call x1, Pallas kernels, on_device(): pl.pallas_call(first_kernel, out_shape=(jax.ShapeDtypeStruct((slots, colu...  5.76 us
    pallas_call x1, Pallas kernels, on_device(): pl.pallas_call(functools.partial(normal_kernel, total_rows), out_shape=(o...  5.22 us
  transfers between devices with their start and end apart: 5, of which 5 were waited for; matrix products, arithmetic and copies ran while one was open for 0% of the time, Pallas kernels for 3%

profile of v11, /device:TPU:1, one launch (start us, length us, event | category | flops | bytes accessed | tf_op | source)
XLA Modules:
  0.0 198.4 jit_solution(18324848236420643934)
XLA Ops:
  1.3 0.0 copy-start.2
  1.3 0.6 copy-done.2
  1.9 0.8 ask.1
  2.8 11.5 %all-to-all-start = ((s32[128,1,128]{2,1,0:T(1,128)}), s32[128,1,128]{2,1,0:T(1,128)S(1)}, u32[]{:S(2)}, u32[]{:S(2)}) async-start(s32[128,1,128]{2,1,0:T(1,128)} %ask.1), calls=%async_computation | async-start | bytes 131072 | tf_op jit(solution)/shard_map/all_to_all | solution.py:329
  14.3 0.8 pad_add_fusion.table_ref
  15.0 0.0 copy-start.1
  15.0 0.8 copy-done.1
  15.9 5.8 %first.1 = (bf16[92,64,256]{2,1,0:T(8,128)(2,1)S(1)}, bf16[2,64,256]{2,1,0:T(8,128)(2,1)S(1)}) custom-call(s32[186]{0:T(256)S(1)} %pad_add_fusion.table_ref, bf16[64,512]{1,0:T(8,128)(2,1)S(1)} %bitcast.4, bf16[92,256,256]{2,1,0:T(8,128)(2,1)} %held.3), custom_call_target="tpu_custom_call" | custom-call | tf_op jit(solution)/shard_map/first/pallas_call | solution.py:369
  21.6 2.1 %all-to-all-done.wanted_ref = s32[128,1,128]{2,1,0:T(1,128)S(1)} async-done(((s32[128,1,128]{2,1,0:T(1,128)}), s32[128,1,128]{2,1,0:T(1,128)S(1)}, u32[]{:S(2)}, u32[]{:S(2)}) %all-to-all-start) | async-done | bytes 65568 | tf_op jit(solution)/shard_map/all_to_all | solution.py:329
  23.7 0.0 copy-start
  23.7 1.3 place.1
  25.0 58.6 %all_to_all.25.arrived_ref = bf16[128,64,256]{2,1,0:T(8,128)(2,1)S(1)} all-to-all(bf16[128,64,256]{2,1,0:T(8,128)(2,1)S(1)} %place.1), channel_id=1, replica_groups=mesh['rows'=64,'grp'=2] {'rows','grp'}, dimensions={0} | all-to-all | bytes 8388608 | tf_op jit(solution)/shard_map/all_to_all | solution.py:329
  83.6 0.0 copy-done
  83.6 5.1 %image.2 = (f32[2,64,256]{2,1,0:T(8,128)S(1)}, f32[1,1152]{1,0:T(1,128)S(1)}, f32[1,1152]{1,0:T(1,128)S(1)}, bf16[92,256,256]{2,1,0:T(8,128)(2,1)S(1)}) custom-call(s32[186]{0:T(256)S(1)} %pad_add_fusion.table_ref, s32[128,1,128]{2,1,0:T(1,128)S(1)} %all-to-all-done.wanted_ref, bf16[2,64,256]{2,1,0:T(8,128)(2,1)S(1)} %get-tuple-element.15.tiles_ref, ...), custom_call_target="tpu_custom_call" | custom-call | tf_op jit(solution)/shard_map/image/pallas_call | solution.py:360
  88.7 1.3 collective-permute-start
  90.0 0.8 collective-permute-done.given_ref
  90.9 14.2 %all_to_all.26.parts_ref = f32[64,1,1152]{2,1,0:T(1,128)S(1)} all-to-all(f32[64,1,1152]{2,1,0:T(1,128)S(1)} %spread.2), channel_id=1, replica_groups=mesh['rows'=64,'grp'=2] {'rows'}, dimensions={0} | all-to-all | bytes 589824 | tf_op jit(solution)/shard_map/all_to_all | solution.py:324
  105.1 1.6 collective-permute-start.1
  106.7 0.8 collective-permute-done.1.other_ref
  107.5 5.2 %normal.1 = (bf16[128,64,256]{2,1,0:T(8,128)(2,1)S(1)}, bf16[2,64,256]{2,1,0:T(8,128)(2,1)S(1)}) custom-call(s32[186]{0:T(256)S(1)} %pad_add_fusion.table_ref, s32[128,1,128]{2,1,0:T(1,128)S(1)} %all-to-all-done.wanted_ref, f32[1,1152]{1,0:T(1,128)S(1)} %total.2.own_ref, f32[1,1152]{1,0:T(1,128)S(1)} %collective-permute-done.1.other_ref, ...), custom_call_target="tpu_custom_call" | custom-call | tf_op jit(solution)/shard_map/normal/pallas_call | solution.py:391
  112.7 56.4 %all_to_all.27.arrived_ref = bf16[128,64,256]{2,1,0:T(8,128)(2,1)S(1)} all-to-all(bf16[128,64,256]{2,1,0:T(8,128)(2,1)S(1)} %get-tuple-element.21), channel_id=1, replica_groups=mesh['rows'=64,'grp'=2] {'rows','grp'}, dimensions={0} | all-to-all | bytes 8388608 | tf_op jit(solution)/shard_map/all_to_all | solution.py:329
  169.1 3.8 %image.3 = (f32[2,64,256]{2,1,0:T(8,128)S(1)}, f32[1,2176]{1,0:T(1,128)S(1)}, f32[1,2176]{1,0:T(1,128)S(1)}) custom-call(s32[186]{0:T(256)S(1)} %pad_add_fusion.table_ref, s32[128,1,128]{2,1,0:T(1,128)S(1)} %all-to-all-done.wanted_ref, bf16[2,64,256]{2,1,0:T(8,128)(2,1)S(1)} %get-tuple-element.20.tiles_ref, ...), custom_call_target="tpu_custom_call" | custom-call | tf_op jit(solution)/shard_map/image/pallas_call | solution.py:360
  172.9 1.1 collective-permute-start.2
  174.1 0.8 collective-permute-done.2.given_ref
  174.9 0.1 spread.3
  175.0 17.3 %all_to_all.28.parts_ref = f32[64,1,2176]{2,1,0:T(1,128)S(1)} all-to-all(f32[64,1,2176]{2,1,0:T(1,128)S(1)} %spread.3), channel_id=1, replica_groups=mesh['rows'=64,'grp'=2] {'rows'}, dimensions={0} | all-to-all | bytes 1114112 | tf_op jit(solution)/shard_map/all_to_all | solution.py:324
  192.3 1.9 collective-permute-start.3
  194.2 0.8 collective-permute-done.3.other_ref
  195.0 3.4 %last.1 = (f32[64,512]{1,0:T(8,128)}, f32[64,64]{1,0:T(8,128)}) custom-call(s32[186]{0:T(256)S(1)} %pad_add_fusion.table_ref, f32[1,2176]{1,0:T(1,128)S(1)} %total.3.own_ref, f32[1,2176]{1,0:T(1,128)S(1)} %collective-permute-done.3.other_ref, f32[2,64,256]{2,1,0:T(8,128)S(1)} %get-tuple-element.25.image_ref), custom_call_target="tpu_custom_call" | custom-call | tf_op jit(solution)/shard_map/last/pallas_call | solution.py:401
  (3 shorter events, 0.1 us)
Async XLA Ops:
  1.3 0.7 copy-start.2
  2.8 20.9 %all-to-all-start = ((s32[128,1,128]{2,1,0:T(1,128)}), s32[128,1,128]{2,1,0:T(1,128)S(1)}, u32[]{:S(2)}, u32[]{:S(2)}) async-start(s32[128,1,128]{2,1,0:T(1,128)} %ask.1), calls=%async_computation | async-start | bytes 131072 | tf_op jit(solution)/shard_map/all_to_all | solution.py:329
  15.0 0.8 copy-start.1
  23.7 59.9 %copy-start = (bf16[92,256,256]{2,1,0:T(8,128)(2,1)S(1)}, bf16[92,256,256]{2,1,0:T(8,128)(2,1)}, u32[]{:S(2)}) copy-start(bf16[92,256,256]{2,1,0:T(8,128)(2,1)} %held.3) | copy-start | bytes 36175876
  88.7 2.1 %collective-permute-start = (f32[1,1152]{1,0:T(1,128)S(1)}, f32[1,1152]{1,0:T(1,128)S(1)}, u32[]{:S(2)}, u32[]{:S(2)}) collective-permute-start(f32[1,1152]{1,0:T(1,128)S(1)} %get-tuple-element.18), channel_id=1, source_target_pairs={{0,1},{1,0},{2,3},{3,2},{4,5},{5,4},{6,7},{7,6},{8,9},{9,8},{10,11... | collective-permute-start | bytes 13832 | tf_op jit(solution)/shard_map/ppermute | solution.py:316
  105.1 2.4 %collective-permute-start.1 = (f32[1,1152]{1,0:T(1,128)S(1)}, f32[1,1152]{1,0:T(1,128)S(1)}, u32[]{:S(2)}, u32[]{:S(2)}) collective-permute-start(f32[1,1152]{1,0:T(1,128)S(1)} %total.2.own_ref), channel_id=1, source_target_pairs={{0,1},{1,0},{2,3},{3,2},{4,5},{5,4},{6,7},{7,6},{8,9},{9,8},{10,11... | collective-permute-start | bytes 13832 | tf_op jit(solution)/shard_map/ppermute | solution.py:325
  172.9 2.0 collective-permute-start.2
  192.3 2.7 %collective-permute-start.3 = (f32[1,2176]{1,0:T(1,128)S(1)}, f32[1,2176]{1,0:T(1,128)S(1)}, u32[]{:S(2)}, u32[]{:S(2)}) collective-permute-start(f32[1,2176]{1,0:T(1,128)S(1)} %total.3.own_ref), channel_id=1, source_target_pairs={{0,1},{1,0},{2,3},{3,2},{4,5},{5,4},{6,7},{7,6},{8,9},{9,8},{10,11... | collective-permute-start | bytes 26120 | tf_op jit(solution)/shard_map/ppermute | solution.py:325

commit v12 on v11

--- a/solution.py
+++ b/solution.py
@@ -42,6 +42,10 @@
 def over_slots(live, turn):
     full = (live + CHUNK - 2 * FEW - 1) // CHUNK
 
+    def double(i, carry):
+        turn(i * 2 * CHUNK, 2 * CHUNK)
+        return carry
+
     def whole(i, carry):
         turn(i * CHUNK, CHUNK)
         return carry
@@ -50,7 +54,8 @@
         turn(full * CHUNK + i * FEW, FEW)
         return carry
 
-    lax.fori_loop(0, full, whole, 0)
+    lax.fori_loop(0, full // 2, double, 0)
+    lax.fori_loop(full // 2 * 2, full, whole, 0)
     lax.fori_loop(0, (jnp.maximum(live - full * CHUNK, 0) + FEW - 1) // FEW, part, 0)
 
 

time: 199 us -> 199 us (level)
  no operation moved by 1% of the time
where the time goes in v12:
time: 199 us; the launch traced here: 198 us
  blocking collectives  147 us (74%)
  Pallas kernels  25.4 us (13%)
  starting transfers between devices  17 us (9%)
  waiting for transfers between devices  5.36 us (3%)
    all_to_all x2, blocking collectives, exchange(): lax.all_to_all(outgoing, AXES, split_axis=0, concat_axis=0, tiled=True)  115 us
    all_to_all x2, blocking collectives, sum_over_devices(): lax.all_to_all(spread, 'rows', 0, 0, tiled=True)  32 us
    all_to_all x1, starting transfers between devices, exchange(): lax.all_to_all(outgoing, AXES, split_axis=0, concat_axis=0, tiled=True)  11.5 us
    pallas_call x2, Pallas kernels, image_of(): pl.pallas_call(functools.partial(image_kernel, with_projection), out_shap...  8.89 us
    pallas_call x1, Pallas kernels, on_device(): pl.pallas_call(first_kernel, out_shape=(jax.ShapeDtypeStruct((slots, colu...  5.76 us
    pallas_call x1, Pallas kernels, on_device(): pl.pallas_call(functools.partial(normal_kernel, total_rows), out_shape=(o...  5.09 us
  transfers between devices with their start and end apart: 5, of which 5 were waited for; matrix products, arithmetic and copies ran while one was open for 0% of the time, Pallas kernels for 3%

profile of v12, /device:TPU:1, one launch (start us, length us, event | category | flops | bytes accessed | tf_op | source)
XLA Modules:
  0.0 198.4 jit_solution(1703845991822217916)
XLA Ops:
  1.3 0.0 copy-start.2
  1.3 0.6 copy-done.2
  1.9 0.8 ask.1
  2.8 11.5 %all-to-all-start = ((s32[128,1,128]{2,1,0:T(1,128)}), s32[128,1,128]{2,1,0:T(1,128)S(1)}, u32[]{:S(2)}, u32[]{:S(2)}) async-start(s32[128,1,128]{2,1,0:T(1,128)} %ask.1), calls=%async_computation | async-start | bytes 131072 | tf_op jit(solution)/shard_map/all_to_all | solution.py:334
  14.3 0.8 pad_add_fusion.table_ref
  15.0 0.0 copy-start.1
  15.0 0.8 copy-done.1
  15.9 5.8 %first.1 = (bf16[92,64,256]{2,1,0:T(8,128)(2,1)S(1)}, bf16[2,64,256]{2,1,0:T(8,128)(2,1)S(1)}) custom-call(s32[186]{0:T(256)S(1)} %pad_add_fusion.table_ref, bf16[64,512]{1,0:T(8,128)(2,1)S(1)} %bitcast.4, bf16[92,256,256]{2,1,0:T(8,128)(2,1)} %held.3), custom_call_target="tpu_custom_call" | custom-call | tf_op jit(solution)/shard_map/first/pallas_call | solution.py:374
  21.6 2.1 %all-to-all-done.wanted_ref = s32[128,1,128]{2,1,0:T(1,128)S(1)} async-done(((s32[128,1,128]{2,1,0:T(1,128)}), s32[128,1,128]{2,1,0:T(1,128)S(1)}, u32[]{:S(2)}, u32[]{:S(2)}) %all-to-all-start) | async-done | bytes 65568 | tf_op jit(solution)/shard_map/all_to_all | solution.py:334
  23.7 0.0 copy-start
  23.7 1.3 place.1
  25.0 58.8 %all_to_all.25.arrived_ref = bf16[128,64,256]{2,1,0:T(8,128)(2,1)S(1)} all-to-all(bf16[128,64,256]{2,1,0:T(8,128)(2,1)S(1)} %place.1), channel_id=1, replica_groups=mesh['rows'=64,'grp'=2] {'rows','grp'}, dimensions={0} | all-to-all | bytes 8388608 | tf_op jit(solution)/shard_map/all_to_all | solution.py:334
  83.8 0.0 copy-done
  83.8 5.1 %image.2 = (f32[2,64,256]{2,1,0:T(8,128)S(1)}, f32[1,1152]{1,0:T(1,128)S(1)}, f32[1,1152]{1,0:T(1,128)S(1)}, bf16[92,256,256]{2,1,0:T(8,128)(2,1)S(1)}) custom-call(s32[186]{0:T(256)S(1)} %pad_add_fusion.table_ref, s32[128,1,128]{2,1,0:T(1,128)S(1)} %all-to-all-done.wanted_ref, bf16[2,64,256]{2,1,0:T(8,128)(2,1)S(1)} %get-tuple-element.15.tiles_ref, ...), custom_call_target="tpu_custom_call" | custom-call | tf_op jit(solution)/shard_map/image/pallas_call | solution.py:365
  88.9 1.0 collective-permute-start
  89.9 0.8 collective-permute-done.given_ref
  90.8 14.3 %all_to_all.26.parts_ref = f32[64,1,1152]{2,1,0:T(1,128)S(1)} all-to-all(f32[64,1,1152]{2,1,0:T(1,128)S(1)} %spread.2), channel_id=1, replica_groups=mesh['rows'=64,'grp'=2] {'rows'}, dimensions={0} | all-to-all | bytes 589824 | tf_op jit(solution)/shard_map/all_to_all | solution.py:329
  105.1 1.6 collective-permute-start.1
  106.7 0.8 collective-permute-done.1.other_ref
  107.5 5.1 %normal.1 = (bf16[128,64,256]{2,1,0:T(8,128)(2,1)S(1)}, bf16[2,64,256]{2,1,0:T(8,128)(2,1)S(1)}) custom-call(s32[186]{0:T(256)S(1)} %pad_add_fusion.table_ref, s32[128,1,128]{2,1,0:T(1,128)S(1)} %all-to-all-done.wanted_ref, f32[1,1152]{1,0:T(1,128)S(1)} %total.2.own_ref, f32[1,1152]{1,0:T(1,128)S(1)} %collective-permute-done.1.other_ref, ...), custom_call_target="tpu_custom_call" | custom-call | tf_op jit(solution)/shard_map/normal/pallas_call | solution.py:396
  112.6 56.3 %all_to_all.27.arrived_ref = bf16[128,64,256]{2,1,0:T(8,128)(2,1)S(1)} all-to-all(bf16[128,64,256]{2,1,0:T(8,128)(2,1)S(1)} %get-tuple-element.21), channel_id=1, replica_groups=mesh['rows'=64,'grp'=2] {'rows','grp'}, dimensions={0} | all-to-all | bytes 8388608 | tf_op jit(solution)/shard_map/all_to_all | solution.py:334
  168.9 3.8 %image.3 = (f32[2,64,256]{2,1,0:T(8,128)S(1)}, f32[1,2176]{1,0:T(1,128)S(1)}, f32[1,2176]{1,0:T(1,128)S(1)}) custom-call(s32[186]{0:T(256)S(1)} %pad_add_fusion.table_ref, s32[128,1,128]{2,1,0:T(1,128)S(1)} %all-to-all-done.wanted_ref, bf16[2,64,256]{2,1,0:T(8,128)(2,1)S(1)} %get-tuple-element.20.tiles_ref, ...), custom_call_target="tpu_custom_call" | custom-call | tf_op jit(solution)/shard_map/image/pallas_call | solution.py:365
  172.7 1.0 collective-permute-start.2
  173.7 0.8 collective-permute-done.2.given_ref
  174.6 0.1 spread.3
  174.6 17.7 %all_to_all.28.parts_ref = f32[64,1,2176]{2,1,0:T(1,128)S(1)} all-to-all(f32[64,1,2176]{2,1,0:T(1,128)S(1)} %spread.3), channel_id=1, replica_groups=mesh['rows'=64,'grp'=2] {'rows'}, dimensions={0} | all-to-all | bytes 1114112 | tf_op jit(solution)/shard_map/all_to_all | solution.py:329
  192.4 1.9 collective-permute-start.3
  194.2 0.8 collective-permute-done.3.other_ref
  195.1 3.4 %last.1 = (f32[64,512]{1,0:T(8,128)}, f32[64,64]{1,0:T(8,128)}) custom-call(s32[186]{0:T(256)S(1)} %pad_add_fusion.table_ref, f32[1,2176]{1,0:T(1,128)S(1)} %total.3.own_ref, f32[1,2176]{1,0:T(1,128)S(1)} %collective-permute-done.3.other_ref, f32[2,64,256]{2,1,0:T(8,128)S(1)} %get-tuple-element.25.image_ref), custom_call_target="tpu_custom_call" | custom-call | tf_op jit(solution)/shard_map/last/pallas_call | solution.py:406
  (3 shorter events, 0.1 us)
Async XLA Ops:
  1.3 0.7 copy-start.2
  2.8 20.9 %all-to-all-start = ((s32[128,1,128]{2,1,0:T(1,128)}), s32[128,1,128]{2,1,0:T(1,128)S(1)}, u32[]{:S(2)}, u32[]{:S(2)}) async-start(s32[128,1,128]{2,1,0:T(1,128)} %ask.1), calls=%async_computation | async-start | bytes 131072 | tf_op jit(solution)/shard_map/all_to_all | solution.py:334
  15.0 0.8 copy-start.1
  23.7 60.1 %copy-start = (bf16[92,256,256]{2,1,0:T(8,128)(2,1)S(1)}, bf16[92,256,256]{2,1,0:T(8,128)(2,1)}, u32[]{:S(2)}) copy-start(bf16[92,256,256]{2,1,0:T(8,128)(2,1)} %held.3) | copy-start | bytes 36175876
  88.9 1.8 collective-permute-start
  105.1 2.5 %collective-permute-start.1 = (f32[1,1152]{1,0:T(1,128)S(1)}, f32[1,1152]{1,0:T(1,128)S(1)}, u32[]{:S(2)}, u32[]{:S(2)}) collective-permute-start(f32[1,1152]{1,0:T(1,128)S(1)} %total.2.own_ref), channel_id=1, source_target_pairs={{0,1},{1,0},{2,3},{3,2},{4,5},{5,4},{6,7},{7,6},{8,9},{9,8},{10,11... | collective-permute-start | bytes 13832 | tf_op jit(solution)/shard_map/ppermute | solution.py:330
  172.7 1.8 collective-permute-start.2
  192.4 2.7 %collective-permute-start.3 = (f32[1,2176]{1,0:T(1,128)S(1)}, f32[1,2176]{1,0:T(1,128)S(1)}, u32[]{:S(2)}, u32[]{:S(2)}) collective-permute-start(f32[1,2176]{1,0:T(1,128)S(1)} %total.3.own_ref), channel_id=1, source_target_pairs={{0,1},{1,0},{2,3},{3,2},{4,5},{5,4},{6,7},{7,6},{8,9},{9,8},{10,11... | collective-permute-start | bytes 26120 | tf_op jit(solution)/shard_map/ppermute | solution.py:330
